TPU v7x, 512 devices: a whole 4x4x16 slice. The times are simulated.
512 devices in a mesh: aux: 32 (over z_lo, y), row: 4 (over x), col: 4 (over z_hi, core).
Axes of the slice: x: 4, y: 4, z: 16 (z_hi: 2, z_lo: 8; z = z_hi * 8 + z_lo), core: 2. Of those that a mesh axis runs over, the one named last changes fastest.
Arguments:
- g_plus: bfloat16 [2048, 2048], P('row', ('aux', 'col')), may hold values from -0.125 to 0.125
- g_minus: bfloat16 [2048, 2048], P(('aux', 'row'), 'col'), may hold values from -0.125 to 0.125
- coulomb: bfloat16 [64, 2048, 2048], P('aux', 'row'), may hold values from -3 to 3
Outputs:
- sigma: bfloat16 [2048, 2048], P('row', 'col')
All inputs are finite; a program needn't handle non-finite values.
Results may differ from a plain program's by a relative error of at most 0.0057.
Values may be sent and summed in bfloat16 or wider, within the bound.
No kernel may reach another device: no remote copies, remote signals or barrier semaphores. Data moves between devices by JAX's collectives and lax.ppermute only.
A program may use at most 64 MiB of HBM per device.

v0:
```python
import jax
import jax.numpy as jnp
from jax import lax
from jax.sharding import PartitionSpec as P


def local(g_plus, g_minus, coulomb):
    count = coulomb.shape[0]
    strip = coulomb
    half = jnp.einsum(
        "qik,kj->qij",
        strip,
        lax.all_gather(g_minus, ("aux", "row"), axis=0, tiled=True),
        preferred_element_type=jnp.float32,
    ).astype(jnp.bfloat16)
    pieces = []
    for index in range(count):
        pieces.append(lax.all_gather(half[index], "row", axis=0, tiled=True))
    columns = jnp.stack(pieces, axis=0)
    strip = columns
    pair = jnp.einsum(
        "ik,qkj->qij",
        lax.all_gather(g_plus, ("aux", "col"), axis=1, tiled=True),
        strip,
        preferred_element_type=jnp.float32,
    )
    local_sum = jnp.sum(pair * half.astype(jnp.float32), axis=0)
    whole = lax.psum(local_sum, "aux")
    return (-whole).astype(jnp.bfloat16)


def solution(mesh):
    in_specs = (P("row", ("aux", "col")), P(("aux", "row"), "col"), P("aux", "row", None))
    out_specs = P("row", "col")
    return jax.shard_map(local, mesh=mesh, in_specs=in_specs, out_specs=out_specs, check_vma=False)
```

profile of v0, /device:TPU:2, one launch (start us, length us, event | category | flops | bytes accessed | tf_op | source)
XLA Modules:
  0.0 1739.7 jit_solution(18407722494647900248)
XLA Ops:
  6.5 0.0 all-gather.7.cloned.1.call-start
  6.5 0.7 all-gather.7.cloned.1.call-update
  7.3 0.0 all-gather.9.cloned.1.call-start
  7.3 0.7 all-gather.9.cloned.1.call-update
  8.0 0.0 all-gather.11.cloned.1.call-start
  8.1 962.0 %all-gather.7.cloned.1.call-done = bf16[2048,512]{1,0:T(8,128)(2,1)} async-done(((bf16[16,512]{1,0:T(8,128)(2,1)}), bf16[2048,512]{1,0:T(8,128)(2,1)}) %all-gather.7.cloned.1.call-update) | async-done | bytes 2097168 | tf_op jit(solution)/shard_map/all_gather | solution.py:13
  970.1 5.2 fusion.8
  975.3 1.1 fusion.16
  976.3 0.0 all-gather.11.cloned.1.call-update
  976.4 0.0 all-gather.13.cloned.1.call-start
  976.4 0.5 all-gather.13.cloned.1.call-update
  976.9 0.0 all-reduce.2.cloned.1.call-start
  977.0 214.2 %all-gather.9.cloned.1.call-done = bf16[512,2048]{0,1:T(8,128)(2,1)} async-done(((bf16[512,16]{0,1:T(8,128)(2,1)}), bf16[512,2048]{0,1:T(8,128)(2,1)}) %all-gather.9.cloned.1.call-update) | async-done | bytes 2097168 | tf_op jit(solution)/shard_map/all_gather | solution.py:23
  1191.2 36.3 %all-gather.11.cloned.1.call-done = bf16[1,2048,512]{2,1,0:T(8,128)(2,1)} async-done(((bf16[1,512,512]{2,1,0:T(8,128)(2,1)}), bf16[1,2048,512]{2,1,0:T(8,128)(2,1)}) %all-gather.11.cloned.1.call-update) | async-done | bytes 2097168 | tf_op jit(solution)/shard_map/all_gather | solution.py:18
  1227.5 40.6 %all-gather.13.cloned.1.call-done = bf16[1,2048,512]{2,1,0:T(8,128)(2,1)} async-done(((bf16[1,512,512]{2,1,0:T(8,128)(2,1)}), bf16[1,2048,512]{2,1,0:T(8,128)(2,1)}) %all-gather.13.cloned.1.call-update) | async-done | bytes 2097168 | tf_op jit(solution)/shard_map/all_gather | solution.py:18
  1268.1 6.3 fusion.4
  1274.4 0.0 all-reduce.2.cloned.1.call-update
  1274.4 456.5 %all-reduce.2.cloned.1.call-done = f32[512,512]{1,0:T(8,128)} async-done(((f32[512,512]{1,0:T(8,128)}), f32[512,512]{1,0:T(8,128)}) %all-reduce.2.cloned.1.call-update) | async-done | bytes 1048592 | tf_op jit(solution)/shard_map/psum | solution.py:28
  1731.0 2.1 negate_convert_fusion
Async XLA Ops:
  6.5 963.6 %all-gather.7.cloned.1.call-start = ((), (), s32[]{:S(2)}) async-start(), calls=%async_computation | async-start | bytes 2113536 | tf_op jit(solution)/shard_map/all_gather | solution.py:13
  7.3 1183.9 %all-gather.9.cloned.1.call-start = ((), (), s32[]{:S(2)}) async-start(), calls=%async_computation.1 | async-start | bytes 2113536 | tf_op jit(solution)/shard_map/all_gather | solution.py:23
  8.0 1219.5 %all-gather.11.cloned.1.call-start = ((), (), s32[]{:S(2)}) async-start(), calls=%async_computation.3 | async-start | bytes 2621440 | tf_op jit(solution)/shard_map/all_gather | solution.py:18
  976.4 291.8 %all-gather.13.cloned.1.call-start = ((), (), s32[]{:S(2)}) async-start(), calls=%async_computation.4 | async-start | bytes 2621440 | tf_op jit(solution)/shard_map/all_gather | solution.py:18
  976.9 754.0 %all-reduce.2.cloned.1.call-start = ((), (), s32[]{:S(2)}) async-start(), calls=%async_computation.2 | async-start | bytes 2097152 | tf_op jit(solution)/shard_map/psum | solution.py:28
Sparse Core Ops, SparseCore 0:
  9.4 960.6 all-gather.6
  972.2 218.8 all-gather.8
  1193.3 34.1 all-gather.10
  1229.5 38.5 all-gather.12
  1274.6 456.3 all-reduce.1
where the time goes:
time: 1740 us
  waiting for transfers between devices  1710 us (98%)
    all_gather x1, waiting for transfers between devices, local(): lax.all_gather(g_minus, ('aux', 'row'), axis=0, tiled=True)  962 us
    psum x1, waiting for transfers between devices, local(): whole = lax.psum(local_sum, 'aux')  457 us
    all_gather x1, waiting for transfers between devices, local(): lax.all_gather(g_plus, ('aux', 'col'), axis=1, tiled=True)  214 us
    all_gather x2, waiting for transfers between devices, local(): pieces.append(lax.all_gather(half[index], 'row', axis=0, tiled=True))  76.9 us
  transfers between devices with their start and end apart: 5, of which 5 were waited for; matrix products, arithmetic and copies ran while one was open for 0% of the time, Pallas kernels for 0%

commit v1 on v0

v1 whole, which is shorter than its diff:
```python
import jax
import jax.numpy as jnp
from jax import lax
from jax.sharding import Mesh, PartitionSpec as P

BF = jnp.bfloat16
F32 = jnp.float32


def spread(block, axes, count):
    return lax.all_to_all(jnp.broadcast_to(block[None], (count,) + block.shape), axes, 0, 0)


def shift(count, by):
    return [(index, (index + by) % count) for index in range(count)]


def solution(mesh):
    aux, row, col = (mesh.shape[name] for name in ("aux", "row", "col"))
    zl, y, zh, core = aux // 4, 4, col // 2, 2
    fine = Mesh(mesh.devices.reshape(zl, y, row, zh, core), ("zl", "y", "row", "zh", "core"))

    def local(g_plus, g_minus, coulomb):
        count, rows, n = coulomb.shape
        cols = g_minus.shape[1]
        depth = g_minus.shape[0]
        minus = spread(g_minus, "zl", zl)
        minus = spread(minus, ("y", "row"), y * row)
        minus = minus.reshape(y, row, zl, depth, cols).transpose(2, 0, 1, 3, 4).reshape(n, cols)
        thin = g_plus.shape[1]
        plus = spread(g_plus.T, ("zl", "zh"), zl * zh)
        plus = spread(plus, "y", y)
        plus = spread(plus, "core", core)
        plus = plus.reshape(core, y, zl, zh, thin, rows).transpose(2, 1, 3, 0, 4, 5).reshape(n, rows)

        half = jnp.einsum("qik,kj->qij", coulomb, minus, preferred_element_type=F32).astype(BF)

        me = lax.axis_index("row")
        left = lax.ppermute(half, "row", shift(row, 1))
        right = lax.ppermute(half, "row", shift(row, -1))
        cut = rows // 2
        top = lax.ppermute(left[:, :cut], "row", shift(row, 1))
        bottom = lax.ppermute(right[:, cut:], "row", shift(row, -1))

        def part(strip, owner, start):
            size = strip.shape[1]
            block = lax.dynamic_slice_in_dim(plus, owner * rows + start, size, axis=0)
            return jnp.einsum("ki,qkj->qij", block, strip, preferred_element_type=F32)

        pair = part(half, me, 0)
        pair += part(left, (me + row - 1) % row, 0)
        pair += part(right, (me + 1) % row, 0)
        pair += part(top, (me + 2) % row, 0)
        pair += part(bottom, (me + 2) % row, cut)
        total = jnp.sum(pair * half.astype(F32), axis=0)

        total = lax.all_to_all(total.astype(BF).reshape(y, rows // y, cols), "y", 0, 0)
        total = jnp.sum(total.astype(F32), axis=0)
        total = lax.all_to_all(total.astype(BF).reshape(zl, rows // y // zl, cols), "zl", 0, 0)
        total = -jnp.sum(total.astype(F32), axis=0)
        whole = spread(total.astype(BF), "zl", zl)
        whole = spread(whole, "y", y)
        return whole.reshape(rows, cols)

    in_specs = (
        P("row", ("zl", "y", "zh", "core")),
        P(("zl", "y", "row"), ("zh", "core")),
        P(("zl", "y"), "row", None),
    )
    out_specs = P("row", ("zh", "core"))
    return jax.shard_map(local, mesh=fine, in_specs=in_specs, out_specs=out_specs, check_vma=False)
```

time: 1740 us -> 193 us (0.11)
  the two profiles are of different devices: /device:TPU:2 before, /device:TPU:8 now
where the time goes in v1:
time: 193 us; the launch traced here: 192 us
  blocking collectives  143 us (74%)
  starting transfers between devices  17.6 us (9%)
  waiting for transfers between devices  16.6 us (9%)
  local copies, waits for them, and re-layouts  7.48 us (4%)
  matrix products  7.28 us (4%)
    all_to_all x6, blocking collectives, spread(): lax.all_to_all(jnp.broadcast_to(block[None], (count,) + block.shape), axe...  109 us
    all_to_all x1, blocking collectives, local(): lax.all_to_all(total.astype(BF).reshape(zl, rows // y // zl, cols), 'zl',...  23 us
    all_to_all x1, blocking collectives, local(): lax.all_to_all(total.astype(BF).reshape(y, rows // y, cols), 'y', 0, 0)  11.2 us
    ppermute x1, waiting for transfers between devices, local(): right = lax.ppermute(half, 'row', shift(row, -1))  10.1 us
    ppermute x1, waiting for transfers between devices, local(): top = lax.ppermute(left[:, :cut], 'row', shift(row, 1))  6.51 us
    all_to_all x1, starting transfers between devices, spread(): lax.all_to_all(jnp.broadcast_to(block[None], (count,) + block.shape), axe...  5.89 us
    dot_general x5, matrix products, part(): return jnp.einsum('ki,qkj->qij', block, strip, preferred_element_type=F32)  4.96 us
  transfers between devices with their start and end apart: 5, of which 2 were waited for; matrix products, arithmetic and copies ran while one was open for 4% of the time, Pallas kernels for 0%

profile of v1, /device:TPU:8, one launch (start us, length us, event | category | flops | bytes accessed | tf_op | source)
XLA Modules:
  0.0 192.4 jit_solution(18166698346244800232)
XLA Ops:
  0.0 0.7 broadcast_in_dim.14
  0.7 24.3 %all_to_all.45 = bf16[8,16,512]{2,1,0:T(8,128)(2,1)S(1)} all-to-all(bf16[8,16,512]{2,1,0:T(8,128)(2,1)S(1)} %broadcast_in_dim.14), channel_id=1, replica_groups=mesh['zl'=8,'y'=4,'row'=4,'zh'=2,'core'=2] {'zl'}, dimensions={0} | all-to-all | bytes 262144 | tf_op jit(solution)/shard_map/all_to_all | solution.py:11
  25.0 0.7 broadcast_in_dim.16
  25.7 25.9 %all_to_all.46 = bf16[16,16,512]{2,1,0:T(8,128)(2,1)S(1)} all-to-all(bf16[16,16,512]{2,1,0:T(8,128)(2,1)S(1)} %broadcast_in_dim.16), channel_id=1, replica_groups=mesh['zl'=8,'y'=4,'row'=4,'zh'=2,'core'=2] {'zl','zh'}, dimensions={0} | all-to-all | bytes 524288 | tf_op jit(solution)/shard_map/all_to_all | solution.py:11
  51.7 0.3 broadcast_in_dim.15
  51.9 28.4 %all_to_all.47 = bf16[16,8,16,512]{3,2,1,0:T(8,128)(2,1)S(1)} all-to-all(bf16[16,8,16,512]{3,2,1,0:T(8,128)(2,1)S(1)} %broadcast_in_dim.15), channel_id=1, replica_groups=mesh['zl'=8,'y'=4,'row'=4,'zh'=2,'core'=2] {'y','row'}, dimensions={0} | all-to-all | bytes 4194304 | tf_op jit(solution)/shard_map/all_to_all | solution.py:11
  80.3 1.2 broadcast_in_dim.17
  81.5 5.9 %all-to-all-start.3 = ((bf16[4,16,16,512]{3,2,1,0:T(8,128)(2,1)}), bf16[4,16,16,512]{3,2,1,0:T(8,128)(2,1)S(1)}, u32[]{:S(2)}, u32[]{:S(2)}) async-start(bf16[4,16,16,512]{3,2,1,0:T(8,128)(2,1)} %broadcast_in_dim.17), calls=%async_computation.3 | async-start | bytes 2097152 | tf_op jit(solution)/shard_map/all_to_all | solution.py:11
  87.4 0.2 copy.37
  87.6 2.0 %copy-done = bf16[2,512,2048]{2,1,0:T(8,128)(2,1)S(1)} copy-done((bf16[2,512,2048]{2,1,0:T(8,128)(2,1)S(1)}, bf16[2,512,2048]{2,1,0:T(8,128)(2,1)}, u32[]{:S(2)}) %copy-start) | copy-done | bytes 4194328
  89.6 2.3 %convolution_convert_fusion = bf16[2,512,512]{2,1,0:T(8,128)(2,1)S(1)} fusion(bf16[2,512,2048]{2,1,0:T(8,128)(2,1)S(1)} %copy-done, bf16[2048,512,1]{1,0,2:T(8,128)(2,1)S(1)} %bitcast.49), kind=kOutput, calls=%fused_computation.2 | convolution fusion | flops 2148007936 | bytes 7340032 | tf_op jit(solution)/shard_map/qik,kj->qij/dot_general | solution.py:36
  91.9 2.2 %collective-permute-start.1 = (bf16[2,512,512]{2,1,0:T(8,128)(2,1)S(1)}, bf16[2,512,512]{2,1,0:T(8,128)(2,1)S(1)}, u32[]{:S(2)}, u32[]{:S(2)}) collective-permute-start(bf16[2,512,512]{2,1,0:T(8,128)(2,1)S(1)} %convolution_convert_fusion), channel_id=1, source_target_pairs={{0,12},{4,0},{8,4},{12,8},{1,13},{5,1},{9,5},{13,9},{2,14},{6,2},{... | collective-permute-start | bytes 3145736 | tf_op jit(solution)/shard_map/ppermute | solution.py:40
  94.1 3.6 %collective-permute-start = (bf16[2,512,512]{2,1,0:T(8,128)(2,1)S(1)}, bf16[2,512,512]{2,1,0:T(8,128)(2,1)}, u32[]{:S(2)}, u32[]{:S(2)}) collective-permute-start(bf16[2,512,512]{2,1,0:T(8,128)(2,1)S(1)} %convolution_convert_fusion), channel_id=1, source_target_pairs={{0,4},{4,8},{8,12},{12,0},{1,5},{5,9},{9,13},{13,1},{2,6},{6,10},{... | collective-permute-start | bytes 3145736 | tf_op jit(solution)/shard_map/ppermute | solution.py:39
  97.8 0.3 broadcast_in_dim.18
  98.1 5.4 %all_to_all.48 = bf16[2,4,16,16,512]{4,3,2,1,0:T(8,128)(2,1)S(1)} all-to-all(bf16[2,4,16,16,512]{4,3,2,1,0:T(8,128)(2,1)S(1)} %broadcast_in_dim.18), channel_id=1, replica_groups=mesh['zl'=8,'y'=4,'row'=4,'zh'=2,'core'=2] {'core'}, dimensions={0} | all-to-all | bytes 4194304 | tf_op jit(solution)/shard_map/all_to_all | solution.py:11
  103.5 0.2 copy.38
  103.7 0.8 fusion.5
  104.5 10.1 %collective-permute-done.1 = bf16[2,512,512]{2,1,0:T(8,128)(2,1)S(1)} collective-permute-done((bf16[2,512,512]{2,1,0:T(8,128)(2,1)S(1)}, bf16[2,512,512]{2,1,0:T(8,128)(2,1)S(1)}, u32[]{:S(2)}, u32[]{:S(2)}) %collective-permute-start.1) | collective-permute-done | bytes 1048608 | tf_op jit(solution)/shard_map/ppermute | solution.py:40
  114.6 2.8 %collective-permute-start.3 = (bf16[2,256,512]{2,1,0:T(8,128)(2,1)S(1)}, bf16[2,256,512]{2,1,0:T(8,128)(2,1)S(1)}, u32[]{:S(2)}, u32[]{:S(2)}) collective-permute-start(bf16[2,256,512]{2,1,0:T(8,128)(2,1)S(1)} %slice.9), channel_id=1, source_target_pairs={{0,12},{4,0},{8,4},{12,8},{1,13},{5,1},{9,5},{13,9},{2,14},{6,2},{... | collective-permute-start | bytes 1572872 | tf_op jit(solution)/shard_map/ppermute | solution.py:43
  117.5 1.1 slice.8
  118.5 3.0 %collective-permute-start.2 = (bf16[2,256,512]{2,1,0:T(8,128)(2,1)S(1)}, bf16[2,256,512]{2,1,0:T(8,128)(2,1)S(1)}, u32[]{:S(2)}, u32[]{:S(2)}) collective-permute-start(bf16[2,256,512]{2,1,0:T(8,128)(2,1)S(1)} %slice.8), channel_id=1, source_target_pairs={{0,4},{4,8},{8,12},{12,0},{1,5},{5,9},{9,13},{13,1},{2,6},{6,10},{... | collective-permute-start | bytes 1572872 | tf_op jit(solution)/shard_map/ppermute | solution.py:42
  121.6 0.8 fusion.1
  122.3 2.0 %fusion.3 = f32[2,512,512]{1,2,0:T(8,128)S(1)} fusion(bf16[2,512,512]{2,1,0:T(8,128)(2,1)} %collective-permute-done, bf16[2048,512]{1,0:T(8,128)(2,1)S(1)} %bitcast.44, s32[]{:T(128)S(6)} %select_n.34), kind=kOutput, calls=%fused_computation.5 | convolution fusion | flops 536870912 | bytes 3670020 | tf_op jit(solution)/shard_map/ki,qkj->qij/dot_general | solution.py:48
  124.3 6.5 %collective-permute-done.2 = bf16[2,256,512]{2,1,0:T(8,128)(2,1)S(1)} collective-permute-done((bf16[2,256,512]{2,1,0:T(8,128)(2,1)S(1)}, bf16[2,256,512]{2,1,0:T(8,128)(2,1)S(1)}, u32[]{:S(2)}, u32[]{:S(2)}) %collective-permute-start.2) | collective-permute-done | bytes 524320 | tf_op jit(solution)/shard_map/ppermute | solution.py:42
  130.8 0.5 fusion.14
  131.3 1.0 fusion
  132.3 11.2 %all_to_all.49 = bf16[4,128,512]{2,1,0:T(8,128)(2,1)S(1)} all-to-all(bf16[4,128,512]{2,1,0:T(8,128)(2,1)S(1)} %bitcast.51), channel_id=1, replica_groups=mesh['zl'=8,'y'=4,'row'=4,'zh'=2,'core'=2] {'y'}, dimensions={0} | all-to-all | bytes 1048576 | tf_op jit(solution)/shard_map/all_to_all | solution.py:57
  143.5 0.1 reduce_sum.31
  143.6 23.0 %all_to_all.50 = bf16[8,16,512]{2,1,0:T(8,128)(2,1)S(1)} all-to-all(bf16[8,16,512]{2,1,0:T(8,128)(2,1)S(1)} %bitcast.52), channel_id=1, replica_groups=mesh['zl'=8,'y'=4,'row'=4,'zh'=2,'core'=2] {'zl'}, dimensions={0} | all-to-all | bytes 262144 | tf_op jit(solution)/shard_map/all_to_all | solution.py:59
  166.7 14.4 %all_to_all.51 = bf16[8,16,512]{2,1,0:T(8,128)(2,1)S(1)} all-to-all(bf16[8,16,512]{2,1,0:T(8,128)(2,1)S(1)} %broadcast_in_dim.19), channel_id=1, replica_groups=mesh['zl'=8,'y'=4,'row'=4,'zh'=2,'core'=2] {'zl'}, dimensions={0} | all-to-all | bytes 262144 | tf_op jit(solution)/shard_map/all_to_all | solution.py:11
  181.2 10.5 %all_to_all.52 = bf16[4,8,16,512]{3,2,1,0:T(8,128)(2,1)S(1)} all-to-all(bf16[4,8,16,512]{3,2,1,0:T(8,128)(2,1)S(1)} %broadcast_in_dim.20), channel_id=1, replica_groups=mesh['zl'=8,'y'=4,'row'=4,'zh'=2,'core'=2] {'y'}, dimensions={0} | all-to-all | bytes 1048576 | tf_op jit(solution)/shard_map/all_to_all | solution.py:11
  191.6 0.8 copy.60
  (9 shorter events, 0.1 us)
Async XLA Ops:
  81.5 16.3 %all-to-all-start.3 = ((bf16[4,16,16,512]{3,2,1,0:T(8,128)(2,1)}), bf16[4,16,16,512]{3,2,1,0:T(8,128)(2,1)S(1)}, u32[]{:S(2)}, u32[]{:S(2)}) async-start(bf16[4,16,16,512]{3,2,1,0:T(8,128)(2,1)} %broadcast_in_dim.17), calls=%async_computation.3 | async-start | bytes 2097152 | tf_op jit(solution)/shard_map/all_to_all | solution.py:11
  87.4 2.2 %copy-start = (bf16[2,512,2048]{2,1,0:T(8,128)(2,1)S(1)}, bf16[2,512,2048]{2,1,0:T(8,128)(2,1)}, u32[]{:S(2)}) copy-start(bf16[2,512,2048]{2,1,0:T(8,128)(2,1)} %param.5) | copy-start | bytes 12582916
  91.9 22.7 %collective-permute-start.1 = (bf16[2,512,512]{2,1,0:T(8,128)(2,1)S(1)}, bf16[2,512,512]{2,1,0:T(8,128)(2,1)S(1)}, u32[]{:S(2)}, u32[]{:S(2)}) collective-permute-start(bf16[2,512,512]{2,1,0:T(8,128)(2,1)S(1)} %convolution_convert_fusion), channel_id=1, source_target_pairs={{0,12},{4,0},{8,4},{12,8},{1,13},{5,1},{9,5},{13,9},{2,14},{6,2},{... | collective-permute-start | bytes 3145736 | tf_op jit(solution)/shard_map/ppermute | solution.py:40
  94.1 23.3 %collective-permute-start = (bf16[2,512,512]{2,1,0:T(8,128)(2,1)S(1)}, bf16[2,512,512]{2,1,0:T(8,128)(2,1)}, u32[]{:S(2)}, u32[]{:S(2)}) collective-permute-start(bf16[2,512,512]{2,1,0:T(8,128)(2,1)S(1)} %convolution_convert_fusion), channel_id=1, source_target_pairs={{0,4},{4,8},{8,12},{12,0},{1,5},{5,9},{9,13},{13,1},{2,6},{6,10},{... | collective-permute-start | bytes 3145736 | tf_op jit(solution)/shard_map/ppermute | solution.py:39
  114.6 16.7 %collective-permute-start.3 = (bf16[2,256,512]{2,1,0:T(8,128)(2,1)S(1)}, bf16[2,256,512]{2,1,0:T(8,128)(2,1)S(1)}, u32[]{:S(2)}, u32[]{:S(2)}) collective-permute-start(bf16[2,256,512]{2,1,0:T(8,128)(2,1)S(1)} %slice.9), channel_id=1, source_target_pairs={{0,12},{4,0},{8,4},{12,8},{1,13},{5,1},{9,5},{13,9},{2,14},{6,2},{... | collective-permute-start | bytes 1572872 | tf_op jit(solution)/shard_map/ppermute | solution.py:43
  118.5 12.3 %collective-permute-start.2 = (bf16[2,256,512]{2,1,0:T(8,128)(2,1)S(1)}, bf16[2,256,512]{2,1,0:T(8,128)(2,1)S(1)}, u32[]{:S(2)}, u32[]{:S(2)}) collective-permute-start(bf16[2,256,512]{2,1,0:T(8,128)(2,1)S(1)} %slice.8), channel_id=1, source_target_pairs={{0,4},{4,8},{8,12},{12,0},{1,5},{5,9},{9,13},{13,1},{2,6},{6,10},{... | collective-permute-start | bytes 1572872 | tf_op jit(solution)/shard_map/ppermute | solution.py:42

commit v2 on v1

--- a/solution.py
+++ b/solution.py
@@ -27,13 +27,14 @@
         minus = spread(g_minus, "zl", zl)
         minus = spread(minus, ("y", "row"), y * row)
         minus = minus.reshape(y, row, zl, depth, cols).transpose(2, 0, 1, 3, 4).reshape(n, cols)
+        half = jnp.einsum("qik,kj->qij", coulomb, minus, preferred_element_type=F32).astype(BF)
+
         thin = g_plus.shape[1]
-        plus = spread(g_plus.T, ("zl", "zh"), zl * zh)
+        plus = lax.all_gather(g_plus.T, ("zl", "zh"), axis=0, tiled=True)
+        plus, later = lax.optimization_barrier((plus, half))
         plus = spread(plus, "y", y)
         plus = spread(plus, "core", core)
         plus = plus.reshape(core, y, zl, zh, thin, rows).transpose(2, 1, 3, 0, 4, 5).reshape(n, rows)
-
-        half = jnp.einsum("qik,kj->qij", coulomb, minus, preferred_element_type=F32).astype(BF)
 
         me = lax.axis_index("row")
         left = lax.ppermute(half, "row", shift(row, 1))
@@ -52,7 +53,7 @@
         pair += part(right, (me + 1) % row, 0)
         pair += part(top, (me + 2) % row, 0)
         pair += part(bottom, (me + 2) % row, cut)
-        total = jnp.sum(pair * half.astype(F32), axis=0)
+        total = jnp.sum(pair * later.astype(F32), axis=0)
 
         total = lax.all_to_all(total.astype(BF).reshape(y, rows // y, cols), "y", 0, 0)
         total = jnp.sum(total.astype(F32), axis=0)

time: 193 us -> 204 us (1.057)
  starting transfers between devices: 17.6 us -> 26.3 us
  blocking collectives: 143 us -> 147 us
  waiting for transfers between devices: 16.6 us -> 14 us
    all_gather x0 -> x1, blocking collectives: none -> 61.5 us  [local(): plus = lax.all_gather(g_plus.T, ('zl', 'zh'), axis=0, tiled=True)]
    all_to_all x6 -> x4, blocking collectives: 109 us -> 54.6 us  [spread(): lax.all_to_all(jnp.broadcast_to(block[None], (count,) + block.shape), axe...]
    ppermute x1, waiting for transfers between devices: 10.1 us -> 1.99 us  [local(): right = lax.ppermute(half, 'row', shift(row, -1))]
    all_to_all x1 -> x2, starting transfers between devices: 5.89 us -> 12.3 us  [spread(): lax.all_to_all(jnp.broadcast_to(block[None], (count,) + block.shape), axe...]
    all_to_all x1 -> x2, waiting for transfers between devices: 0.01 us -> 2.87 us  [spread(): lax.all_to_all(jnp.broadcast_to(block[None], (count,) + block.shape), axe...]
    ppermute x1, starting transfers between devices: 2.83 us -> 5.6 us  [local(): bottom = lax.ppermute(right[:, cut:], 'row', shift(row, -1))]
    ppermute x1, waiting for transfers between devices: 6.51 us -> 9.11 us  [local(): top = lax.ppermute(left[:, :cut], 'row', shift(row, 1))]
    ppermute x1, starting transfers between devices: 2.21 us -> 4.57 us  [local(): right = lax.ppermute(half, 'row', shift(row, -1))]
  transfers between devices with their start and end apart: 5 -> 6, of which waited for: 2 -> 3; matrix products, arithmetic and copies ran while one was open for 4% -> 3% of each run, Pallas kernels for 0% -> 0%
where the time goes in v2:
time: 204 us; the launch traced here: 203 us
  blocking collectives  147 us (72%)
  starting transfers between devices  26.3 us (13%)
  waiting for transfers between devices  14 us (7%)
  local copies, waits for them, and re-layouts  8.03 us (4%)
  matrix products  7.28 us (4%)
    all_gather x1, blocking collectives, local(): plus = lax.all_gather(g_plus.T, ('zl', 'zh'), axis=0, tiled=True)  61.5 us
    all_to_all x4, blocking collectives, spread(): lax.all_to_all(jnp.broadcast_to(block[None], (count,) + block.shape), axe...  54.6 us
    all_to_all x1, blocking collectives, local(): lax.all_to_all(total.astype(BF).reshape(zl, rows // y // zl, cols), 'zl',...  20.8 us
    all_to_all x2, starting transfers between devices, spread(): lax.all_to_all(jnp.broadcast_to(block[None], (count,) + block.shape), axe...  12.3 us
    all_to_all x1, blocking collectives, local(): lax.all_to_all(total.astype(BF).reshape(y, rows // y, cols), 'y', 0, 0)  10.5 us
    ppermute x1, waiting for transfers between devices, local(): top = lax.ppermute(left[:, :cut], 'row', shift(row, 1))  9.11 us
    ppermute x1, starting transfers between devices, local(): bottom = lax.ppermute(right[:, cut:], 'row', shift(row, -1))  5.6 us
    dot_general x5, matrix products, part(): return jnp.einsum('ki,qkj->qij', block, strip, preferred_element_type=F32)  4.97 us
  transfers between devices with their start and end apart: 6, of which 3 were waited for; matrix products, arithmetic and copies ran while one was open for 3% of the time, Pallas kernels for 0%

profile of v2, /device:TPU:8, one launch (start us, length us, event | category | flops | bytes accessed | tf_op | source)
XLA Modules:
  0.0 203.3 jit_solution(6668767578843190451)
XLA Ops:
  0.0 0.7 broadcast_in_dim.12
  0.7 24.3 %all_to_all.40 = bf16[8,16,512]{2,1,0:T(8,128)(2,1)S(1)} all-to-all(bf16[8,16,512]{2,1,0:T(8,128)(2,1)S(1)} %broadcast_in_dim.12), channel_id=1, replica_groups=mesh['zl'=8,'y'=4,'row'=4,'zh'=2,'core'=2] {'zl'}, dimensions={0} | all-to-all | bytes 262144 | tf_op jit(solution)/shard_map/all_to_all | solution.py:11
  25.0 1.6 broadcast_in_dim.13
  26.6 7.5 %all-to-all-start.1 = ((bf16[16,8,16,512]{3,2,1,0:T(8,128)(2,1)}), bf16[16,8,16,512]{3,2,1,0:T(8,128)(2,1)S(1)}, u32[]{:S(2)}, u32[]{:S(2)}) async-start(bf16[16,8,16,512]{3,2,1,0:T(8,128)(2,1)} %broadcast_in_dim.13), calls=%async_computation.1 | async-start | bytes 4194304 | tf_op jit(solution)/shard_map/all_to_all | solution.py:11
  34.1 61.5 %all_gather.3 = bf16[256,512]{1,0:T(8,128)(2,1)S(1)} all-gather(bf16[16,512]{1,0:T(8,128)(2,1)S(1)} %bitcast.53), channel_id=1, replica_groups=mesh['zl'=8,'y'=4,'row'=4,'zh'=2,'core'=2] {'zl','zh'}, dimensions={0}, use_global_device_ids=true | all-gather | bytes 278528 | tf_op jit(solution)/shard_map/all_gather | solution.py:33
  95.6 0.2 copy.37
  95.8 2.0 copy-done.1
  97.8 2.3 %convolution_convert_fusion = bf16[2,512,512]{2,1,0:T(8,128)(2,1)S(1)} fusion(bf16[2,512,2048]{2,1,0:T(8,128)(2,1)S(1)} %copy-done.1, bf16[2048,512,1]{1,0,2:T(8,128)(2,1)S(1)} %bitcast.49), kind=kOutput, calls=%fused_computation.2 | convolution fusion | flops 2148007936 | bytes 7340032 | tf_op jit(solution)/shard_map/qik,kj->qij/dot_general | solution.py:30
  100.1 1.1 broadcast_in_dim.14
  101.2 4.8 %all-to-all-start.2 = ((bf16[4,256,512]{2,1,0:T(8,128)(2,1)}), bf16[4,256,512]{2,1,0:T(8,128)(2,1)S(1)}, u32[]{:S(2)}, u32[]{:S(2)}) async-start(bf16[4,256,512]{2,1,0:T(8,128)(2,1)} %broadcast_in_dim.14), calls=%async_computation.2 | async-start | bytes 2097152 | tf_op jit(solution)/shard_map/all_to_all | solution.py:11
  106.0 4.6 %collective-permute-start.1 = (bf16[2,512,512]{2,1,0:T(8,128)(2,1)S(1)}, bf16[2,512,512]{2,1,0:T(8,128)(2,1)S(1)}, u32[]{:S(2)}, u32[]{:S(2)}) collective-permute-start(bf16[2,512,512]{2,1,0:T(8,128)(2,1)S(1)} %convolution_convert_fusion), channel_id=1, source_target_pairs={{0,12},{4,0},{8,4},{12,8},{1,13},{5,1},{9,5},{13,9},{2,14},{6,2},{... | collective-permute-start | bytes 3145736 | tf_op jit(solution)/shard_map/ppermute | solution.py:41
  110.6 1.9 collective-permute-start
  112.6 2.9 %all-to-all-done.2 = bf16[4,256,512]{2,1,0:T(8,128)(2,1)S(1)} async-done(((bf16[4,256,512]{2,1,0:T(8,128)(2,1)}), bf16[4,256,512]{2,1,0:T(8,128)(2,1)S(1)}, u32[]{:S(2)}, u32[]{:S(2)}) %all-to-all-start.2) | async-done | bytes 1048608 | tf_op jit(solution)/shard_map/all_to_all | solution.py:11
  115.5 0.2 broadcast_in_dim.15
  115.7 5.4 %all_to_all.41 = bf16[2,4,256,512]{3,2,1,0:T(8,128)(2,1)S(1)} all-to-all(bf16[2,4,256,512]{3,2,1,0:T(8,128)(2,1)S(1)} %broadcast_in_dim.15), channel_id=1, replica_groups=mesh['zl'=8,'y'=4,'row'=4,'zh'=2,'core'=2] {'core'}, dimensions={0} | all-to-all | bytes 4194304 | tf_op jit(solution)/shard_map/all_to_all | solution.py:11
  121.1 0.3 copy.38
  121.3 0.8 fusion.5
  122.1 2.0 collective-permute-done.1
  124.1 5.6 %collective-permute-start.3 = (bf16[2,256,512]{2,1,0:T(8,128)(2,1)S(1)}, bf16[2,256,512]{2,1,0:T(8,128)(2,1)S(1)}, u32[]{:S(2)}, u32[]{:S(2)}) collective-permute-start(bf16[2,256,512]{2,1,0:T(8,128)(2,1)S(1)} %slice.9), channel_id=1, source_target_pairs={{0,12},{4,0},{8,4},{12,8},{1,13},{5,1},{9,5},{13,9},{2,14},{6,2},{... | collective-permute-start | bytes 1572872 | tf_op jit(solution)/shard_map/ppermute | solution.py:44
  129.8 1.1 slice.8
  130.9 1.9 collective-permute-start.2
  132.8 0.8 fusion.1
  133.6 2.0 fusion.3
  135.5 9.1 %collective-permute-done.2 = bf16[2,256,512]{2,1,0:T(8,128)(2,1)S(1)} collective-permute-done((bf16[2,256,512]{2,1,0:T(8,128)(2,1)S(1)}, bf16[2,256,512]{2,1,0:T(8,128)(2,1)S(1)}, u32[]{:S(2)}, u32[]{:S(2)}) %collective-permute-start.2) | collective-permute-done | bytes 524320 | tf_op jit(solution)/shard_map/ppermute | solution.py:43
  144.6 0.5 fusion.14
  145.2 1.0 fusion
  146.1 10.5 %all_to_all.42 = bf16[4,128,512]{2,1,0:T(8,128)(2,1)S(1)} all-to-all(bf16[4,128,512]{2,1,0:T(8,128)(2,1)S(1)} %bitcast.51), channel_id=1, replica_groups=mesh['zl'=8,'y'=4,'row'=4,'zh'=2,'core'=2] {'y'}, dimensions={0} | all-to-all | bytes 1048576 | tf_op jit(solution)/shard_map/all_to_all | solution.py:58
  156.6 0.1 reduce_sum.31
  156.7 20.8 %all_to_all.43 = bf16[8,16,512]{2,1,0:T(8,128)(2,1)S(1)} all-to-all(bf16[8,16,512]{2,1,0:T(8,128)(2,1)S(1)} %bitcast.52), channel_id=1, replica_groups=mesh['zl'=8,'y'=4,'row'=4,'zh'=2,'core'=2] {'zl'}, dimensions={0} | all-to-all | bytes 262144 | tf_op jit(solution)/shard_map/all_to_all | solution.py:60
  177.5 14.5 %all_to_all.44 = bf16[8,16,512]{2,1,0:T(8,128)(2,1)S(1)} all-to-all(bf16[8,16,512]{2,1,0:T(8,128)(2,1)S(1)} %broadcast_in_dim.16), channel_id=1, replica_groups=mesh['zl'=8,'y'=4,'row'=4,'zh'=2,'core'=2] {'zl'}, dimensions={0} | all-to-all | bytes 262144 | tf_op jit(solution)/shard_map/all_to_all | solution.py:11
  192.0 10.5 %all_to_all.45 = bf16[4,8,16,512]{3,2,1,0:T(8,128)(2,1)S(1)} all-to-all(bf16[4,8,16,512]{3,2,1,0:T(8,128)(2,1)S(1)} %broadcast_in_dim.17), channel_id=1, replica_groups=mesh['zl'=8,'y'=4,'row'=4,'zh'=2,'core'=2] {'y'}, dimensions={0} | all-to-all | bytes 1048576 | tf_op jit(solution)/shard_map/all_to_all | solution.py:11
  202.5 0.8 copy.60
  (11 shorter events, 0.1 us)
Async XLA Ops:
  26.6 7.5 %copy-start = (bf16[512,16]{0,1:T(8,128)(2,1)S(1)}, bf16[512,16]{0,1:T(8,128)(2,1)}, u32[]{:S(2)}) copy-start(bf16[512,16]{0,1:T(8,128)(2,1)} %param.3) | copy-start | bytes 49156
  26.6 69.0 %all-to-all-start.1 = ((bf16[16,8,16,512]{3,2,1,0:T(8,128)(2,1)}), bf16[16,8,16,512]{3,2,1,0:T(8,128)(2,1)S(1)}, u32[]{:S(2)}, u32[]{:S(2)}) async-start(bf16[16,8,16,512]{3,2,1,0:T(8,128)(2,1)} %broadcast_in_dim.13), calls=%async_computation.1 | async-start | bytes 4194304 | tf_op jit(solution)/shard_map/all_to_all | solution.py:11
  95.6 2.2 %copy-start.1 = (bf16[2,512,2048]{2,1,0:T(8,128)(2,1)S(1)}, bf16[2,512,2048]{2,1,0:T(8,128)(2,1)}, u32[]{:S(2)}) copy-start(bf16[2,512,2048]{2,1,0:T(8,128)(2,1)} %param.5) | copy-start | bytes 12582916
  101.2 14.2 %all-to-all-start.2 = ((bf16[4,256,512]{2,1,0:T(8,128)(2,1)}), bf16[4,256,512]{2,1,0:T(8,128)(2,1)S(1)}, u32[]{:S(2)}, u32[]{:S(2)}) async-start(bf16[4,256,512]{2,1,0:T(8,128)(2,1)} %broadcast_in_dim.14), calls=%async_computation.2 | async-start | bytes 2097152 | tf_op jit(solution)/shard_map/all_to_all | solution.py:11
  106.0 18.1 %collective-permute-start.1 = (bf16[2,512,512]{2,1,0:T(8,128)(2,1)S(1)}, bf16[2,512,512]{2,1,0:T(8,128)(2,1)S(1)}, u32[]{:S(2)}, u32[]{:S(2)}) collective-permute-start(bf16[2,512,512]{2,1,0:T(8,128)(2,1)S(1)} %convolution_convert_fusion), channel_id=1, source_target_pairs={{0,12},{4,0},{8,4},{12,8},{1,13},{5,1},{9,5},{13,9},{2,14},{6,2},{... | collective-permute-start | bytes 3145736 | tf_op jit(solution)/shard_map/ppermute | solution.py:41
  110.6 19.1 %collective-permute-start = (bf16[2,512,512]{2,1,0:T(8,128)(2,1)S(1)}, bf16[2,512,512]{2,1,0:T(8,128)(2,1)}, u32[]{:S(2)}, u32[]{:S(2)}) collective-permute-start(bf16[2,512,512]{2,1,0:T(8,128)(2,1)S(1)} %convolution_convert_fusion), channel_id=1, source_target_pairs={{0,4},{4,8},{8,12},{12,0},{1,5},{5,9},{9,13},{13,1},{2,6},{6,10},{... | collective-permute-start | bytes 3145736 | tf_op jit(solution)/shard_map/ppermute | solution.py:40
  124.1 21.0 %collective-permute-start.3 = (bf16[2,256,512]{2,1,0:T(8,128)(2,1)S(1)}, bf16[2,256,512]{2,1,0:T(8,128)(2,1)S(1)}, u32[]{:S(2)}, u32[]{:S(2)}) collective-permute-start(bf16[2,256,512]{2,1,0:T(8,128)(2,1)S(1)} %slice.9), channel_id=1, source_target_pairs={{0,12},{4,0},{8,4},{12,8},{1,13},{5,1},{9,5},{13,9},{2,14},{6,2},{... | collective-permute-start | bytes 1572872 | tf_op jit(solution)/shard_map/ppermute | solution.py:44
  130.9 13.8 %collective-permute-start.2 = (bf16[2,256,512]{2,1,0:T(8,128)(2,1)S(1)}, bf16[2,256,512]{2,1,0:T(8,128)(2,1)S(1)}, u32[]{:S(2)}, u32[]{:S(2)}) collective-permute-start(bf16[2,256,512]{2,1,0:T(8,128)(2,1)S(1)} %slice.8), channel_id=1, source_target_pairs={{0,4},{4,8},{8,12},{12,0},{1,5},{5,9},{9,13},{13,1},{2,6},{6,10},{... | collective-permute-start | bytes 1572872 | tf_op jit(solution)/shard_map/ppermute | solution.py:43

commit v3 on v2

--- a/solution.py
+++ b/solution.py
@@ -15,6 +15,15 @@
     return [(index, (index + by) % count) for index in range(count)]
 
 
+def partner(block, axis):
+    return lax.ppermute(block, axis, shift(2, 1))
+
+
+def order(mine, theirs, axis):
+    first = lax.axis_index(axis) == 0
+    return jnp.stack([jnp.where(first, mine, theirs), jnp.where(first, theirs, mine)])
+
+
 def solution(mesh):
     aux, row, col = (mesh.shape[name] for name in ("aux", "row", "col"))
     zl, y, zh, core = aux // 4, 4, col // 2, 2
@@ -22,19 +31,19 @@
 
     def local(g_plus, g_minus, coulomb):
         count, rows, n = coulomb.shape
-        cols = g_minus.shape[1]
-        depth = g_minus.shape[0]
-        minus = spread(g_minus, "zl", zl)
+        depth, cols = g_minus.shape
+        thin = g_plus.shape[1]
+        slabs = spread(jnp.concatenate([g_minus, g_plus.T]), "zl", zl)
+        minus, plus = slabs[:, :depth], slabs[:, depth:]
+        theirs = partner(plus, "zh")
         minus = spread(minus, ("y", "row"), y * row)
         minus = minus.reshape(y, row, zl, depth, cols).transpose(2, 0, 1, 3, 4).reshape(n, cols)
         half = jnp.einsum("qik,kj->qij", coulomb, minus, preferred_element_type=F32).astype(BF)
 
-        thin = g_plus.shape[1]
-        plus = lax.all_gather(g_plus.T, ("zl", "zh"), axis=0, tiled=True)
-        plus, later = lax.optimization_barrier((plus, half))
-        plus = spread(plus, "y", y)
-        plus = spread(plus, "core", core)
-        plus = plus.reshape(core, y, zl, zh, thin, rows).transpose(2, 1, 3, 0, 4, 5).reshape(n, rows)
+        plus, theirs, later = lax.optimization_barrier((plus, theirs, half))
+        plus = spread(order(plus, theirs, "zh"), "y", y)
+        plus = order(plus, partner(plus, "core"), "core")
+        plus = plus.reshape(core, y, zh, zl, thin, rows).transpose(3, 1, 2, 0, 4, 5).reshape(n, rows)
 
         me = lax.axis_index("row")
         left = lax.ppermute(half, "row", shift(row, 1))

time: 204 us -> 179 us (0.88)
  blocking collectives: 147 us -> 91.3 us
  waiting for transfers between devices: 14 us -> 34.2 us
  starting transfers between devices: 26.3 us -> 34.7 us
  other arithmetic: 0.11 us -> 3.95 us
    all_gather x1 -> x0, blocking collectives: 61.5 us -> none  [local(): plus = lax.all_gather(g_plus.T, ('zl', 'zh'), axis=0, tiled=True)]
    all_to_all x2, waiting for transfers between devices: 2.87 us -> 19.5 us  [spread(): lax.all_to_all(jnp.broadcast_to(block[None], (count,) + block.shape), axe...]
    ppermute x0 -> x2, starting transfers between devices: none -> 10.1 us  [partner(): return lax.ppermute(block, axis, shift(2, 1))]
    ppermute x1, waiting for transfers between devices: 1.99 us -> 10.8 us  [local(): right = lax.ppermute(half, 'row', shift(row, -1))]
    all_to_all x1, blocking collectives: 20.8 us -> 26.2 us  [local(): lax.all_to_all(total.astype(BF).reshape(zl, rows // y // zl, cols), 'zl',...]
    ppermute x1, waiting for transfers between devices: 9.11 us -> 3.85 us  [local(): top = lax.ppermute(left[:, :cut], 'row', shift(row, 1))]
    ppermute x1, starting transfers between devices: 5.6 us -> 1.92 us  [local(): bottom = lax.ppermute(right[:, cut:], 'row', shift(row, -1))]
    ppermute x1, starting transfers between devices: 4.57 us -> 1.91 us  [local(): right = lax.ppermute(half, 'row', shift(row, -1))]
  transfers between devices with their start and end apart: 6 -> 8, of which waited for: 3 -> 4; matrix products, arithmetic and copies ran while one was open for 3% -> 5% of each run, Pallas kernels for 0% -> 0%
where the time goes in v3:
time: 179 us; the launch traced here: 178 us
  blocking collectives  91.3 us (51%)
  starting transfers between devices  34.7 us (19%)
  waiting for transfers between devices  34.2 us (19%)
  local copies, waits for them, and re-layouts  7.43 us (4%)
  matrix products  6.58 us (4%)
  other arithmetic  3.95 us (2%)
    all_to_all x3, blocking collectives, spread(): lax.all_to_all(jnp.broadcast_to(block[None], (count,) + block.shape), axe...  53.9 us
    all_to_all x1, blocking collectives, local(): lax.all_to_all(total.astype(BF).reshape(zl, rows // y // zl, cols), 'zl',...  26.2 us
    all_to_all x2, waiting for transfers between devices, spread(): lax.all_to_all(jnp.broadcast_to(block[None], (count,) + block.shape), axe...  19.5 us
    all_to_all x2, starting transfers between devices, spread(): lax.all_to_all(jnp.broadcast_to(block[None], (count,) + block.shape), axe...  12.9 us
    all_to_all x1, blocking collectives, local(): lax.all_to_all(total.astype(BF).reshape(y, rows // y, cols), 'y', 0, 0)  11.2 us
    ppermute x1, waiting for transfers between devices, local(): right = lax.ppermute(half, 'row', shift(row, -1))  10.8 us
    ppermute x2, starting transfers between devices, partner(): return lax.ppermute(block, axis, shift(2, 1))  10.1 us
    dot_general x5, matrix products, part(): return jnp.einsum('ki,qkj->qij', block, strip, preferred_element_type=F32)  4.2 us
  transfers between devices with their start and end apart: 8, of which 4 were waited for; matrix products, arithmetic and copies ran while one was open for 5% of the time, Pallas kernels for 0%

profile of v3, /device:TPU:8, one launch (start us, length us, event | category | flops | bytes accessed | tf_op | source)
XLA Modules:
  0.0 178.4 jit_solution(305849393947710918)
XLA Ops:
  0.0 0.7 pad_maximum_fusion.1
  0.8 29.0 %all_to_all.35 = bf16[8,32,512]{2,1,0:T(8,128)(2,1)S(1)} all-to-all(bf16[8,32,512]{2,1,0:T(8,128)(2,1)S(1)} %broadcast_in_dim.10), channel_id=1, replica_groups=mesh['zl'=8,'y'=4,'row'=4,'zh'=2,'core'=2] {'zl'}, dimensions={0} | all-to-all | bytes 524288 | tf_op jit(solution)/shard_map/all_to_all | solution.py:11
  29.8 1.6 broadcast_in_dim.11
  31.4 7.4 %all-to-all-start.1 = ((bf16[16,8,16,512]{3,2,1,0:T(8,128)(2,1)}), bf16[16,8,16,512]{3,2,1,0:T(8,128)(2,1)S(1)}, u32[]{:S(2)}, u32[]{:S(2)}) async-start(bf16[16,8,16,512]{3,2,1,0:T(8,128)(2,1)} %broadcast_in_dim.11), calls=%async_computation.1 | async-start | bytes 4194304 | tf_op jit(solution)/shard_map/all_to_all | solution.py:11
  38.8 8.2 %collective-permute-start = (bf16[8,16,512]{2,1,0:T(8,128)(2,1)S(1)}, bf16[8,16,512]{2,1,0:T(8,128)(2,1)S(1)}, u32[]{:S(2)}, u32[]{:S(2)}) collective-permute-start(bf16[8,16,512]{2,1,0:T(8,128)(2,1)S(1)} %get-tuple-element.8), channel_id=1, source_target_pairs={{0,2},{2,0},{1,3},{3,1},{4,6},{6,4},{5,7},{7,5},{8,10},{10,8},{9,1... | collective-permute-start | bytes 393224 | tf_op jit(solution)/shard_map/ppermute | solution.py:19
  47.0 15.9 %all-to-all-done.1 = bf16[16,8,16,512]{3,2,1,0:T(8,128)(2,1)S(1)} async-done(((bf16[16,8,16,512]{3,2,1,0:T(8,128)(2,1)}), bf16[16,8,16,512]{3,2,1,0:T(8,128)(2,1)S(1)}, u32[]{:S(2)}, u32[]{:S(2)}) %all-to-all-start.1) | async-done | bytes 2097184 | tf_op jit(solution)/shard_map/all_to_all | solution.py:11
  63.2 1.9 %copy-done = bf16[2,512,2048]{2,1,0:T(8,128)(2,1)S(1)} copy-done((bf16[2,512,2048]{2,1,0:T(8,128)(2,1)S(1)}, bf16[2,512,2048]{2,1,0:T(8,128)(2,1)}, u32[]{:S(2)}) %copy-start) | copy-done | bytes 4194328
  65.1 2.4 %fusion.1 = bf16[2,512,512]{1,2,0:T(8,128)(2,1)S(1)} fusion(bf16[2048,512,1]{1,0,2:T(8,128)(2,1)S(1)} %bitcast.61, bf16[2,512,2048]{2,1,0:T(8,128)(2,1)S(1)} %copy-done), kind=kOutput, calls=%fused_computation.4 | convolution fusion | flops 2148007936 | bytes 7340032 | tf_op jit(solution)/shard_map/qik,kj->qij/dot_general | solution.py:41
  67.6 1.2 broadcast_in_dim.12
  68.8 5.5 %all-to-all-start.2 = ((bf16[4,2,8,16,512]{4,3,1,2,0:T(8,128)(2,1)}), bf16[4,2,8,16,512]{4,3,1,2,0:T(8,128)(2,1)S(1)}, u32[]{:S(2)}, u32[]{:S(2)}) async-start(bf16[4,2,8,16,512]{4,3,1,2,0:T(8,128)(2,1)} %broadcast_in_dim.12), calls=%async_computation.2 | async-start | bytes 2097152 | tf_op jit(solution)/shard_map/all_to_all | solution.py:11
  74.2 1.9 %collective-permute-start.3 = (bf16[2,512,512]{1,2,0:T(8,128)(2,1)S(1)}, bf16[2,512,512]{1,2,0:T(8,128)(2,1)}, u32[]{:S(2)}, u32[]{:S(2)}) collective-permute-start(bf16[2,512,512]{1,2,0:T(8,128)(2,1)S(1)} %fusion.1), channel_id=1, source_target_pairs={{0,12},{4,0},{8,4},{12,8},{1,13},{5,1},{9,5},{13,9},{2,14},{6,2},{... | collective-permute-start | bytes 3145736 | tf_op jit(solution)/shard_map/ppermute | solution.py:50
  76.2 3.9 %collective-permute-start.2 = (bf16[2,512,512]{1,2,0:T(8,128)(2,1)S(1)}, bf16[2,512,512]{1,2,0:T(8,128)(2,1)S(1)}, u32[]{:S(2)}, u32[]{:S(2)}) collective-permute-start(bf16[2,512,512]{1,2,0:T(8,128)(2,1)S(1)} %fusion.1), channel_id=1, source_target_pairs={{0,4},{4,8},{8,12},{12,0},{1,5},{5,9},{9,13},{13,1},{2,6},{6,10},{... | collective-permute-start | bytes 3145736 | tf_op jit(solution)/shard_map/ppermute | solution.py:49
  80.1 3.6 %all-to-all-done.2 = bf16[4,2,8,16,512]{4,3,1,2,0:T(8,128)(2,1)S(1)} async-done(((bf16[4,2,8,16,512]{4,3,1,2,0:T(8,128)(2,1)}), bf16[4,2,8,16,512]{4,3,1,2,0:T(8,128)(2,1)S(1)}, u32[]{:S(2)}, u32[]{:S(2)}) %all-to-all-start.2) | async-done | bytes 1048608 | tf_op jit(solution)/shard_map/all_to_all | solution.py:11
  83.7 1.9 %collective-permute-start.1 = (bf16[4,2,8,16,512]{4,3,1,2,0:T(8,128)(2,1)S(1)}, bf16[4,2,8,16,512]{4,3,1,2,0:T(8,128)(2,1)}, u32[]{:S(2)}, u32[]{:S(2)}) collective-permute-start(bf16[4,2,8,16,512]{4,3,1,2,0:T(8,128)(2,1)S(1)} %all-to-all-done.2), channel_id=1, source_target_pairs={{0,1},{1,0},{2,3},{3,2},{4,5},{5,4},{6,7},{7,6},{8,9},{9,8},{10,11... | collective-permute-start | bytes 3145736 | tf_op jit(solution)/shard_map/ppermute | solution.py:19
  85.7 10.8 %collective-permute-done.3 = bf16[2,512,512]{1,2,0:T(8,128)(2,1)} collective-permute-done((bf16[2,512,512]{1,2,0:T(8,128)(2,1)S(1)}, bf16[2,512,512]{1,2,0:T(8,128)(2,1)}, u32[]{:S(2)}, u32[]{:S(2)}) %collective-permute-start.3) | collective-permute-done | bytes 1048608 | tf_op jit(solution)/shard_map/ppermute | solution.py:50
  96.5 1.1 slice.19
  97.6 1.9 %collective-permute-start.5 = (bf16[2,256,512]{1,2,0:T(8,128)(2,1)S(1)}, bf16[2,256,512]{1,2,0:T(8,128)(2,1)S(1)}, u32[]{:S(2)}, u32[]{:S(2)}) collective-permute-start(bf16[2,256,512]{1,2,0:T(8,128)(2,1)S(1)} %slice.19), channel_id=1, source_target_pairs={{0,12},{4,0},{8,4},{12,8},{1,13},{5,1},{9,5},{13,9},{2,14},{6,2},{... | collective-permute-start | bytes 1572872 | tf_op jit(solution)/shard_map/ppermute | solution.py:53
  99.5 3.9 %collective-permute-start.4 = (bf16[2,256,512]{1,2,0:T(8,128)(2,1)S(1)}, bf16[2,256,512]{1,2,0:T(8,128)(2,1)S(1)}, u32[]{:S(2)}, u32[]{:S(2)}) collective-permute-start(bf16[2,256,512]{1,2,0:T(8,128)(2,1)S(1)} %slice.18), channel_id=1, source_target_pairs={{0,4},{4,8},{8,12},{12,0},{1,5},{5,9},{9,13},{13,1},{2,6},{6,10},{... | collective-permute-start | bytes 1572872 | tf_op jit(solution)/shard_map/ppermute | solution.py:52
  103.5 1.4 select_bitcast_fusion.1
  105.1 0.3 copy.23
  105.3 0.7 fusion.6
  106.0 1.9 %fusion.2 = f32[2,512,512]{2,1,0:T(8,128)S(1)} fusion(bf16[2,512,512]{1,2,0:T(8,128)(2,1)} %collective-permute-done.3, bf16[2048,512]{1,0:T(8,128)(2,1)S(1)} %bitcast.57, s32[]{:T(128)S(6)} %select_n.66), kind=kOutput, calls=%fused_computation.8 | convolution fusion | flops 536870912 | bytes 3670020 | tf_op jit(solution)/shard_map/ki,qkj->qij/dot_general | solution.py:58
  108.0 3.9 %collective-permute-done.4 = bf16[2,256,512]{1,2,0:T(8,128)(2,1)S(1)} collective-permute-done((bf16[2,256,512]{1,2,0:T(8,128)(2,1)S(1)}, bf16[2,256,512]{1,2,0:T(8,128)(2,1)S(1)}, u32[]{:S(2)}, u32[]{:S(2)}) %collective-permute-start.4) | collective-permute-done | bytes 524320 | tf_op jit(solution)/shard_map/ppermute | solution.py:52
  111.8 0.4 fusion.13
  112.3 0.7 fusion.4
  113.0 0.4 fusion.11
  113.4 1.5 fusion
  115.0 11.2 %all_to_all.36 = bf16[4,128,512]{1,2,0:T(8,128)(2,1)S(1)} all-to-all(bf16[4,128,512]{1,2,0:T(8,128)(2,1)S(1)} %copy_bitcast_fusion), channel_id=1, replica_groups=mesh['zl'=8,'y'=4,'row'=4,'zh'=2,'core'=2] {'y'}, dimensions={0} | all-to-all | bytes 1048576 | tf_op jit(solution)/shard_map/all_to_all | solution.py:67
  126.4 26.2 %all_to_all.37 = bf16[8,16,512]{2,1,0:T(8,128)(2,1)S(1)} all-to-all(bf16[8,16,512]{2,1,0:T(8,128)(2,1)S(1)} %bitcast.63), channel_id=1, replica_groups=mesh['zl'=8,'y'=4,'row'=4,'zh'=2,'core'=2] {'zl'}, dimensions={0} | all-to-all | bytes 262144 | tf_op jit(solution)/shard_map/all_to_all | solution.py:69
  152.7 14.4 %all_to_all.38 = bf16[8,16,512]{2,1,0:T(8,128)(2,1)S(1)} all-to-all(bf16[8,16,512]{2,1,0:T(8,128)(2,1)S(1)} %broadcast_in_dim.13), channel_id=1, replica_groups=mesh['zl'=8,'y'=4,'row'=4,'zh'=2,'core'=2] {'zl'}, dimensions={0} | all-to-all | bytes 262144 | tf_op jit(solution)/shard_map/all_to_all | solution.py:11
  167.1 10.5 %all_to_all.39 = bf16[4,8,16,512]{3,2,1,0:T(8,128)(2,1)S(1)} all-to-all(bf16[4,8,16,512]{3,2,1,0:T(8,128)(2,1)S(1)} %broadcast_in_dim.14), channel_id=1, replica_groups=mesh['zl'=8,'y'=4,'row'=4,'zh'=2,'core'=2] {'y'}, dimensions={0} | all-to-all | bytes 1048576 | tf_op jit(solution)/shard_map/all_to_all | solution.py:11
  177.6 0.8 copy.33
  (20 shorter events, 1.0 us)
Async XLA Ops:
  31.4 31.5 %all-to-all-start.1 = ((bf16[16,8,16,512]{3,2,1,0:T(8,128)(2,1)}), bf16[16,8,16,512]{3,2,1,0:T(8,128)(2,1)S(1)}, u32[]{:S(2)}, u32[]{:S(2)}) async-start(bf16[16,8,16,512]{3,2,1,0:T(8,128)(2,1)} %broadcast_in_dim.11), calls=%async_computation.1 | async-start | bytes 4194304 | tf_op jit(solution)/shard_map/all_to_all | solution.py:11
  38.8 28.7 %collective-permute-start = (bf16[8,16,512]{2,1,0:T(8,128)(2,1)S(1)}, bf16[8,16,512]{2,1,0:T(8,128)(2,1)S(1)}, u32[]{:S(2)}, u32[]{:S(2)}) collective-permute-start(bf16[8,16,512]{2,1,0:T(8,128)(2,1)S(1)} %get-tuple-element.8), channel_id=1, source_target_pairs={{0,2},{2,0},{1,3},{3,1},{4,6},{6,4},{5,7},{7,5},{8,10},{10,8},{9,1... | collective-permute-start | bytes 393224 | tf_op jit(solution)/shard_map/ppermute | solution.py:19
  62.9 2.2 %copy-start = (bf16[2,512,2048]{2,1,0:T(8,128)(2,1)S(1)}, bf16[2,512,2048]{2,1,0:T(8,128)(2,1)}, u32[]{:S(2)}) copy-start(bf16[2,512,2048]{2,1,0:T(8,128)(2,1)} %param.5) | copy-start | bytes 12582916
  68.8 14.9 %all-to-all-start.2 = ((bf16[4,2,8,16,512]{4,3,1,2,0:T(8,128)(2,1)}), bf16[4,2,8,16,512]{4,3,1,2,0:T(8,128)(2,1)S(1)}, u32[]{:S(2)}, u32[]{:S(2)}) async-start(bf16[4,2,8,16,512]{4,3,1,2,0:T(8,128)(2,1)} %broadcast_in_dim.12), calls=%async_computation.2 | async-start | bytes 2097152 | tf_op jit(solution)/shard_map/all_to_all | solution.py:11
  74.2 22.2 %collective-permute-start.3 = (bf16[2,512,512]{1,2,0:T(8,128)(2,1)S(1)}, bf16[2,512,512]{1,2,0:T(8,128)(2,1)}, u32[]{:S(2)}, u32[]{:S(2)}) collective-permute-start(bf16[2,512,512]{1,2,0:T(8,128)(2,1)S(1)} %fusion.1), channel_id=1, source_target_pairs={{0,12},{4,0},{8,4},{12,8},{1,13},{5,1},{9,5},{13,9},{2,14},{6,2},{... | collective-permute-start | bytes 3145736 | tf_op jit(solution)/shard_map/ppermute | solution.py:50
  76.2 23.3 %collective-permute-start.2 = (bf16[2,512,512]{1,2,0:T(8,128)(2,1)S(1)}, bf16[2,512,512]{1,2,0:T(8,128)(2,1)S(1)}, u32[]{:S(2)}, u32[]{:S(2)}) collective-permute-start(bf16[2,512,512]{1,2,0:T(8,128)(2,1)S(1)} %fusion.1), channel_id=1, source_target_pairs={{0,4},{4,8},{8,12},{12,0},{1,5},{5,9},{9,13},{13,1},{2,6},{6,10},{... | collective-permute-start | bytes 3145736 | tf_op jit(solution)/shard_map/ppermute | solution.py:49
  83.7 19.8 %collective-permute-start.1 = (bf16[4,2,8,16,512]{4,3,1,2,0:T(8,128)(2,1)S(1)}, bf16[4,2,8,16,512]{4,3,1,2,0:T(8,128)(2,1)}, u32[]{:S(2)}, u32[]{:S(2)}) collective-permute-start(bf16[4,2,8,16,512]{4,3,1,2,0:T(8,128)(2,1)S(1)} %all-to-all-done.2), channel_id=1, source_target_pairs={{0,1},{1,0},{2,3},{3,2},{4,5},{5,4},{6,7},{7,6},{8,9},{9,8},{10,11... | collective-permute-start | bytes 3145736 | tf_op jit(solution)/shard_map/ppermute | solution.py:19
  97.6 15.4 %collective-permute-start.5 = (bf16[2,256,512]{1,2,0:T(8,128)(2,1)S(1)}, bf16[2,256,512]{1,2,0:T(8,128)(2,1)S(1)}, u32[]{:S(2)}, u32[]{:S(2)}) collective-permute-start(bf16[2,256,512]{1,2,0:T(8,128)(2,1)S(1)} %slice.19), channel_id=1, source_target_pairs={{0,12},{4,0},{8,4},{12,8},{1,13},{5,1},{9,5},{13,9},{2,14},{6,2},{... | collective-permute-start | bytes 1572872 | tf_op jit(solution)/shard_map/ppermute | solution.py:53
  99.5 12.3 %collective-permute-start.4 = (bf16[2,256,512]{1,2,0:T(8,128)(2,1)S(1)}, bf16[2,256,512]{1,2,0:T(8,128)(2,1)S(1)}, u32[]{:S(2)}, u32[]{:S(2)}) collective-permute-start(bf16[2,256,512]{1,2,0:T(8,128)(2,1)S(1)} %slice.18), channel_id=1, source_target_pairs={{0,4},{4,8},{8,12},{12,0},{1,5},{5,9},{9,13},{13,1},{2,6},{6,10},{... | collective-permute-start | bytes 1572872 | tf_op jit(solution)/shard_map/ppermute | solution.py:52

commit v4 on v3

--- a/solution.py
+++ b/solution.py
@@ -42,27 +42,26 @@
 
         plus, theirs, later = lax.optimization_barrier((plus, theirs, half))
         plus = spread(order(plus, theirs, "zh"), "y", y)
+        left = lax.ppermute(half, "row", shift(row, 1))
+        right = lax.ppermute(half, "row", shift(row, -1))
+        plus, left, right = lax.optimization_barrier((plus, left, right))
         plus = order(plus, partner(plus, "core"), "core")
         plus = plus.reshape(core, y, zh, zl, thin, rows).transpose(3, 1, 2, 0, 4, 5).reshape(n, rows)
 
         me = lax.axis_index("row")
-        left = lax.ppermute(half, "row", shift(row, 1))
-        right = lax.ppermute(half, "row", shift(row, -1))
-        cut = rows // 2
-        top = lax.ppermute(left[:, :cut], "row", shift(row, 1))
-        bottom = lax.ppermute(right[:, cut:], "row", shift(row, -1))
+        far0 = lax.ppermute(left[0], "row", shift(row, 1))
+        far1 = lax.ppermute(right[1], "row", shift(row, -1))
 
-        def part(strip, owner, start):
-            size = strip.shape[1]
-            block = lax.dynamic_slice_in_dim(plus, owner * rows + start, size, axis=0)
-            return jnp.einsum("ki,qkj->qij", block, strip, preferred_element_type=F32)
+        def block(owner):
+            return lax.dynamic_slice_in_dim(plus, owner % row * rows, rows, axis=0)
 
-        pair = part(half, me, 0)
-        pair += part(left, (me + row - 1) % row, 0)
-        pair += part(right, (me + 1) % row, 0)
-        pair += part(top, (me + 2) % row, 0)
-        pair += part(bottom, (me + 2) % row, cut)
-        total = jnp.sum(pair * later.astype(F32), axis=0)
+        def part(owner, *strips):
+            factor = block(owner)
+            return [jnp.einsum("ki,kj->ij", factor, strip, preferred_element_type=F32) for strip in strips]
+
+        parts = [part(me, *half), part(me + row - 1, *left), part(me + 1, *right), part(me + 2, far0, far1)]
+        pair0, pair1 = (sum(piece[index] for piece in parts) for index in (0, 1))
+        total = pair0 * later[0].astype(F32) + pair1 * later[1].astype(F32)
 
         total = lax.all_to_all(total.astype(BF).reshape(y, rows // y, cols), "y", 0, 0)
         total = jnp.sum(total.astype(F32), axis=0)

time: 179 us -> 182 us (1.017)
  blocking collectives: 91.3 us -> 105 us
  waiting for transfers between devices: 34.2 us -> 27.9 us
  starting transfers between devices: 34.7 us -> 32.1 us
    all_to_all x3 -> x4, blocking collectives: 53.9 us -> 68 us  [spread(): lax.all_to_all(jnp.broadcast_to(block[None], (count,) + block.shape), axe...]
    ppermute x1, waiting for transfers between devices: 10.8 us -> 1.18 us  [local(): right = lax.ppermute(half, 'row', shift(row, -1))]
    ppermute x2, waiting for transfers between devices: 3.86 us -> 10.2 us  [the longest x1 5.96 us: local(): far0 = lax.ppermute(left[0], 'row', shift(row, 1))]
    all_to_all x2 -> x1, starting transfers between devices: 12.9 us -> 7.39 us  [spread(): lax.all_to_all(jnp.broadcast_to(block[None], (count,) + block.shape), axe...]
    all_to_all x2 -> x1, waiting for transfers between devices: 19.5 us -> 15.9 us  [spread(): lax.all_to_all(jnp.broadcast_to(block[None], (count,) + block.shape), axe...]
    ppermute x1, starting transfers between devices: 1.91 us -> 4.58 us  [local(): right = lax.ppermute(half, 'row', shift(row, -1))]
    dot_general x5 -> x8, matrix products: 4.2 us -> 3.56 us  [part(): jnp.einsum('ki,kj->ij', factor, strip, preferred_element_type=F32)]
  transfers between devices with their start and end apart: 8 -> 7, of which waited for: 4 -> 5; matrix products, arithmetic and copies ran while one was open for 5% -> 5% of each run, Pallas kernels for 0% -> 0%
where the time goes in v4:
time: 182 us
  blocking collectives  105 us (58%)
  starting transfers between devices  32.1 us (18%)
  waiting for transfers between devices  27.9 us (15%)
  local copies, waits for them, and re-layouts  7.6 us (4%)
  matrix products  5.93 us (3%)
  other arithmetic  2.46 us (1%)
    all_to_all x4, blocking collectives, spread(): lax.all_to_all(jnp.broadcast_to(block[None], (count,) + block.shape), axe...  68 us
    all_to_all x1, blocking collectives, local(): lax.all_to_all(total.astype(BF).reshape(zl, rows // y // zl, cols), 'zl',...  24.5 us
    all_to_all x1, waiting for transfers between devices, spread(): lax.all_to_all(jnp.broadcast_to(block[None], (count,) + block.shape), axe...  15.9 us
    all_to_all x1, blocking collectives, local(): lax.all_to_all(total.astype(BF).reshape(y, rows // y, cols), 'y', 0, 0)  12.8 us
    ppermute x2, starting transfers between devices, partner(): return lax.ppermute(block, axis, shift(2, 1))  10.1 us
    all_to_all x1, starting transfers between devices, spread(): lax.all_to_all(jnp.broadcast_to(block[None], (count,) + block.shape), axe...  7.39 us
    ppermute x1, waiting for transfers between devices, local(): far0 = lax.ppermute(left[0], 'row', shift(row, 1))  5.96 us
    ppermute x1, starting transfers between devices, local(): far1 = lax.ppermute(right[1], 'row', shift(row, -1))  5.6 us
  transfers between devices with their start and end apart: 7, of which 5 were waited for; matrix products, arithmetic and copies ran while one was open for 5% of the time, Pallas kernels for 0%

profile of v4, /device:TPU:8, one launch (start us, length us, event | category | flops | bytes accessed | tf_op | source)
XLA Modules:
  0.0 181.6 jit_solution(2261054279958132453)
XLA Ops:
  0.0 0.7 pad_maximum_fusion.2
  0.8 29.0 %all_to_all.35 = bf16[8,32,512]{2,1,0:T(8,128)(2,1)S(1)} all-to-all(bf16[8,32,512]{2,1,0:T(8,128)(2,1)S(1)} %broadcast_in_dim.10), channel_id=1, replica_groups=mesh['zl'=8,'y'=4,'row'=4,'zh'=2,'core'=2] {'zl'}, dimensions={0} | all-to-all | bytes 524288 | tf_op jit(solution)/shard_map/all_to_all | solution.py:11
  29.8 1.6 broadcast_in_dim.11
  31.4 7.4 %all-to-all-start.1 = ((bf16[16,8,16,512]{3,2,1,0:T(8,128)(2,1)}), bf16[16,8,16,512]{3,2,1,0:T(8,128)(2,1)S(1)}, u32[]{:S(2)}, u32[]{:S(2)}) async-start(bf16[16,8,16,512]{3,2,1,0:T(8,128)(2,1)} %broadcast_in_dim.11), calls=%async_computation.1 | async-start | bytes 4194304 | tf_op jit(solution)/shard_map/all_to_all | solution.py:11
  38.8 8.2 %collective-permute-start = (bf16[8,16,512]{2,1,0:T(8,128)(2,1)S(1)}, bf16[8,16,512]{2,1,0:T(8,128)(2,1)S(1)}, u32[]{:S(2)}, u32[]{:S(2)}) collective-permute-start(bf16[8,16,512]{2,1,0:T(8,128)(2,1)S(1)} %get-tuple-element.11), channel_id=1, source_target_pairs={{0,2},{2,0},{1,3},{3,1},{4,6},{6,4},{5,7},{7,5},{8,10},{10,8},{9,1... | collective-permute-start | bytes 393224 | tf_op jit(solution)/shard_map/ppermute | solution.py:19
  47.0 15.9 %all-to-all-done.1 = bf16[16,8,16,512]{3,2,1,0:T(8,128)(2,1)S(1)} async-done(((bf16[16,8,16,512]{3,2,1,0:T(8,128)(2,1)}), bf16[16,8,16,512]{3,2,1,0:T(8,128)(2,1)S(1)}, u32[]{:S(2)}, u32[]{:S(2)}) %all-to-all-start.1) | async-done | bytes 2097184 | tf_op jit(solution)/shard_map/all_to_all | solution.py:11
  63.2 1.9 %copy-done.2 = bf16[2,512,2048]{2,1,0:T(8,128)(2,1)S(1)} copy-done((bf16[2,512,2048]{2,1,0:T(8,128)(2,1)S(1)}, bf16[2,512,2048]{2,1,0:T(8,128)(2,1)}, u32[]{:S(2)}) %copy-start.2) | copy-done | bytes 4194328
  65.1 2.4 %fusion = bf16[2,512,512]{1,2,0:T(8,128)(2,1)S(1)} fusion(bf16[2048,512,1]{1,0,2:T(8,128)(2,1)S(1)} %bitcast.66, bf16[2,512,2048]{2,1,0:T(8,128)(2,1)S(1)} %copy-done.2), kind=kOutput, calls=%fused_computation.2 | convolution fusion | flops 2148007936 | bytes 7340032 | tf_op jit(solution)/shard_map/qik,kj->qij/dot_general | solution.py:41
  67.5 2.5 %collective-permute-start.1 = (bf16[2,512,512]{1,2,0:T(8,128)(2,1)S(1)}, bf16[2,512,512]{1,2,0:T(8,128)(2,1)S(1)}, u32[]{:S(2)}, u32[]{:S(2)}) collective-permute-start(bf16[2,512,512]{1,2,0:T(8,128)(2,1)S(1)} %fusion), channel_id=1, source_target_pairs={{0,4},{4,8},{8,12},{12,0},{1,5},{5,9},{9,13},{13,1},{2,6},{6,10},{... | collective-permute-start | bytes 3145736 | tf_op jit(solution)/shard_map/ppermute | solution.py:45
  70.0 4.6 %collective-permute-start.2 = (bf16[2,512,512]{1,2,0:T(8,128)(2,1)S(1)}, bf16[2,512,512]{1,2,0:T(8,128)(2,1)S(1)}, u32[]{:S(2)}, u32[]{:S(2)}) collective-permute-start(bf16[2,512,512]{1,2,0:T(8,128)(2,1)S(1)} %fusion), channel_id=1, source_target_pairs={{0,12},{4,0},{8,4},{12,8},{1,13},{5,1},{9,5},{13,9},{2,14},{6,2},{... | collective-permute-start | bytes 3145736 | tf_op jit(solution)/shard_map/ppermute | solution.py:46
  74.8 13.9 %all_to_all.36 = bf16[4,2,8,16,512]{4,3,1,2,0:T(8,128)(2,1)S(1)} all-to-all(bf16[4,2,8,16,512]{4,3,1,2,0:T(8,128)(2,1)S(1)} %broadcast_in_dim.12), channel_id=1, replica_groups=mesh['zl'=8,'y'=4,'row'=4,'zh'=2,'core'=2] {'y'}, dimensions={0} | all-to-all | bytes 2097152 | tf_op jit(solution)/shard_map/all_to_all | solution.py:11
  88.7 0.6 collective-permute-done.1
  89.3 1.2 collective-permute-done.2
  90.5 1.1 copy.46
  91.6 1.9 %collective-permute-start.3 = (bf16[4,2,8,16,512]{4,3,1,0,2:T(8,128)(2,1)}, bf16[4,2,8,16,512]{4,3,1,0,2:T(8,128)(2,1)}, u32[]{:S(2)}, u32[]{:S(2)}) collective-permute-start(bf16[4,2,8,16,512]{4,3,1,0,2:T(8,128)(2,1)} %copy.46), channel_id=1, source_target_pairs={{0,1},{1,0},{2,3},{3,2},{4,5},{5,4},{6,7},{7,6},{8,9},{9,8},{10,11... | collective-permute-start | bytes 3145736 | tf_op jit(solution)/shard_map/ppermute | solution.py:19
  93.6 5.6 %collective-permute-start.5 = (bf16[512,512]{0,1:T(8,128)(2,1)S(1)}, bf16[512,512]{0,1:T(8,128)(2,1)S(1)}, u32[]{:S(2)}, u32[]{:S(2)}) collective-permute-start(bf16[512,512]{0,1:T(8,128)(2,1)S(1)} %slice_bitcast_fusion.4), channel_id=1, source_target_pairs={{0,12},{4,0},{8,4},{12,8},{1,13},{5,1},{9,5},{13,9},{2,14},{6,2},{... | collective-permute-start | bytes 1572872 | tf_op jit(solution)/shard_map/ppermute | solution.py:53
  99.2 1.1 slice_bitcast_fusion.5
  100.3 1.9 %collective-permute-start.4 = (bf16[512,512]{0,1:T(8,128)(2,1)S(1)}, bf16[512,512]{0,1:T(8,128)(2,1)S(1)}, u32[]{:S(2)}, u32[]{:S(2)}) collective-permute-start(bf16[512,512]{0,1:T(8,128)(2,1)S(1)} %slice_bitcast_fusion.5), channel_id=1, source_target_pairs={{0,4},{4,8},{8,12},{12,0},{1,5},{5,9},{9,13},{13,1},{2,6},{6,10},{... | collective-permute-start | bytes 1572872 | tf_op jit(solution)/shard_map/ppermute | solution.py:52
  102.3 1.4 select_bitcast_fusion.1
  103.9 0.4 fusion.6
  104.3 0.4 fusion.7
  105.5 0.4 convolution_add_fusion.5
  106.0 0.4 convolution_add_fusion.1
  106.4 0.4 convolution_add_fusion.4
  106.9 4.2 %collective-permute-done.5 = bf16[512,512]{0,1:T(8,128)(2,1)S(1)} collective-permute-done((bf16[512,512]{0,1:T(8,128)(2,1)S(1)}, bf16[512,512]{0,1:T(8,128)(2,1)S(1)}, u32[]{:S(2)}, u32[]{:S(2)}) %collective-permute-start.5) | collective-permute-done | bytes 524320 | tf_op jit(solution)/shard_map/ppermute | solution.py:53
  111.5 6.0 %collective-permute-done.4 = bf16[512,512]{0,1:T(8,128)(2,1)S(1)} collective-permute-done((bf16[512,512]{0,1:T(8,128)(2,1)S(1)}, bf16[512,512]{0,1:T(8,128)(2,1)S(1)}, u32[]{:S(2)}, u32[]{:S(2)}) %collective-permute-start.4) | collective-permute-done | bytes 524320 | tf_op jit(solution)/shard_map/ppermute | solution.py:52
  117.5 0.5 fusion.5
  118.1 12.8 %all_to_all.37 = bf16[4,128,512]{1,2,0:T(8,128)(2,1)S(1)} all-to-all(bf16[4,128,512]{1,2,0:T(8,128)(2,1)S(1)} %bitcast.67), channel_id=1, replica_groups=mesh['zl'=8,'y'=4,'row'=4,'zh'=2,'core'=2] {'y'}, dimensions={0} | all-to-all | bytes 1048576 | tf_op jit(solution)/shard_map/all_to_all | solution.py:66
  131.1 24.5 %all_to_all.38 = bf16[8,16,512]{2,1,0:T(8,128)(2,1)S(1)} all-to-all(bf16[8,16,512]{2,1,0:T(8,128)(2,1)S(1)} %bitcast.69), channel_id=1, replica_groups=mesh['zl'=8,'y'=4,'row'=4,'zh'=2,'core'=2] {'zl'}, dimensions={0} | all-to-all | bytes 262144 | tf_op jit(solution)/shard_map/all_to_all | solution.py:68
  155.6 14.7 %all_to_all.39 = bf16[8,16,512]{2,1,0:T(8,128)(2,1)S(1)} all-to-all(bf16[8,16,512]{2,1,0:T(8,128)(2,1)S(1)} %broadcast_in_dim.13), channel_id=1, replica_groups=mesh['zl'=8,'y'=4,'row'=4,'zh'=2,'core'=2] {'zl'}, dimensions={0} | all-to-all | bytes 262144 | tf_op jit(solution)/shard_map/all_to_all | solution.py:11
  170.4 10.5 %all_to_all.40 = bf16[4,8,16,512]{3,2,1,0:T(8,128)(2,1)S(1)} all-to-all(bf16[4,8,16,512]{3,2,1,0:T(8,128)(2,1)S(1)} %broadcast_in_dim.14), channel_id=1, replica_groups=mesh['zl'=8,'y'=4,'row'=4,'zh'=2,'core'=2] {'y'}, dimensions={0} | all-to-all | bytes 1048576 | tf_op jit(solution)/shard_map/all_to_all | solution.py:11
  180.8 0.8 copy.77
  (25 shorter events, 2.3 us)
Async XLA Ops:
  31.4 31.5 %all-to-all-start.1 = ((bf16[16,8,16,512]{3,2,1,0:T(8,128)(2,1)}), bf16[16,8,16,512]{3,2,1,0:T(8,128)(2,1)S(1)}, u32[]{:S(2)}, u32[]{:S(2)}) async-start(bf16[16,8,16,512]{3,2,1,0:T(8,128)(2,1)} %broadcast_in_dim.11), calls=%async_computation.1 | async-start | bytes 4194304 | tf_op jit(solution)/shard_map/all_to_all | solution.py:11
  38.8 35.8 %collective-permute-start = (bf16[8,16,512]{2,1,0:T(8,128)(2,1)S(1)}, bf16[8,16,512]{2,1,0:T(8,128)(2,1)S(1)}, u32[]{:S(2)}, u32[]{:S(2)}) collective-permute-start(bf16[8,16,512]{2,1,0:T(8,128)(2,1)S(1)} %get-tuple-element.11), channel_id=1, source_target_pairs={{0,2},{2,0},{1,3},{3,1},{4,6},{6,4},{5,7},{7,5},{8,10},{10,8},{9,1... | collective-permute-start | bytes 393224 | tf_op jit(solution)/shard_map/ppermute | solution.py:19
  62.9 2.2 %copy-start.2 = (bf16[2,512,2048]{2,1,0:T(8,128)(2,1)S(1)}, bf16[2,512,2048]{2,1,0:T(8,128)(2,1)}, u32[]{:S(2)}) copy-start(bf16[2,512,2048]{2,1,0:T(8,128)(2,1)} %param.5) | copy-start | bytes 12582916
  67.5 21.8 %collective-permute-start.1 = (bf16[2,512,512]{1,2,0:T(8,128)(2,1)S(1)}, bf16[2,512,512]{1,2,0:T(8,128)(2,1)S(1)}, u32[]{:S(2)}, u32[]{:S(2)}) collective-permute-start(bf16[2,512,512]{1,2,0:T(8,128)(2,1)S(1)} %fusion), channel_id=1, source_target_pairs={{0,4},{4,8},{8,12},{12,0},{1,5},{5,9},{9,13},{13,1},{2,6},{6,10},{... | collective-permute-start | bytes 3145736 | tf_op jit(solution)/shard_map/ppermute | solution.py:45
  70.0 20.5 %collective-permute-start.2 = (bf16[2,512,512]{1,2,0:T(8,128)(2,1)S(1)}, bf16[2,512,512]{1,2,0:T(8,128)(2,1)S(1)}, u32[]{:S(2)}, u32[]{:S(2)}) collective-permute-start(bf16[2,512,512]{1,2,0:T(8,128)(2,1)S(1)} %fusion), channel_id=1, source_target_pairs={{0,12},{4,0},{8,4},{12,8},{1,13},{5,1},{9,5},{13,9},{2,14},{6,2},{... | collective-permute-start | bytes 3145736 | tf_op jit(solution)/shard_map/ppermute | solution.py:46
  89.3 1.2 copy-start
  91.6 10.6 %collective-permute-start.3 = (bf16[4,2,8,16,512]{4,3,1,0,2:T(8,128)(2,1)}, bf16[4,2,8,16,512]{4,3,1,0,2:T(8,128)(2,1)}, u32[]{:S(2)}, u32[]{:S(2)}) collective-permute-start(bf16[4,2,8,16,512]{4,3,1,0,2:T(8,128)(2,1)} %copy.46), channel_id=1, source_target_pairs={{0,1},{1,0},{2,3},{3,2},{4,5},{5,4},{6,7},{7,6},{8,9},{9,8},{10,11... | collective-permute-start | bytes 3145736 | tf_op jit(solution)/shard_map/ppermute | solution.py:19
  93.6 17.4 %collective-permute-start.5 = (bf16[512,512]{0,1:T(8,128)(2,1)S(1)}, bf16[512,512]{0,1:T(8,128)(2,1)S(1)}, u32[]{:S(2)}, u32[]{:S(2)}) collective-permute-start(bf16[512,512]{0,1:T(8,128)(2,1)S(1)} %slice_bitcast_fusion.4), channel_id=1, source_target_pairs={{0,12},{4,0},{8,4},{12,8},{1,13},{5,1},{9,5},{13,9},{2,14},{6,2},{... | collective-permute-start | bytes 1572872 | tf_op jit(solution)/shard_map/ppermute | solution.py:53
  100.3 17.2 %collective-permute-start.4 = (bf16[512,512]{0,1:T(8,128)(2,1)S(1)}, bf16[512,512]{0,1:T(8,128)(2,1)S(1)}, u32[]{:S(2)}, u32[]{:S(2)}) collective-permute-start(bf16[512,512]{0,1:T(8,128)(2,1)S(1)} %slice_bitcast_fusion.5), channel_id=1, source_target_pairs={{0,4},{4,8},{8,12},{12,0},{1,5},{5,9},{9,13},{13,1},{2,6},{6,10},{... | collective-permute-start | bytes 1572872 | tf_op jit(solution)/shard_map/ppermute | solution.py:52
  103.8 1.2 copy-start.1

commit v5 on v4

--- a/solution.py
+++ b/solution.py
@@ -37,20 +37,25 @@
         minus, plus = slabs[:, :depth], slabs[:, depth:]
         theirs = partner(plus, "zh")
         minus = spread(minus, ("y", "row"), y * row)
+        minus, plus, theirs = lax.optimization_barrier((minus, plus, theirs))
+        plus = order(plus, theirs, "zh")
+        theirs = partner(plus, "core")
         minus = minus.reshape(y, row, zl, depth, cols).transpose(2, 0, 1, 3, 4).reshape(n, cols)
-        half = jnp.einsum("qik,kj->qij", coulomb, minus, preferred_element_type=F32).astype(BF)
+        q0, q1 = (jnp.dot(coulomb[q], minus, preferred_element_type=F32).astype(BF) for q in (0, 1))
 
-        plus, theirs, later = lax.optimization_barrier((plus, theirs, half))
-        plus = spread(order(plus, theirs, "zh"), "y", y)
-        left = lax.ppermute(half, "row", shift(row, 1))
-        right = lax.ppermute(half, "row", shift(row, -1))
-        plus, left, right = lax.optimization_barrier((plus, left, right))
-        plus = order(plus, partner(plus, "core"), "core")
-        plus = plus.reshape(core, y, zh, zl, thin, rows).transpose(3, 1, 2, 0, 4, 5).reshape(n, rows)
+        left0 = lax.ppermute(q0, "row", shift(row, 1))
+        right1 = lax.ppermute(q1, "row", shift(row, -1))
+        left1 = lax.ppermute(q1, "row", shift(row, 1))
+        right0 = lax.ppermute(q0, "row", shift(row, -1))
+        far0 = lax.ppermute(left0, "row", shift(row, 1))
+        far1 = lax.ppermute(right1, "row", shift(row, -1))
+
+        plus, theirs, later0, later1 = lax.optimization_barrier((plus, theirs, q0, q1))
+        plus = spread(order(plus, theirs, "core"), "y", y)
+        plus, left1, right0 = lax.optimization_barrier((plus, left1, right0))
+        plus = plus.reshape(y, core, zh, zl, thin, rows).transpose(3, 0, 2, 1, 4, 5).reshape(n, rows)
 
         me = lax.axis_index("row")
-        far0 = lax.ppermute(left[0], "row", shift(row, 1))
-        far1 = lax.ppermute(right[1], "row", shift(row, -1))
 
         def block(owner):
             return lax.dynamic_slice_in_dim(plus, owner % row * rows, rows, axis=0)
@@ -59,9 +64,9 @@
             factor = block(owner)
             return [jnp.einsum("ki,kj->ij", factor, strip, preferred_element_type=F32) for strip in strips]
 
-        parts = [part(me, *half), part(me + row - 1, *left), part(me + 1, *right), part(me + 2, far0, far1)]
+        parts = [part(me, q0, q1), part(me + row - 1, left0, left1), part(me + 1, right0, right1), part(me + 2, far0, far1)]
         pair0, pair1 = (sum(piece[index] for piece in parts) for index in (0, 1))
-        total = pair0 * later[0].astype(F32) + pair1 * later[1].astype(F32)
+        total = pair0 * later0.astype(F32) + pair1 * later1.astype(F32)
 
         total = lax.all_to_all(total.astype(BF).reshape(y, rows // y, cols), "y", 0, 0)
         total = jnp.sum(total.astype(F32), axis=0)

time: 182 us -> 179 us (0.984)
  blocking collectives: 105 us -> 86.9 us
  starting transfers between devices: 32.1 us -> 42.1 us
  matrix products: 5.93 us -> 12.4 us
  local copies, waits for them, and re-layouts: 7.6 us -> 4.76 us
  waiting for transfers between devices: 27.9 us -> 30.2 us
    all_to_all x1 -> x2, waiting for transfers between devices: 15.9 us -> 1.55 us  [spread(): lax.all_to_all(jnp.broadcast_to(block[None], (count,) + block.shape), axe...]
    ppermute x2, waiting for transfers between devices: 0.01 us -> 14.4 us  [partner(): return lax.ppermute(block, axis, shift(2, 1))]
    all_to_all x4 -> x3, blocking collectives: 68 us -> 54 us  [spread(): lax.all_to_all(jnp.broadcast_to(block[None], (count,) + block.shape), axe...]
    dot_general x8, matrix products: 3.56 us -> 9.8 us  [part(): jnp.einsum('ki,kj->ij', factor, strip, preferred_element_type=F32)]
    all_to_all x1 -> x2, starting transfers between devices: 7.39 us -> 13 us  [spread(): lax.all_to_all(jnp.broadcast_to(block[None], (count,) + block.shape), axe...]
    ppermute x4 -> x6, starting transfers between devices: 14.6 us -> 18.7 us  [the longest x1 4.81 us: local(): right0 = lax.ppermute(q0, 'row', shift(row, -1))]
    all_to_all x1, blocking collectives: 24.5 us -> 21.1 us  [local(): lax.all_to_all(total.astype(BF).reshape(zl, rows // y // zl, cols), 'zl',...]
    unnamed x7 -> x3, local copies, waits for them, and re-layouts: 3.07 us -> 0.8 us
  transfers between devices with their start and end apart: 7 -> 10, of which waited for: 5 -> 5; matrix products, arithmetic and copies ran while one was open for 5% -> 6% of each run, Pallas kernels for 0% -> 0%
where the time goes in v5:
time: 179 us; the launch traced here: 178 us
  blocking collectives  86.9 us (49%)
  starting transfers between devices  42.1 us (24%)
  waiting for transfers between devices  30.2 us (17%)
  matrix products  12.4 us (7%)
  local copies, waits for them, and re-layouts  4.76 us (3%)
    all_to_all x3, blocking collectives, spread(): lax.all_to_all(jnp.broadcast_to(block[None], (count,) + block.shape), axe...  54 us
    all_to_all x1, blocking collectives, local(): lax.all_to_all(total.astype(BF).reshape(zl, rows // y // zl, cols), 'zl',...  21.1 us
    ppermute x2, waiting for transfers between devices, partner(): return lax.ppermute(block, axis, shift(2, 1))  14.4 us
    all_to_all x2, starting transfers between devices, spread(): lax.all_to_all(jnp.broadcast_to(block[None], (count,) + block.shape), axe...  13 us
    all_to_all x1, blocking collectives, local(): lax.all_to_all(total.astype(BF).reshape(y, rows // y, cols), 'y', 0, 0)  11.8 us
    ppermute x2, starting transfers between devices, partner(): return lax.ppermute(block, axis, shift(2, 1))  10.4 us
    dot_general x8, matrix products, part(): jnp.einsum('ki,kj->ij', factor, strip, preferred_element_type=F32)  9.8 us
    ppermute x1, waiting for transfers between devices, local(): left1 = lax.ppermute(q1, 'row', shift(row, 1))  8.87 us
  transfers between devices with their start and end apart: 10, of which 5 were waited for; matrix products, arithmetic and copies ran while one was open for 6% of the time, Pallas kernels for 0%

profile of v5, /device:TPU:8, one launch (start us, length us, event | category | flops | bytes accessed | tf_op | source)
XLA Modules:
  0.0 177.6 jit_solution(3934747001415881341)
XLA Ops:
  0.0 0.7 pad_maximum_fusion.2
  0.8 29.0 %all_to_all.35 = bf16[8,32,512]{2,1,0:T(8,128)(2,1)S(1)} all-to-all(bf16[8,32,512]{2,1,0:T(8,128)(2,1)S(1)} %broadcast_in_dim.10), channel_id=1, replica_groups=mesh['zl'=8,'y'=4,'row'=4,'zh'=2,'core'=2] {'zl'}, dimensions={0} | all-to-all | bytes 524288 | tf_op jit(solution)/shard_map/all_to_all | solution.py:11
  29.8 1.6 broadcast_in_dim.11
  31.4 7.4 %all-to-all-start.1 = ((bf16[16,8,16,512]{3,2,1,0:T(8,128)(2,1)}), bf16[16,8,16,512]{3,2,1,0:T(8,128)(2,1)S(1)}, u32[]{:S(2)}, u32[]{:S(2)}) async-start(bf16[16,8,16,512]{3,2,1,0:T(8,128)(2,1)} %broadcast_in_dim.11), calls=%async_computation.1 | async-start | bytes 4194304 | tf_op jit(solution)/shard_map/all_to_all | solution.py:11
  38.8 8.2 %collective-permute-start = (bf16[8,16,512]{2,1,0:T(8,128)(2,1)S(1)}, bf16[8,16,512]{2,1,0:T(8,128)(2,1)S(1)}, u32[]{:S(2)}, u32[]{:S(2)}) collective-permute-start(bf16[8,16,512]{2,1,0:T(8,128)(2,1)S(1)} %get-tuple-element.15), channel_id=1, source_target_pairs={{0,2},{2,0},{1,3},{3,1},{4,6},{6,4},{5,7},{7,5},{8,10},{10,8},{9,1... | collective-permute-start | bytes 393224 | tf_op jit(solution)/shard_map/ppermute | solution.py:19
  47.0 14.4 %collective-permute-done = bf16[8,16,512]{2,1,0:T(8,128)(2,1)S(1)} collective-permute-done((bf16[8,16,512]{2,1,0:T(8,128)(2,1)S(1)}, bf16[8,16,512]{2,1,0:T(8,128)(2,1)S(1)}, u32[]{:S(2)}, u32[]{:S(2)}) %collective-permute-start) | collective-permute-done | bytes 131104 | tf_op jit(solution)/shard_map/ppermute | solution.py:19
  61.4 1.5 all-to-all-done.1
  63.2 2.2 %collective-permute-start.1 = (bf16[2,8,16,512]{3,2,1,0:T(8,128)(2,1)S(1)}, bf16[2,8,16,512]{3,2,1,0:T(8,128)(2,1)S(1)}, u32[]{:S(2)}, u32[]{:S(2)}) collective-permute-start(bf16[2,8,16,512]{3,2,1,0:T(8,128)(2,1)S(1)} %pad_maximum_fusion.1), channel_id=1, source_target_pairs={{0,1},{1,0},{2,3},{3,2},{4,5},{5,4},{6,7},{7,6},{8,9},{9,8},{10,11... | collective-permute-start | bytes 786440 | tf_op jit(solution)/shard_map/ppermute | solution.py:19
  65.4 1.3 fusion.12
  66.7 1.3 fusion.9
  68.2 1.6 broadcast_in_dim.12
  69.8 5.6 %all-to-all-start.2 = ((bf16[4,2,2,8,16,512]{5,4,1,2,3,0:T(8,128)(2,1)}), bf16[4,2,2,8,16,512]{5,4,1,2,3,0:T(8,128)(2,1)S(1)}, u32[]{:S(2)}, u32[]{:S(2)}) async-start(bf16[4,2,2,8,16,512]{5,4,1,2,3,0:T(8,128)(2,1)} %broadcast_in_dim.12), calls=%async_computation.2 | async-start | bytes 4194304 | tf_op jit(solution)/shard_map/all_to_all | solution.py:11
  75.3 2.2 %collective-permute-start.6 = (bf16[512,512]{0,1:T(8,128)(2,1)S(1)}, bf16[512,512]{0,1:T(8,128)(2,1)}, u32[]{:S(2)}, u32[]{:S(2)}) collective-permute-start(bf16[512,512]{0,1:T(8,128)(2,1)S(1)} %bitcast.59), channel_id=1, source_target_pairs={{0,12},{4,0},{8,4},{12,8},{1,13},{5,1},{9,5},{13,9},{2,14},{6,2},{... | collective-permute-start | bytes 1572872 | tf_op jit(solution)/shard_map/ppermute | solution.py:47
  77.6 3.6 %collective-permute-start.4 = (bf16[512,512]{0,1:T(8,128)(2,1)S(1)}, bf16[512,512]{0,1:T(8,128)(2,1)}, u32[]{:S(2)}, u32[]{:S(2)}) collective-permute-start(bf16[512,512]{0,1:T(8,128)(2,1)S(1)} %bitcast.54), channel_id=1, source_target_pairs={{0,4},{4,8},{8,12},{12,0},{1,5},{5,9},{9,13},{13,1},{2,6},{6,10},{... | collective-permute-start | bytes 1572872 | tf_op jit(solution)/shard_map/ppermute | solution.py:46
  81.2 2.2 %collective-permute-start.2 = (bf16[512,512]{0,1:T(8,128)(2,1)S(1)}, bf16[512,512]{0,1:T(8,128)(2,1)}, u32[]{:S(2)}, u32[]{:S(2)}) collective-permute-start(bf16[512,512]{0,1:T(8,128)(2,1)S(1)} %bitcast.60), channel_id=1, source_target_pairs={{0,4},{4,8},{8,12},{12,0},{1,5},{5,9},{9,13},{13,1},{2,6},{6,10},{... | collective-permute-start | bytes 1572872 | tf_op jit(solution)/shard_map/ppermute | solution.py:48
  83.4 4.8 %collective-permute-start.3 = (bf16[512,512]{0,1:T(8,128)(2,1)S(1)}, bf16[512,512]{0,1:T(8,128)(2,1)}, u32[]{:S(2)}, u32[]{:S(2)}) collective-permute-start(bf16[512,512]{0,1:T(8,128)(2,1)S(1)} %bitcast.55), channel_id=1, source_target_pairs={{0,12},{4,0},{8,4},{12,8},{1,13},{5,1},{9,5},{13,9},{2,14},{6,2},{... | collective-permute-start | bytes 1572872 | tf_op jit(solution)/shard_map/ppermute | solution.py:49
  88.3 3.8 %collective-permute-done.6 = bf16[512,512]{0,1:T(8,128)(2,1)} collective-permute-done((bf16[512,512]{0,1:T(8,128)(2,1)S(1)}, bf16[512,512]{0,1:T(8,128)(2,1)}, u32[]{:S(2)}, u32[]{:S(2)}) %collective-permute-start.6) | collective-permute-done | bytes 524320 | tf_op jit(solution)/shard_map/ppermute | solution.py:47
  92.1 3.5 %collective-permute-start.7 = (bf16[512,512]{0,1:T(8,128)(2,1)}, bf16[512,512]{0,1:T(8,128)(2,1)}, u32[]{:S(2)}, u32[]{:S(2)}) collective-permute-start(bf16[512,512]{0,1:T(8,128)(2,1)} %collective-permute-done.6), channel_id=1, source_target_pairs={{0,12},{4,0},{8,4},{12,8},{1,13},{5,1},{9,5},{13,9},{2,14},{6,2},{... | collective-permute-start | bytes 1572872 | tf_op jit(solution)/shard_map/ppermute | solution.py:51
  95.6 2.4 %collective-permute-start.5 = (bf16[512,512]{0,1:T(8,128)(2,1)}, bf16[512,512]{0,1:T(8,128)(2,1)}, u32[]{:S(2)}, u32[]{:S(2)}) collective-permute-start(bf16[512,512]{0,1:T(8,128)(2,1)} %collective-permute-done.4), channel_id=1, source_target_pairs={{0,4},{4,8},{8,12},{12,0},{1,5},{5,9},{9,13},{13,1},{2,6},{6,10},{... | collective-permute-start | bytes 1572872 | tf_op jit(solution)/shard_map/ppermute | solution.py:50
  98.0 8.9 %collective-permute-done.2 = bf16[512,512]{0,1:T(8,128)(2,1)} collective-permute-done((bf16[512,512]{0,1:T(8,128)(2,1)S(1)}, bf16[512,512]{0,1:T(8,128)(2,1)}, u32[]{:S(2)}, u32[]{:S(2)}) %collective-permute-start.2) | collective-permute-done | bytes 524320 | tf_op jit(solution)/shard_map/ppermute | solution.py:48
  108.0 1.5 convolution_add_fusion.2
  109.5 1.5 convolution_add_fusion.5
  111.0 1.5 convolution_add_fusion.4
  112.4 1.5 convolution_add_fusion.1
  113.9 1.5 fusion.6
  115.4 1.5 collective-permute-done.5
  117.0 1.5 fusion.16
  118.6 11.8 %all_to_all.36 = bf16[4,128,512]{1,2,0:T(8,128)(2,1)S(1)} all-to-all(bf16[4,128,512]{1,2,0:T(8,128)(2,1)S(1)} %bitcast.62), channel_id=1, replica_groups=mesh['zl'=8,'y'=4,'row'=4,'zh'=2,'core'=2] {'y'}, dimensions={0} | all-to-all | bytes 1048576 | tf_op jit(solution)/shard_map/all_to_all | solution.py:71
  130.6 21.1 %all_to_all.37 = bf16[8,16,512]{2,1,0:T(8,128)(2,1)S(1)} all-to-all(bf16[8,16,512]{2,1,0:T(8,128)(2,1)S(1)} %bitcast.64), channel_id=1, replica_groups=mesh['zl'=8,'y'=4,'row'=4,'zh'=2,'core'=2] {'zl'}, dimensions={0} | all-to-all | bytes 262144 | tf_op jit(solution)/shard_map/all_to_all | solution.py:73
  151.8 14.5 %all_to_all.38 = bf16[8,16,512]{2,1,0:T(8,128)(2,1)S(1)} all-to-all(bf16[8,16,512]{2,1,0:T(8,128)(2,1)S(1)} %broadcast_in_dim.13), channel_id=1, replica_groups=mesh['zl'=8,'y'=4,'row'=4,'zh'=2,'core'=2] {'zl'}, dimensions={0} | all-to-all | bytes 262144 | tf_op jit(solution)/shard_map/all_to_all | solution.py:11
  166.3 10.5 %all_to_all.39 = bf16[4,8,16,512]{3,2,1,0:T(8,128)(2,1)S(1)} all-to-all(bf16[4,8,16,512]{3,2,1,0:T(8,128)(2,1)S(1)} %broadcast_in_dim.14), channel_id=1, replica_groups=mesh['zl'=8,'y'=4,'row'=4,'zh'=2,'core'=2] {'y'}, dimensions={0} | all-to-all | bytes 1048576 | tf_op jit(solution)/shard_map/all_to_all | solution.py:11
  176.8 0.8 copy.62
  (25 shorter events, 2.0 us)
Async XLA Ops:
  31.4 31.5 %all-to-all-start.1 = ((bf16[16,8,16,512]{3,2,1,0:T(8,128)(2,1)}), bf16[16,8,16,512]{3,2,1,0:T(8,128)(2,1)S(1)}, u32[]{:S(2)}, u32[]{:S(2)}) async-start(bf16[16,8,16,512]{3,2,1,0:T(8,128)(2,1)} %broadcast_in_dim.11), calls=%async_computation.1 | async-start | bytes 4194304 | tf_op jit(solution)/shard_map/all_to_all | solution.py:11
  38.8 22.6 %collective-permute-start = (bf16[8,16,512]{2,1,0:T(8,128)(2,1)S(1)}, bf16[8,16,512]{2,1,0:T(8,128)(2,1)S(1)}, u32[]{:S(2)}, u32[]{:S(2)}) collective-permute-start(bf16[8,16,512]{2,1,0:T(8,128)(2,1)S(1)} %get-tuple-element.15), channel_id=1, source_target_pairs={{0,2},{2,0},{1,3},{3,1},{4,6},{6,4},{5,7},{7,5},{8,10},{10,8},{9,1... | collective-permute-start | bytes 393224 | tf_op jit(solution)/shard_map/ppermute | solution.py:19
  62.9 2.5 %copy-start = (bf16[2,512,2048]{2,1,0:T(8,128)(2,1)S(1)}, bf16[2,512,2048]{2,1,0:T(8,128)(2,1)}, u32[]{:S(2)}) copy-start(bf16[2,512,2048]{2,1,0:T(8,128)(2,1)} %param.5) | copy-start | bytes 12582916
  63.2 4.8 %collective-permute-start.1 = (bf16[2,8,16,512]{3,2,1,0:T(8,128)(2,1)S(1)}, bf16[2,8,16,512]{3,2,1,0:T(8,128)(2,1)S(1)}, u32[]{:S(2)}, u32[]{:S(2)}) collective-permute-start(bf16[2,8,16,512]{3,2,1,0:T(8,128)(2,1)S(1)} %pad_maximum_fusion.1), channel_id=1, source_target_pairs={{0,1},{1,0},{2,3},{3,2},{4,5},{5,4},{6,7},{7,6},{8,9},{9,8},{10,11... | collective-permute-start | bytes 786440 | tf_op jit(solution)/shard_map/ppermute | solution.py:19
  69.8 37.1 %all-to-all-start.2 = ((bf16[4,2,2,8,16,512]{5,4,1,2,3,0:T(8,128)(2,1)}), bf16[4,2,2,8,16,512]{5,4,1,2,3,0:T(8,128)(2,1)S(1)}, u32[]{:S(2)}, u32[]{:S(2)}) async-start(bf16[4,2,2,8,16,512]{5,4,1,2,3,0:T(8,128)(2,1)} %broadcast_in_dim.12), calls=%async_computation.2 | async-start | bytes 4194304 | tf_op jit(solution)/shard_map/all_to_all | solution.py:11
  75.3 16.7 %collective-permute-start.6 = (bf16[512,512]{0,1:T(8,128)(2,1)S(1)}, bf16[512,512]{0,1:T(8,128)(2,1)}, u32[]{:S(2)}, u32[]{:S(2)}) collective-permute-start(bf16[512,512]{0,1:T(8,128)(2,1)S(1)} %bitcast.59), channel_id=1, source_target_pairs={{0,12},{4,0},{8,4},{12,8},{1,13},{5,1},{9,5},{13,9},{2,14},{6,2},{... | collective-permute-start | bytes 1572872 | tf_op jit(solution)/shard_map/ppermute | solution.py:47
  77.6 18.0 %collective-permute-start.4 = (bf16[512,512]{0,1:T(8,128)(2,1)S(1)}, bf16[512,512]{0,1:T(8,128)(2,1)}, u32[]{:S(2)}, u32[]{:S(2)}) collective-permute-start(bf16[512,512]{0,1:T(8,128)(2,1)S(1)} %bitcast.54), channel_id=1, source_target_pairs={{0,4},{4,8},{8,12},{12,0},{1,5},{5,9},{9,13},{13,1},{2,6},{6,10},{... | collective-permute-start | bytes 1572872 | tf_op jit(solution)/shard_map/ppermute | solution.py:46
  81.2 25.7 %collective-permute-start.2 = (bf16[512,512]{0,1:T(8,128)(2,1)S(1)}, bf16[512,512]{0,1:T(8,128)(2,1)}, u32[]{:S(2)}, u32[]{:S(2)}) collective-permute-start(bf16[512,512]{0,1:T(8,128)(2,1)S(1)} %bitcast.60), channel_id=1, source_target_pairs={{0,4},{4,8},{8,12},{12,0},{1,5},{5,9},{9,13},{13,1},{2,6},{6,10},{... | collective-permute-start | bytes 1572872 | tf_op jit(solution)/shard_map/ppermute | solution.py:48
  83.4 23.4 %collective-permute-start.3 = (bf16[512,512]{0,1:T(8,128)(2,1)S(1)}, bf16[512,512]{0,1:T(8,128)(2,1)}, u32[]{:S(2)}, u32[]{:S(2)}) collective-permute-start(bf16[512,512]{0,1:T(8,128)(2,1)S(1)} %bitcast.55), channel_id=1, source_target_pairs={{0,12},{4,0},{8,4},{12,8},{1,13},{5,1},{9,5},{13,9},{2,14},{6,2},{... | collective-permute-start | bytes 1572872 | tf_op jit(solution)/shard_map/ppermute | solution.py:49
  92.1 21.8 %collective-permute-start.7 = (bf16[512,512]{0,1:T(8,128)(2,1)}, bf16[512,512]{0,1:T(8,128)(2,1)}, u32[]{:S(2)}, u32[]{:S(2)}) collective-permute-start(bf16[512,512]{0,1:T(8,128)(2,1)} %collective-permute-done.6), channel_id=1, source_target_pairs={{0,12},{4,0},{8,4},{12,8},{1,13},{5,1},{9,5},{13,9},{2,14},{6,2},{... | collective-permute-start | bytes 1572872 | tf_op jit(solution)/shard_map/ppermute | solution.py:51
  95.6 21.4 %collective-permute-start.5 = (bf16[512,512]{0,1:T(8,128)(2,1)}, bf16[512,512]{0,1:T(8,128)(2,1)}, u32[]{:S(2)}, u32[]{:S(2)}) collective-permute-start(bf16[512,512]{0,1:T(8,128)(2,1)} %collective-permute-done.4), channel_id=1, source_target_pairs={{0,4},{4,8},{8,12},{12,0},{1,5},{5,9},{9,13},{13,1},{2,6},{6,10},{... | collective-permute-start | bytes 1572872 | tf_op jit(solution)/shard_map/ppermute | solution.py:50

commit v6 on v5

--- a/solution.py
+++ b/solution.py
@@ -26,14 +26,17 @@
 
 def solution(mesh):
     aux, row, col = (mesh.shape[name] for name in ("aux", "row", "col"))
-    zl, y, zh, core = aux // 4, 4, col // 2, 2
-    fine = Mesh(mesh.devices.reshape(zl, y, row, zh, core), ("zl", "y", "row", "zh", "core"))
+    z2, z1, y, zh, core = 2, aux // 8, 4, col // 2, 2
+    zl = z2 * z1
+    names = ("z2", "z1", "y", "row", "zh", "core")
+    fine = Mesh(mesh.devices.reshape(z2, z1, y, row, zh, core), names)
+    line = ("z2", "z1")
 
     def local(g_plus, g_minus, coulomb):
         count, rows, n = coulomb.shape
         depth, cols = g_minus.shape
         thin = g_plus.shape[1]
-        slabs = spread(jnp.concatenate([g_minus, g_plus.T]), "zl", zl)
+        slabs = spread(jnp.concatenate([g_minus, g_plus.T]), line, zl)
         minus, plus = slabs[:, :depth], slabs[:, depth:]
         theirs = partner(plus, "zh")
         minus = spread(minus, ("y", "row"), y * row)
@@ -68,18 +71,16 @@
         pair0, pair1 = (sum(piece[index] for piece in parts) for index in (0, 1))
         total = pair0 * later0.astype(F32) + pair1 * later1.astype(F32)
 
-        total = lax.all_to_all(total.astype(BF).reshape(y, rows // y, cols), "y", 0, 0)
+        parts = y * z1
+        total = lax.all_to_all(total.astype(BF).reshape(parts, rows // parts, cols), ("y", "z1"), 0, 0)
         total = jnp.sum(total.astype(F32), axis=0)
-        total = lax.all_to_all(total.astype(BF).reshape(zl, rows // y // zl, cols), "zl", 0, 0)
-        total = -jnp.sum(total.astype(F32), axis=0)
-        whole = spread(total.astype(BF), "zl", zl)
-        whole = spread(whole, "y", y)
-        return whole.reshape(rows, cols)
+        total = -(total + partner(total, "z2"))
+        return spread(total.astype(BF), ("y", "z1"), parts).reshape(rows, cols)
 
     in_specs = (
-        P("row", ("zl", "y", "zh", "core")),
-        P(("zl", "y", "row"), ("zh", "core")),
-        P(("zl", "y"), "row", None),
+        P("row", ("z2", "z1", "y", "zh", "core")),
+        P(("z2", "z1", "y", "row"), ("zh", "core")),
+        P(("z2", "z1", "y"), "row", None),
     )
     out_specs = P("row", ("zh", "core"))
     return jax.shard_map(local, mesh=fine, in_specs=in_specs, out_specs=out_specs, check_vma=False)

time: 179 us -> 175 us (0.978)
  the two profiles are of different devices: /device:TPU:8 before, /device:TPU:1 now
where the time goes in v6:
time: 175 us; the launch traced here: 174 us
  blocking collectives  66.6 us (38%)
  starting transfers between devices  52.9 us (30%)
  waiting for transfers between devices  36.3 us (21%)
  matrix products  12.4 us (7%)
  local copies, waits for them, and re-layouts  4.76 us (3%)
    all_to_all x2, blocking collectives, spread(): lax.all_to_all(jnp.broadcast_to(block[None], (count,) + block.shape), axe...  44.7 us
    ppermute x3, starting transfers between devices, partner(): return lax.ppermute(block, axis, shift(2, 1))  25.5 us
    all_to_all x1, blocking collectives, local(): lax.all_to_all(total.astype(BF).reshape(parts, rows // parts, cols), ('y'...  22 us
    ppermute x3, waiting for transfers between devices, partner(): return lax.ppermute(block, axis, shift(2, 1))  11.7 us
    all_to_all x2, starting transfers between devices, spread(): lax.all_to_all(jnp.broadcast_to(block[None], (count,) + block.shape), axe...  10.4 us
    dot_general x8, matrix products, part(): jnp.einsum('ki,kj->ij', factor, strip, preferred_element_type=F32)  9.8 us
    all_to_all x2, waiting for transfers between devices, spread(): lax.all_to_all(jnp.broadcast_to(block[None], (count,) + block.shape), axe...  9.46 us
    ppermute x1, waiting for transfers between devices, local(): left1 = lax.ppermute(q1, 'row', shift(row, 1))  8.76 us
  transfers between devices with their start and end apart: 11, of which 7 were waited for; matrix products, arithmetic and copies ran while one was open for 6% of the time, Pallas kernels for 0%

profile of v6, /device:TPU:1, one launch (start us, length us, event | category | flops | bytes accessed | tf_op | source)
XLA Modules:
  0.0 174.3 jit_solution(17607182991441683537)
XLA Ops:
  0.8 25.1 %all_to_all.25 = bf16[8,32,512]{2,1,0:T(8,128)(2,1)S(1)} all-to-all(bf16[8,32,512]{2,1,0:T(8,128)(2,1)S(1)} %broadcast_in_dim.8), channel_id=1, replica_groups=mesh['z2'=2,'z1'=4,'y'=4,'row'=4,'zh'=2,'core'=2] {'z2','z1'}, dimensions={0} | all-to-all | bytes 524288 | tf_op jit(solution)/shard_map/all_to_all | solution.py:11
  25.9 1.6 broadcast_in_dim.9
  27.5 6.8 %all-to-all-start.1 = ((bf16[16,8,16,512]{3,2,1,0:T(8,128)(2,1)}), bf16[16,8,16,512]{3,2,1,0:T(8,128)(2,1)S(1)}, u32[]{:S(2)}, u32[]{:S(2)}) async-start(bf16[16,8,16,512]{3,2,1,0:T(8,128)(2,1)} %broadcast_in_dim.9), calls=%async_computation.1 | async-start | bytes 4194304 | tf_op jit(solution)/shard_map/all_to_all | solution.py:11
  34.2 7.9 %collective-permute-start = (bf16[8,16,512]{2,1,0:T(8,128)(2,1)S(1)}, bf16[8,16,512]{2,1,0:T(8,128)(2,1)S(1)}, u32[]{:S(2)}, u32[]{:S(2)}) collective-permute-start(bf16[8,16,512]{2,1,0:T(8,128)(2,1)S(1)} %get-tuple-element.15), channel_id=1, source_target_pairs={{0,2},{2,0},{1,3},{3,1},{4,6},{6,4},{5,7},{7,5},{8,10},{10,8},{9,1... | collective-permute-start | bytes 393224 | tf_op jit(solution)/shard_map/ppermute | solution.py:19
  42.2 6.7 %collective-permute-done = bf16[8,16,512]{2,1,0:T(8,128)(2,1)S(1)} collective-permute-done((bf16[8,16,512]{2,1,0:T(8,128)(2,1)S(1)}, bf16[8,16,512]{2,1,0:T(8,128)(2,1)S(1)}, u32[]{:S(2)}, u32[]{:S(2)}) %collective-permute-start) | collective-permute-done | bytes 131104 | tf_op jit(solution)/shard_map/ppermute | solution.py:19
  48.8 9.5 %all-to-all-done.1 = bf16[16,8,16,512]{3,2,1,0:T(8,128)(2,1)S(1)} async-done(((bf16[16,8,16,512]{3,2,1,0:T(8,128)(2,1)}), bf16[16,8,16,512]{3,2,1,0:T(8,128)(2,1)S(1)}, u32[]{:S(2)}, u32[]{:S(2)}) %all-to-all-start.1) | async-done | bytes 2097184 | tf_op jit(solution)/shard_map/all_to_all | solution.py:11
  58.6 9.8 %collective-permute-start.1 = (bf16[2,8,16,512]{3,2,1,0:T(8,128)(2,1)S(1)}, bf16[2,8,16,512]{3,2,1,0:T(8,128)(2,1)S(1)}, u32[]{:S(2)}, u32[]{:S(2)}) collective-permute-start(bf16[2,8,16,512]{3,2,1,0:T(8,128)(2,1)S(1)} %pad_maximum_fusion.1), channel_id=1, source_target_pairs={{0,1},{1,0},{2,3},{3,2},{4,5},{5,4},{6,7},{7,6},{8,9},{9,8},{10,11... | collective-permute-start | bytes 786440 | tf_op jit(solution)/shard_map/ppermute | solution.py:19
  68.4 1.3 fusion.12
  69.7 1.3 fusion.9
  71.2 1.6 broadcast_in_dim.10
  72.8 3.6 %all-to-all-start.2 = ((bf16[4,2,2,8,16,512]{5,4,1,2,3,0:T(8,128)(2,1)}), bf16[4,2,2,8,16,512]{5,4,1,2,3,0:T(8,128)(2,1)S(1)}, u32[]{:S(2)}, u32[]{:S(2)}) async-start(bf16[4,2,2,8,16,512]{5,4,1,2,3,0:T(8,128)(2,1)} %broadcast_in_dim.10), calls=%async_computation.2 | async-start | bytes 4194304 | tf_op jit(solution)/shard_map/all_to_all | solution.py:11
  76.4 1.9 %collective-permute-start.6 = (bf16[512,512]{0,1:T(8,128)(2,1)S(1)}, bf16[512,512]{0,1:T(8,128)(2,1)}, u32[]{:S(2)}, u32[]{:S(2)}) collective-permute-start(bf16[512,512]{0,1:T(8,128)(2,1)S(1)} %bitcast.54), channel_id=1, source_target_pairs={{0,12},{4,0},{8,4},{12,8},{1,13},{5,1},{9,5},{13,9},{2,14},{6,2},{... | collective-permute-start | bytes 1572872 | tf_op jit(solution)/shard_map/ppermute | solution.py:50
  78.4 3.4 %collective-permute-start.4 = (bf16[512,512]{0,1:T(8,128)(2,1)S(1)}, bf16[512,512]{0,1:T(8,128)(2,1)}, u32[]{:S(2)}, u32[]{:S(2)}) collective-permute-start(bf16[512,512]{0,1:T(8,128)(2,1)S(1)} %bitcast.49), channel_id=1, source_target_pairs={{0,4},{4,8},{8,12},{12,0},{1,5},{5,9},{9,13},{13,1},{2,6},{6,10},{... | collective-permute-start | bytes 1572872 | tf_op jit(solution)/shard_map/ppermute | solution.py:49
  81.7 2.0 %collective-permute-start.2 = (bf16[512,512]{0,1:T(8,128)(2,1)S(1)}, bf16[512,512]{0,1:T(8,128)(2,1)}, u32[]{:S(2)}, u32[]{:S(2)}) collective-permute-start(bf16[512,512]{0,1:T(8,128)(2,1)S(1)} %bitcast.55), channel_id=1, source_target_pairs={{0,4},{4,8},{8,12},{12,0},{1,5},{5,9},{9,13},{13,1},{2,6},{6,10},{... | collective-permute-start | bytes 1572872 | tf_op jit(solution)/shard_map/ppermute | solution.py:51
  83.7 4.5 %collective-permute-start.3 = (bf16[512,512]{0,1:T(8,128)(2,1)S(1)}, bf16[512,512]{0,1:T(8,128)(2,1)}, u32[]{:S(2)}, u32[]{:S(2)}) collective-permute-start(bf16[512,512]{0,1:T(8,128)(2,1)S(1)} %bitcast.50), channel_id=1, source_target_pairs={{0,12},{4,0},{8,4},{12,8},{1,13},{5,1},{9,5},{13,9},{2,14},{6,2},{... | collective-permute-start | bytes 1572872 | tf_op jit(solution)/shard_map/ppermute | solution.py:52
  88.3 3.7 %collective-permute-done.6 = bf16[512,512]{0,1:T(8,128)(2,1)} collective-permute-done((bf16[512,512]{0,1:T(8,128)(2,1)S(1)}, bf16[512,512]{0,1:T(8,128)(2,1)}, u32[]{:S(2)}, u32[]{:S(2)}) %collective-permute-start.6) | collective-permute-done | bytes 524320 | tf_op jit(solution)/shard_map/ppermute | solution.py:50
  92.0 3.1 %collective-permute-start.7 = (bf16[512,512]{0,1:T(8,128)(2,1)}, bf16[512,512]{0,1:T(8,128)(2,1)}, u32[]{:S(2)}, u32[]{:S(2)}) collective-permute-start(bf16[512,512]{0,1:T(8,128)(2,1)} %collective-permute-done.6), channel_id=1, source_target_pairs={{0,12},{4,0},{8,4},{12,8},{1,13},{5,1},{9,5},{13,9},{2,14},{6,2},{... | collective-permute-start | bytes 1572872 | tf_op jit(solution)/shard_map/ppermute | solution.py:54
  95.1 2.2 %collective-permute-start.5 = (bf16[512,512]{0,1:T(8,128)(2,1)}, bf16[512,512]{0,1:T(8,128)(2,1)}, u32[]{:S(2)}, u32[]{:S(2)}) collective-permute-start(bf16[512,512]{0,1:T(8,128)(2,1)} %collective-permute-done.4), channel_id=1, source_target_pairs={{0,4},{4,8},{8,12},{12,0},{1,5},{5,9},{9,13},{13,1},{2,6},{6,10},{... | collective-permute-start | bytes 1572872 | tf_op jit(solution)/shard_map/ppermute | solution.py:53
  97.3 8.8 %collective-permute-done.2 = bf16[512,512]{0,1:T(8,128)(2,1)} collective-permute-done((bf16[512,512]{0,1:T(8,128)(2,1)S(1)}, bf16[512,512]{0,1:T(8,128)(2,1)}, u32[]{:S(2)}, u32[]{:S(2)}) %collective-permute-start.2) | collective-permute-done | bytes 524320 | tf_op jit(solution)/shard_map/ppermute | solution.py:51
  107.2 1.5 convolution_add_fusion.2
  108.7 1.5 convolution_add_fusion.5
  110.2 1.5 convolution_add_fusion.4
  111.6 1.5 convolution_add_fusion.1
  113.1 1.3 collective-permute-done.7
  114.5 1.5 fusion.6
  115.9 1.3 collective-permute-done.5
  117.3 1.5 fusion.15
  119.0 22.0 %all_to_all.26 = bf16[16,32,512]{2,1,0:T(8,128)(2,1)S(1)} all-to-all(bf16[16,32,512]{2,1,0:T(8,128)(2,1)S(1)} %bitcast.57), channel_id=1, replica_groups=mesh['z2'=2,'z1'=4,'y'=4,'row'=4,'zh'=2,'core'=2] {'y','z1'}, dimensions={0} | all-to-all | bytes 1048576 | tf_op jit(solution)/shard_map/all_to_all | solution.py:75
  141.1 7.7 %collective-permute-start.8 = (f32[32,512]{1,0:T(8,128)S(1)}, f32[32,512]{1,0:T(8,128)S(1)}, u32[]{:S(2)}, u32[]{:S(2)}) collective-permute-start(f32[32,512]{1,0:T(8,128)S(1)} %convert_reduce_fusion), channel_id=1, source_target_pairs={{0,256},{256,0},{1,257},{257,1},{2,258},{258,2},{3,259},{259,3},{4... | collective-permute-start | bytes 196616 | tf_op jit(solution)/shard_map/ppermute | solution.py:19
  148.8 5.1 %collective-permute-done.8 = f32[32,512]{1,0:T(8,128)S(1)} collective-permute-done((f32[32,512]{1,0:T(8,128)S(1)}, f32[32,512]{1,0:T(8,128)S(1)}, u32[]{:S(2)}, u32[]{:S(2)}) %collective-permute-start.8) | collective-permute-done | bytes 65568 | tf_op jit(solution)/shard_map/ppermute | solution.py:19
  153.9 19.6 %all_to_all.27 = bf16[16,32,512]{2,1,0:T(8,128)(2,1)S(1)} all-to-all(bf16[16,32,512]{2,1,0:T(8,128)(2,1)S(1)} %broadcast_in_dim.11), channel_id=1, replica_groups=mesh['z2'=2,'z1'=4,'y'=4,'row'=4,'zh'=2,'core'=2] {'y','z1'}, dimensions={0} | all-to-all | bytes 1048576 | tf_op jit(solution)/shard_map/all_to_all | solution.py:11
  173.5 0.8 copy.44
  (22 shorter events, 2.6 us)
Async XLA Ops:
  27.5 30.8 %all-to-all-start.1 = ((bf16[16,8,16,512]{3,2,1,0:T(8,128)(2,1)}), bf16[16,8,16,512]{3,2,1,0:T(8,128)(2,1)S(1)}, u32[]{:S(2)}, u32[]{:S(2)}) async-start(bf16[16,8,16,512]{3,2,1,0:T(8,128)(2,1)} %broadcast_in_dim.9), calls=%async_computation.1 | async-start | bytes 4194304 | tf_op jit(solution)/shard_map/all_to_all | solution.py:11
  34.2 14.6 %collective-permute-start = (bf16[8,16,512]{2,1,0:T(8,128)(2,1)S(1)}, bf16[8,16,512]{2,1,0:T(8,128)(2,1)S(1)}, u32[]{:S(2)}, u32[]{:S(2)}) collective-permute-start(bf16[8,16,512]{2,1,0:T(8,128)(2,1)S(1)} %get-tuple-element.15), channel_id=1, source_target_pairs={{0,2},{2,0},{1,3},{3,1},{4,6},{6,4},{5,7},{7,5},{8,10},{10,8},{9,1... | collective-permute-start | bytes 393224 | tf_op jit(solution)/shard_map/ppermute | solution.py:19
  58.3 10.1 %copy-start = (bf16[2,512,2048]{2,1,0:T(8,128)(2,1)S(1)}, bf16[2,512,2048]{2,1,0:T(8,128)(2,1)}, u32[]{:S(2)}) copy-start(bf16[2,512,2048]{2,1,0:T(8,128)(2,1)} %param.5) | copy-start | bytes 12582916
  58.6 12.5 %collective-permute-start.1 = (bf16[2,8,16,512]{3,2,1,0:T(8,128)(2,1)S(1)}, bf16[2,8,16,512]{3,2,1,0:T(8,128)(2,1)S(1)}, u32[]{:S(2)}, u32[]{:S(2)}) collective-permute-start(bf16[2,8,16,512]{3,2,1,0:T(8,128)(2,1)S(1)} %pad_maximum_fusion.1), channel_id=1, source_target_pairs={{0,1},{1,0},{2,3},{3,2},{4,5},{5,4},{6,7},{7,6},{8,9},{9,8},{10,11... | collective-permute-start | bytes 786440 | tf_op jit(solution)/shard_map/ppermute | solution.py:19
  72.8 33.2 %all-to-all-start.2 = ((bf16[4,2,2,8,16,512]{5,4,1,2,3,0:T(8,128)(2,1)}), bf16[4,2,2,8,16,512]{5,4,1,2,3,0:T(8,128)(2,1)S(1)}, u32[]{:S(2)}, u32[]{:S(2)}) async-start(bf16[4,2,2,8,16,512]{5,4,1,2,3,0:T(8,128)(2,1)} %broadcast_in_dim.10), calls=%async_computation.2 | async-start | bytes 4194304 | tf_op jit(solution)/shard_map/all_to_all | solution.py:11
  76.4 15.5 %collective-permute-start.6 = (bf16[512,512]{0,1:T(8,128)(2,1)S(1)}, bf16[512,512]{0,1:T(8,128)(2,1)}, u32[]{:S(2)}, u32[]{:S(2)}) collective-permute-start(bf16[512,512]{0,1:T(8,128)(2,1)S(1)} %bitcast.54), channel_id=1, source_target_pairs={{0,12},{4,0},{8,4},{12,8},{1,13},{5,1},{9,5},{13,9},{2,14},{6,2},{... | collective-permute-start | bytes 1572872 | tf_op jit(solution)/shard_map/ppermute | solution.py:50
  78.4 16.8 %collective-permute-start.4 = (bf16[512,512]{0,1:T(8,128)(2,1)S(1)}, bf16[512,512]{0,1:T(8,128)(2,1)}, u32[]{:S(2)}, u32[]{:S(2)}) collective-permute-start(bf16[512,512]{0,1:T(8,128)(2,1)S(1)} %bitcast.49), channel_id=1, source_target_pairs={{0,4},{4,8},{8,12},{12,0},{1,5},{5,9},{9,13},{13,1},{2,6},{6,10},{... | collective-permute-start | bytes 1572872 | tf_op jit(solution)/shard_map/ppermute | solution.py:49
  81.7 24.3 %collective-permute-start.2 = (bf16[512,512]{0,1:T(8,128)(2,1)S(1)}, bf16[512,512]{0,1:T(8,128)(2,1)}, u32[]{:S(2)}, u32[]{:S(2)}) collective-permute-start(bf16[512,512]{0,1:T(8,128)(2,1)S(1)} %bitcast.55), channel_id=1, source_target_pairs={{0,4},{4,8},{8,12},{12,0},{1,5},{5,9},{9,13},{13,1},{2,6},{6,10},{... | collective-permute-start | bytes 1572872 | tf_op jit(solution)/shard_map/ppermute | solution.py:51
  83.7 22.3 %collective-permute-start.3 = (bf16[512,512]{0,1:T(8,128)(2,1)S(1)}, bf16[512,512]{0,1:T(8,128)(2,1)}, u32[]{:S(2)}, u32[]{:S(2)}) collective-permute-start(bf16[512,512]{0,1:T(8,128)(2,1)S(1)} %bitcast.50), channel_id=1, source_target_pairs={{0,12},{4,0},{8,4},{12,8},{1,13},{5,1},{9,5},{13,9},{2,14},{6,2},{... | collective-permute-start | bytes 1572872 | tf_op jit(solution)/shard_map/ppermute | solution.py:52
  92.0 22.5 %collective-permute-start.7 = (bf16[512,512]{0,1:T(8,128)(2,1)}, bf16[512,512]{0,1:T(8,128)(2,1)}, u32[]{:S(2)}, u32[]{:S(2)}) collective-permute-start(bf16[512,512]{0,1:T(8,128)(2,1)} %collective-permute-done.6), channel_id=1, source_target_pairs={{0,12},{4,0},{8,4},{12,8},{1,13},{5,1},{9,5},{13,9},{2,14},{6,2},{... | collective-permute-start | bytes 1572872 | tf_op jit(solution)/shard_map/ppermute | solution.py:54
  95.1 22.2 %collective-permute-start.5 = (bf16[512,512]{0,1:T(8,128)(2,1)}, bf16[512,512]{0,1:T(8,128)(2,1)}, u32[]{:S(2)}, u32[]{:S(2)}) collective-permute-start(bf16[512,512]{0,1:T(8,128)(2,1)} %collective-permute-done.4), channel_id=1, source_target_pairs={{0,4},{4,8},{8,12},{12,0},{1,5},{5,9},{9,13},{13,1},{2,6},{6,10},{... | collective-permute-start | bytes 1572872 | tf_op jit(solution)/shard_map/ppermute | solution.py:53
  141.1 12.8 %collective-permute-start.8 = (f32[32,512]{1,0:T(8,128)S(1)}, f32[32,512]{1,0:T(8,128)S(1)}, u32[]{:S(2)}, u32[]{:S(2)}) collective-permute-start(f32[32,512]{1,0:T(8,128)S(1)} %convert_reduce_fusion), channel_id=1, source_target_pairs={{0,256},{256,0},{1,257},{257,1},{2,258},{258,2},{3,259},{259,3},{4... | collective-permute-start | bytes 196616 | tf_op jit(solution)/shard_map/ppermute | solution.py:19

commit v7 on v4

v7 whole, which is shorter than its diff:
```python
import jax
import jax.numpy as jnp
import numpy as np
from jax import lax
from jax.sharding import Mesh, PartitionSpec as P

BF = jnp.bfloat16
F32 = jnp.float32


def spread(block, axes, count):
    return lax.all_to_all(jnp.broadcast_to(block[None], (count,) + block.shape), axes, 0, 0)


def shift(count, by):
    return [(index, (index + by) % count) for index in range(count)]


def partner(block, axis):
    return lax.ppermute(block, axis, shift(2, 1))


def solution(mesh):
    aux, row, col = (mesh.shape[name] for name in ("aux", "row", "col"))
    z2, z1, y, zh, core = 2, aux // 8, 4, col // 2, 2
    zl = z2 * z1
    names = ("z2", "z1", "y", "row", "zh", "core")
    fine = Mesh(mesh.devices.reshape(z2, z1, y, row, zh, core), names)
    line = ("z2", "z1")

    def local(g_plus, g_minus, coulomb):
        count, rows, n = coulomb.shape
        depth, cols = g_minus.shape
        thin = g_plus.shape[1]
        me = lax.axis_index("row").astype(jnp.uint32)
        starts = [(me + step) % row * rows for step in range(row)]
        first = lax.axis_index("core") == 0
        lower = lax.axis_index("zh") == 0

        plus = g_plus.T
        theirs = partner(plus, "zh")
        slab = jnp.concatenate([g_minus, jnp.where(lower, plus, theirs), jnp.where(lower, theirs, plus)])
        slab, first, *starts = lax.optimization_barrier((slab, first, *starts))
        slabs = spread(slab, line, zl)
        minus, plus = slabs[:, :depth], slabs[:, depth:]

        minus = spread(minus, ("y", "row"), y * row)
        minus = minus.reshape(y, row, zl, depth, cols).transpose(2, 0, 1, 3, 4).reshape(n, cols)
        half = jnp.einsum("qik,kj->qij", coulomb, minus, preferred_element_type=F32).astype(BF)

        left = lax.ppermute(half, "row", shift(row, 1))
        right = lax.ppermute(half, "row", shift(row, -1))
        far0 = lax.ppermute(left[0], "row", shift(row, 1))
        far1 = lax.ppermute(right[1], "row", shift(row, -1))

        plus, later = lax.optimization_barrier((plus, half))
        plus = spread(plus, "y", y)
        plus, left, right = lax.optimization_barrier((plus, left, right))
        theirs = partner(plus, "core")
        plus = jnp.stack([jnp.where(first, plus, theirs), jnp.where(first, theirs, plus)])
        plus = plus.reshape(core, y, zl, zh, thin, rows).transpose(2, 1, 3, 0, 4, 5).reshape(n, rows)

        def part(step, *strips):
            factor = lax.dynamic_slice(plus, (starts[step], np.uint32(0)), (rows, rows))
            return [jnp.einsum("ki,kj->ij", factor, strip, preferred_element_type=F32) for strip in strips]

        parts = [part(0, *half), part(row - 1, *left), part(1, *right), part(2, far0, far1)]
        pair0, pair1 = (sum(piece[index] for piece in parts) for index in (0, 1))
        total = pair0 * later[0].astype(F32) + pair1 * later[1].astype(F32)

        for axis, size in (("y", y), ("z1", z1)):
            total = total.astype(BF).reshape(size, -1, cols)
            total = jnp.sum(lax.all_to_all(total, axis, 0, 0).astype(F32), axis=0)
        total = -(total + partner(total, "z2"))
        whole = spread(spread(total.astype(BF), "z1", z1), "y", y)
        return whole.reshape(rows, cols)

    in_specs = (
        P("row", ("z2", "z1", "y", "zh", "core")),
        P(("z2", "z1", "y", "row"), ("zh", "core")),
        P(("z2", "z1", "y"), "row", None),
    )
    out_specs = P("row", ("zh", "core"))
    return jax.shard_map(local, mesh=fine, in_specs=in_specs, out_specs=out_specs, check_vma=False)
```

time: 182 us -> 193 us (1.060)
  the two profiles are of different devices: /device:TPU:8 before, /device:TPU:32 now
where the time goes in v7:
time: 193 us
  blocking collectives  120 us (62%)
  starting transfers between devices  37 us (19%)
  waiting for transfers between devices  23.7 us (12%)
  matrix products  6.26 us (3%)
  local copies, waits for them, and re-layouts  3.87 us (2%)
    all_to_all x5, blocking collectives, spread(): lax.all_to_all(jnp.broadcast_to(block[None], (count,) + block.shape), axe...  99.6 us
    ppermute x3, starting transfers between devices, partner(): return lax.ppermute(block, axis, shift(2, 1))  22.7 us
    all_to_all x2, blocking collectives, local(): total = jnp.sum(lax.all_to_all(total, axis, 0, 0).astype(F32), axis=0)  20 us
    ppermute x3, waiting for transfers between devices, partner(): return lax.ppermute(block, axis, shift(2, 1))  7.45 us
    ppermute x1, waiting for transfers between devices, local(): far1 = lax.ppermute(right[1], 'row', shift(row, -1))  6.41 us
    ppermute x1, starting transfers between devices, local(): far1 = lax.ppermute(right[1], 'row', shift(row, -1))  5.41 us
    ppermute x1, waiting for transfers between devices, local(): far0 = lax.ppermute(left[0], 'row', shift(row, 1))  4.88 us
    ppermute x1, starting transfers between devices, local(): right = lax.ppermute(half, 'row', shift(row, -1))  4.26 us
  transfers between devices with their start and end apart: 7, of which 6 were waited for; matrix products, arithmetic and copies ran while one was open for 2% of the time, Pallas kernels for 0%

profile of v7, /device:TPU:32, one launch (start us, length us, event | category | flops | bytes accessed | tf_op | source)
XLA Modules:
  0.0 192.6 jit_solution(7522180699022255433)
XLA Ops:
  0.0 14.8 %collective-permute-start = (bf16[16,512]{1,0:T(8,128)(2,1)}, bf16[16,512]{1,0:T(8,128)(2,1)S(1)}, u32[]{:S(2)}, u32[]{:S(2)}) collective-permute-start(bf16[16,512]{1,0:T(8,128)(2,1)} %bitcast.70), channel_id=1, source_target_pairs={{0,2},{2,0},{1,3},{3,1},{4,6},{6,4},{5,7},{7,5},{8,10},{10,8},{9,1... | collective-permute-start | bytes 49160 | tf_op jit(solution)/shard_map/ppermute | solution.py:20
  14.8 2.2 %collective-permute-done = bf16[16,512]{1,0:T(8,128)(2,1)S(1)} collective-permute-done((bf16[16,512]{1,0:T(8,128)(2,1)}, bf16[16,512]{1,0:T(8,128)(2,1)S(1)}, u32[]{:S(2)}, u32[]{:S(2)}) %collective-permute-start) | collective-permute-done | bytes 16416 | tf_op jit(solution)/shard_map/ppermute | solution.py:20
  17.0 0.7 broadcast_select_fusion.3
  17.7 0.7 pad_maximum_fusion.1
  18.5 30.4 %all_to_all.35 = bf16[8,48,512]{2,1,0:T(8,128)(2,1)S(1)} all-to-all(bf16[8,48,512]{2,1,0:T(8,128)(2,1)S(1)} %broadcast_in_dim.10), channel_id=1, replica_groups=mesh['z2'=2,'z1'=4,'y'=4,'row'=4,'zh'=2,'core'=2] {'z2','z1'}, dimensions={0} | all-to-all | bytes 786432 | tf_op jit(solution)/shard_map/all_to_all | solution.py:12
  49.1 34.8 %all_to_all.36 = bf16[16,8,16,512]{3,2,1,0:T(8,128)(2,1)S(1)} all-to-all(bf16[16,8,16,512]{3,2,1,0:T(8,128)(2,1)S(1)} %broadcast_in_dim.11), channel_id=1, replica_groups=mesh['z2'=2,'z1'=4,'y'=4,'row'=4,'zh'=2,'core'=2] {'y','row'}, dimensions={0} | all-to-all | bytes 4194304 | tf_op jit(solution)/shard_map/all_to_all | solution.py:12
  84.1 2.0 %copy-done = bf16[2,512,2048]{2,1,0:T(8,128)(2,1)S(1)} copy-done((bf16[2,512,2048]{2,1,0:T(8,128)(2,1)S(1)}, bf16[2,512,2048]{2,1,0:T(8,128)(2,1)}, u32[]{:S(2)}) %copy-start) | copy-done | bytes 4194328
  86.1 2.4 %fusion = bf16[2,512,512]{1,2,0:T(8,128)(2,1)S(1)} fusion(bf16[2048,512,1]{1,0,2:T(8,128)(2,1)S(1)} %bitcast.66, bf16[2,512,2048]{2,1,0:T(8,128)(2,1)S(1)} %copy-done), kind=kOutput, calls=%fused_computation.2 | convolution fusion | flops 2148007936 | bytes 7340032 | tf_op jit(solution)/shard_map/qik,kj->qij/dot_general | solution.py:49
  88.5 2.8 %collective-permute-start.1 = (bf16[2,512,512]{1,2,0:T(8,128)(2,1)S(1)}, bf16[2,512,512]{1,2,0:T(8,128)(2,1)S(1)}, u32[]{:S(2)}, u32[]{:S(2)}) collective-permute-start(bf16[2,512,512]{1,2,0:T(8,128)(2,1)S(1)} %fusion), channel_id=1, source_target_pairs={{0,4},{4,8},{8,12},{12,0},{1,5},{5,9},{9,13},{13,1},{2,6},{6,10},{... | collective-permute-start | bytes 3145736 | tf_op jit(solution)/shard_map/ppermute | solution.py:51
  91.3 4.3 %collective-permute-start.2 = (bf16[2,512,512]{1,2,0:T(8,128)(2,1)S(1)}, bf16[2,512,512]{1,2,0:T(8,128)(2,1)S(1)}, u32[]{:S(2)}, u32[]{:S(2)}) collective-permute-start(bf16[2,512,512]{1,2,0:T(8,128)(2,1)S(1)} %fusion), channel_id=1, source_target_pairs={{0,12},{4,0},{8,4},{12,8},{1,13},{5,1},{9,5},{13,9},{2,14},{6,2},{... | collective-permute-start | bytes 3145736 | tf_op jit(solution)/shard_map/ppermute | solution.py:52
  95.7 14.7 %all_to_all.37 = bf16[4,8,32,512]{3,2,1,0:T(8,128)(2,1)S(1)} all-to-all(bf16[4,8,32,512]{3,2,1,0:T(8,128)(2,1)S(1)} %broadcast_in_dim.12), channel_id=1, replica_groups=mesh['z2'=2,'z1'=4,'y'=4,'row'=4,'zh'=2,'core'=2] {'y'}, dimensions={0} | all-to-all | bytes 2097152 | tf_op jit(solution)/shard_map/all_to_all | solution.py:12
  110.4 3.5 %collective-permute-done.1 = bf16[2,512,512]{1,2,0:T(8,128)(2,1)S(1)} collective-permute-done((bf16[2,512,512]{1,2,0:T(8,128)(2,1)S(1)}, bf16[2,512,512]{1,2,0:T(8,128)(2,1)S(1)}, u32[]{:S(2)}, u32[]{:S(2)}) %collective-permute-start.1) | collective-permute-done | bytes 1048608 | tf_op jit(solution)/shard_map/ppermute | solution.py:51
  114.0 1.4 collective-permute-done.2
  115.3 1.9 collective-permute-start.3
  117.3 5.4 %collective-permute-start.5 = (bf16[512,512]{0,1:T(8,128)(2,1)S(1)}, bf16[512,512]{0,1:T(8,128)(2,1)S(1)}, u32[]{:S(2)}, u32[]{:S(2)}) collective-permute-start(bf16[512,512]{0,1:T(8,128)(2,1)S(1)} %slice_bitcast_fusion), channel_id=1, source_target_pairs={{0,12},{4,0},{8,4},{12,8},{1,13},{5,1},{9,5},{13,9},{2,14},{6,2},{... | collective-permute-start | bytes 1572872 | tf_op jit(solution)/shard_map/ppermute | solution.py:54
  122.8 1.9 collective-permute-start.4
  125.2 0.5 fusion.6
  126.2 0.5 convolution_add_fusion.2
  126.7 0.5 convolution_add_fusion.5
  127.1 0.5 convolution_add_fusion.1
  127.6 0.5 convolution_add_fusion.4
  128.1 6.4 %collective-permute-done.5 = bf16[512,512]{0,1:T(8,128)(2,1)S(1)} collective-permute-done((bf16[512,512]{0,1:T(8,128)(2,1)S(1)}, bf16[512,512]{0,1:T(8,128)(2,1)S(1)}, u32[]{:S(2)}, u32[]{:S(2)}) %collective-permute-start.5) | collective-permute-done | bytes 524320 | tf_op jit(solution)/shard_map/ppermute | solution.py:54
  134.5 0.5 fusion.1
  135.0 4.9 %collective-permute-done.4 = bf16[512,512]{0,1:T(8,128)(2,1)S(1)} collective-permute-done((bf16[512,512]{0,1:T(8,128)(2,1)S(1)}, bf16[512,512]{0,1:T(8,128)(2,1)S(1)}, u32[]{:S(2)}, u32[]{:S(2)}) %collective-permute-start.4) | collective-permute-done | bytes 524320 | tf_op jit(solution)/shard_map/ppermute | solution.py:53
  139.9 0.5 fusion.5
  140.5 11.7 %all_to_all.38 = bf16[4,128,512]{1,2,0:T(8,128)(2,1)S(1)} all-to-all(bf16[4,128,512]{1,2,0:T(8,128)(2,1)S(1)} %bitcast.67), channel_id=1, replica_groups=mesh['z2'=2,'z1'=4,'y'=4,'row'=4,'zh'=2,'core'=2] {'y'}, dimensions={0} | all-to-all | bytes 1048576 | tf_op jit(solution)/shard_map/all_to_all | solution.py:73
  152.5 8.3 %all_to_all.39 = bf16[4,32,512]{2,1,0:T(8,128)(2,1)S(1)} all-to-all(bf16[4,32,512]{2,1,0:T(8,128)(2,1)S(1)} %bitcast.69), channel_id=1, replica_groups=mesh['z2'=2,'z1'=4,'y'=4,'row'=4,'zh'=2,'core'=2] {'z1'}, dimensions={0} | all-to-all | bytes 262144 | tf_op jit(solution)/shard_map/all_to_all | solution.py:73
  160.7 5.9 %collective-permute-start.6 = (f32[32,512]{1,0:T(8,128)S(1)}, f32[32,512]{1,0:T(8,128)S(1)}, u32[]{:S(2)}, u32[]{:S(2)}) collective-permute-start(f32[32,512]{1,0:T(8,128)S(1)} %convert_reduce_fusion), channel_id=1, source_target_pairs={{0,256},{256,0},{1,257},{257,1},{2,258},{258,2},{3,259},{259,3},{4... | collective-permute-start | bytes 196616 | tf_op jit(solution)/shard_map/ppermute | solution.py:20
  166.7 5.3 %collective-permute-done.6 = f32[32,512]{1,0:T(8,128)S(1)} collective-permute-done((f32[32,512]{1,0:T(8,128)S(1)}, f32[32,512]{1,0:T(8,128)S(1)}, u32[]{:S(2)}, u32[]{:S(2)}) %collective-permute-start.6) | collective-permute-done | bytes 65568 | tf_op jit(solution)/shard_map/ppermute | solution.py:20
  172.0 9.3 %all_to_all.40 = bf16[4,32,512]{2,1,0:T(8,128)(2,1)S(1)} all-to-all(bf16[4,32,512]{2,1,0:T(8,128)(2,1)S(1)} %broadcast_in_dim.13), channel_id=1, replica_groups=mesh['z2'=2,'z1'=4,'y'=4,'row'=4,'zh'=2,'core'=2] {'z1'}, dimensions={0} | all-to-all | bytes 262144 | tf_op jit(solution)/shard_map/all_to_all | solution.py:12
  181.3 10.5 %all_to_all.41 = bf16[4,4,32,512]{3,2,1,0:T(8,128)(2,1)S(1)} all-to-all(bf16[4,4,32,512]{3,2,1,0:T(8,128)(2,1)S(1)} %broadcast_in_dim.14), channel_id=1, replica_groups=mesh['z2'=2,'z1'=4,'y'=4,'row'=4,'zh'=2,'core'=2] {'y'}, dimensions={0} | all-to-all | bytes 1048576 | tf_op jit(solution)/shard_map/all_to_all | solution.py:12
  191.8 0.8 copy.67
  (22 shorter events, 2.0 us)
Async XLA Ops:
  0.0 17.0 %collective-permute-start = (bf16[16,512]{1,0:T(8,128)(2,1)}, bf16[16,512]{1,0:T(8,128)(2,1)S(1)}, u32[]{:S(2)}, u32[]{:S(2)}) collective-permute-start(bf16[16,512]{1,0:T(8,128)(2,1)} %bitcast.70), channel_id=1, source_target_pairs={{0,2},{2,0},{1,3},{3,1},{4,6},{6,4},{5,7},{7,5},{8,10},{10,8},{9,1... | collective-permute-start | bytes 49160 | tf_op jit(solution)/shard_map/ppermute | solution.py:20
  83.9 2.2 %copy-start = (bf16[2,512,2048]{2,1,0:T(8,128)(2,1)S(1)}, bf16[2,512,2048]{2,1,0:T(8,128)(2,1)}, u32[]{:S(2)}) copy-start(bf16[2,512,2048]{2,1,0:T(8,128)(2,1)} %param.5) | copy-start | bytes 12582916
  88.5 25.5 %collective-permute-start.1 = (bf16[2,512,512]{1,2,0:T(8,128)(2,1)S(1)}, bf16[2,512,512]{1,2,0:T(8,128)(2,1)S(1)}, u32[]{:S(2)}, u32[]{:S(2)}) collective-permute-start(bf16[2,512,512]{1,2,0:T(8,128)(2,1)S(1)} %fusion), channel_id=1, source_target_pairs={{0,4},{4,8},{8,12},{12,0},{1,5},{5,9},{9,13},{13,1},{2,6},{6,10},{... | collective-permute-start | bytes 3145736 | tf_op jit(solution)/shard_map/ppermute | solution.py:51
  91.3 24.0 %collective-permute-start.2 = (bf16[2,512,512]{1,2,0:T(8,128)(2,1)S(1)}, bf16[2,512,512]{1,2,0:T(8,128)(2,1)S(1)}, u32[]{:S(2)}, u32[]{:S(2)}) collective-permute-start(bf16[2,512,512]{1,2,0:T(8,128)(2,1)S(1)} %fusion), channel_id=1, source_target_pairs={{0,12},{4,0},{8,4},{12,8},{1,13},{5,1},{9,5},{13,9},{2,14},{6,2},{... | collective-permute-start | bytes 3145736 | tf_op jit(solution)/shard_map/ppermute | solution.py:52
  115.3 9.4 %collective-permute-start.3 = (bf16[4,8,32,512]{3,2,1,0:T(8,128)(2,1)S(1)}, bf16[4,8,32,512]{3,2,1,0:T(8,128)(2,1)S(1)}, u32[]{:S(2)}, u32[]{:S(2)}) collective-permute-start(bf16[4,8,32,512]{3,2,1,0:T(8,128)(2,1)S(1)} %all_to_all.37), channel_id=1, source_target_pairs={{0,1},{1,0},{2,3},{3,2},{4,5},{5,4},{6,7},{7,6},{8,9},{9,8},{10,11... | collective-permute-start | bytes 3145736 | tf_op jit(solution)/shard_map/ppermute | solution.py:20
  117.3 17.2 %collective-permute-start.5 = (bf16[512,512]{0,1:T(8,128)(2,1)S(1)}, bf16[512,512]{0,1:T(8,128)(2,1)S(1)}, u32[]{:S(2)}, u32[]{:S(2)}) collective-permute-start(bf16[512,512]{0,1:T(8,128)(2,1)S(1)} %slice_bitcast_fusion), channel_id=1, source_target_pairs={{0,12},{4,0},{8,4},{12,8},{1,13},{5,1},{9,5},{13,9},{2,14},{6,2},{... | collective-permute-start | bytes 1572872 | tf_op jit(solution)/shard_map/ppermute | solution.py:54
  122.8 17.2 %collective-permute-start.4 = (bf16[512,512]{0,1:T(8,128)(2,1)S(1)}, bf16[512,512]{0,1:T(8,128)(2,1)S(1)}, u32[]{:S(2)}, u32[]{:S(2)}) collective-permute-start(bf16[512,512]{0,1:T(8,128)(2,1)S(1)} %slice_bitcast_fusion.3), channel_id=1, source_target_pairs={{0,4},{4,8},{8,12},{12,0},{1,5},{5,9},{9,13},{13,1},{2,6},{6,10},{... | collective-permute-start | bytes 1572872 | tf_op jit(solution)/shard_map/ppermute | solution.py:53
  160.7 11.2 %collective-permute-start.6 = (f32[32,512]{1,0:T(8,128)S(1)}, f32[32,512]{1,0:T(8,128)S(1)}, u32[]{:S(2)}, u32[]{:S(2)}) collective-permute-start(f32[32,512]{1,0:T(8,128)S(1)} %convert_reduce_fusion), channel_id=1, source_target_pairs={{0,256},{256,0},{1,257},{257,1},{2,258},{258,2},{3,259},{259,3},{4... | collective-permute-start | bytes 196616 | tf_op jit(solution)/shard_map/ppermute | solution.py:20

commit v8 on v6

--- a/solution.py
+++ b/solution.py
@@ -54,8 +54,10 @@
         far1 = lax.ppermute(right1, "row", shift(row, -1))
 
         plus, theirs, later0, later1 = lax.optimization_barrier((plus, theirs, q0, q1))
-        plus = spread(order(plus, theirs, "core"), "y", y)
-        plus, left1, right0 = lax.optimization_barrier((plus, left1, right0))
+        plus = order(plus, theirs, "core")
+        ring = jnp.stack([plus] + [lax.ppermute(plus, "y", shift(y, step)) for step in range(1, y)])
+        mine = lax.axis_index("y")
+        plus = jnp.stack([lax.dynamic_index_in_dim(ring, (mine - at) % y, 0, keepdims=False) for at in range(y)])
         plus = plus.reshape(y, core, zh, zl, thin, rows).transpose(3, 0, 2, 1, 4, 5).reshape(n, rows)
 
         me = lax.axis_index("row")

time: 175 us -> 171 us (0.977)
  matrix products: 12.4 us -> 6.17 us
  waiting for transfers between devices: 36.3 us -> 40.6 us
  other arithmetic: 0.97 us -> 2.87 us
    ppermute x0 -> x3, waiting for transfers between devices: none -> 11.1 us  [local(): lax.ppermute(plus, 'y', shift(y, step))]
    ppermute x1, waiting for transfers between devices: 8.76 us -> 0.01 us  [local(): left1 = lax.ppermute(q1, 'row', shift(row, 1))]
    ppermute x0 -> x3, starting transfers between devices: none -> 7.27 us  [local(): lax.ppermute(plus, 'y', shift(y, step))]
    dot_general x8, matrix products: 9.8 us -> 3.58 us  [part(): jnp.einsum('ki,kj->ij', factor, strip, preferred_element_type=F32)]
    all_to_all x2 -> x1, starting transfers between devices: 10.4 us -> 6.75 us  [spread(): lax.all_to_all(jnp.broadcast_to(block[None], (count,) + block.shape), axe...]
    ppermute x3, starting transfers between devices: 25.5 us -> 22.9 us  [partner(): return lax.ppermute(block, axis, shift(2, 1))]
    ppermute x1, starting transfers between devices: 4.53 us -> 2.06 us  [local(): right0 = lax.ppermute(q0, 'row', shift(row, -1))]
    ppermute x1, waiting for transfers between devices: 0.01 us -> 2.47 us  [local(): left0 = lax.ppermute(q0, 'row', shift(row, 1))]
  transfers between devices with their start and end apart: 11 -> 13, of which waited for: 7 -> 8; matrix products, arithmetic and copies ran while one was open for 6% -> 5% of each run, Pallas kernels for 0% -> 0%
where the time goes in v8:
time: 171 us
  blocking collectives  66.1 us (39%)
  starting transfers between devices  51.2 us (30%)
  waiting for transfers between devices  40.6 us (24%)
  matrix products  6.17 us (4%)
  local copies, waits for them, and re-layouts  3.2 us (2%)
  other arithmetic  2.87 us (2%)
    all_to_all x2, blocking collectives, spread(): lax.all_to_all(jnp.broadcast_to(block[None], (count,) + block.shape), axe...  43.4 us
    ppermute x3, starting transfers between devices, partner(): return lax.ppermute(block, axis, shift(2, 1))  22.9 us
    all_to_all x1, blocking collectives, local(): lax.all_to_all(total.astype(BF).reshape(parts, rows // parts, cols), ('y'...  22.7 us
    ppermute x3, waiting for transfers between devices, partner(): return lax.ppermute(block, axis, shift(2, 1))  13.4 us
    ppermute x3, waiting for transfers between devices, local(): lax.ppermute(plus, 'y', shift(y, step))  11.1 us
    all_to_all x1, waiting for transfers between devices, spread(): lax.all_to_all(jnp.broadcast_to(block[None], (count,) + block.shape), axe...  9.46 us
    ppermute x3, starting transfers between devices, local(): lax.ppermute(plus, 'y', shift(y, step))  7.27 us
    all_to_all x1, starting transfers between devices, spread(): lax.all_to_all(jnp.broadcast_to(block[None], (count,) + block.shape), axe...  6.75 us
  transfers between devices with their start and end apart: 13, of which 8 were waited for; matrix products, arithmetic and copies ran while one was open for 5% of the time, Pallas kernels for 0%

profile of v8, /device:TPU:1, one launch (start us, length us, event | category | flops | bytes accessed | tf_op | source)
XLA Modules:
  0.0 170.6 jit_solution(1161479587063629051)
XLA Ops:
  0.0 0.7 pad_maximum_fusion.4
  0.8 25.1 %all_to_all.20 = bf16[8,32,512]{2,1,0:T(8,128)(2,1)S(1)} all-to-all(bf16[8,32,512]{2,1,0:T(8,128)(2,1)S(1)} %broadcast_in_dim.6), channel_id=1, replica_groups=mesh['z2'=2,'z1'=4,'y'=4,'row'=4,'zh'=2,'core'=2] {'z2','z1'}, dimensions={0} | all-to-all | bytes 524288 | tf_op jit(solution)/shard_map/all_to_all | solution.py:11
  25.9 1.6 broadcast_in_dim.7
  27.5 6.8 %all-to-all-start.1 = ((bf16[16,8,16,512]{3,2,1,0:T(8,128)(2,1)}), bf16[16,8,16,512]{3,2,1,0:T(8,128)(2,1)S(1)}, u32[]{:S(2)}, u32[]{:S(2)}) async-start(bf16[16,8,16,512]{3,2,1,0:T(8,128)(2,1)} %broadcast_in_dim.7), calls=%async_computation.1 | async-start | bytes 4194304 | tf_op jit(solution)/shard_map/all_to_all | solution.py:11
  34.2 7.9 %collective-permute-start = (bf16[8,16,512]{2,1,0:T(8,128)(2,1)S(1)}, bf16[8,16,512]{2,1,0:T(8,128)(2,1)S(1)}, u32[]{:S(2)}, u32[]{:S(2)}) collective-permute-start(bf16[8,16,512]{2,1,0:T(8,128)(2,1)S(1)} %get-tuple-element.12), channel_id=1, source_target_pairs={{0,2},{2,0},{1,3},{3,1},{4,6},{6,4},{5,7},{7,5},{8,10},{10,8},{9,1... | collective-permute-start | bytes 393224 | tf_op jit(solution)/shard_map/ppermute | solution.py:19
  42.2 6.7 %collective-permute-done = bf16[8,16,512]{2,1,0:T(8,128)(2,1)S(1)} collective-permute-done((bf16[8,16,512]{2,1,0:T(8,128)(2,1)S(1)}, bf16[8,16,512]{2,1,0:T(8,128)(2,1)S(1)}, u32[]{:S(2)}, u32[]{:S(2)}) %collective-permute-start) | collective-permute-done | bytes 131104 | tf_op jit(solution)/shard_map/ppermute | solution.py:19
  48.9 9.5 %all-to-all-done.1 = bf16[16,8,16,512]{3,2,1,0:T(8,128)(2,1)S(1)} async-done(((bf16[16,8,16,512]{3,2,1,0:T(8,128)(2,1)}), bf16[16,8,16,512]{3,2,1,0:T(8,128)(2,1)S(1)}, u32[]{:S(2)}, u32[]{:S(2)}) %all-to-all-start.1) | async-done | bytes 2097184 | tf_op jit(solution)/shard_map/all_to_all | solution.py:11
  58.6 9.8 %collective-permute-start.1 = (bf16[2,8,16,512]{3,2,0,1:T(8,128)(2,1)S(1)}, bf16[2,8,16,512]{3,2,0,1:T(8,128)(2,1)S(1)}, u32[]{:S(2)}, u32[]{:S(2)}) collective-permute-start(bf16[2,8,16,512]{3,2,0,1:T(8,128)(2,1)S(1)} %pad_maximum_fusion.3), channel_id=1, source_target_pairs={{0,1},{1,0},{2,3},{3,2},{4,5},{5,4},{6,7},{7,6},{8,9},{9,8},{10,11... | collective-permute-start | bytes 786440 | tf_op jit(solution)/shard_map/ppermute | solution.py:19
  68.4 1.3 fusion.12
  69.8 1.9 %collective-permute-start.9 = (bf16[512,512]{0,1:T(8,128)(2,1)S(1)}, bf16[512,512]{0,1:T(8,128)(2,1)S(1)}, u32[]{:S(2)}, u32[]{:S(2)}) collective-permute-start(bf16[512,512]{0,1:T(8,128)(2,1)S(1)} %bitcast.69), channel_id=1, source_target_pairs={{0,12},{4,0},{8,4},{12,8},{1,13},{5,1},{9,5},{13,9},{2,14},{6,2},{... | collective-permute-start | bytes 1572872 | tf_op jit(solution)/shard_map/ppermute | solution.py:50
  71.7 1.3 fusion.9
  73.0 3.4 %collective-permute-start.5 = (bf16[512,512]{0,1:T(8,128)(2,1)S(1)}, bf16[512,512]{0,1:T(8,128)(2,1)S(1)}, u32[]{:S(2)}, u32[]{:S(2)}) collective-permute-start(bf16[512,512]{0,1:T(8,128)(2,1)S(1)} %bitcast.64), channel_id=1, source_target_pairs={{0,4},{4,8},{8,12},{12,0},{1,5},{5,9},{9,13},{13,1},{2,6},{6,10},{... | collective-permute-start | bytes 1572872 | tf_op jit(solution)/shard_map/ppermute | solution.py:49
  76.5 2.8 %collective-permute-start.4 = (bf16[2,2,8,16,512]{4,3,0,1,2:T(8,128)(2,1)S(1)}, bf16[2,2,8,16,512]{4,3,0,1,2:T(8,128)(2,1)}, u32[]{:S(2)}, u32[]{:S(2)}) collective-permute-start(bf16[2,2,8,16,512]{4,3,0,1,2:T(8,128)(2,1)S(1)} %get-tuple-element.24), channel_id=1, source_target_pairs={{0,48},{16,0},{32,16},{48,32},{1,49},{17,1},{33,17},{49,33},{2,50}... | collective-permute-start | bytes 1572872 | tf_op jit(solution)/shard_map/ppermute | solution.py:58
  79.3 2.5 %collective-permute-start.3 = (bf16[2,2,8,16,512]{4,3,0,1,2:T(8,128)(2,1)S(1)}, bf16[2,2,8,16,512]{4,3,0,1,2:T(8,128)(2,1)}, u32[]{:S(2)}, u32[]{:S(2)}) collective-permute-start(bf16[2,2,8,16,512]{4,3,0,1,2:T(8,128)(2,1)S(1)} %get-tuple-element.24), channel_id=1, source_target_pairs={{0,32},{16,48},{32,0},{48,16},{1,33},{17,49},{33,1},{49,17},{2,34}... | collective-permute-start | bytes 1572872 | tf_op jit(solution)/shard_map/ppermute | solution.py:58
  81.9 1.9 %collective-permute-start.2 = (bf16[2,2,8,16,512]{4,3,0,1,2:T(8,128)(2,1)S(1)}, bf16[2,2,8,16,512]{4,3,0,1,2:T(8,128)(2,1)}, u32[]{:S(2)}, u32[]{:S(2)}) collective-permute-start(bf16[2,2,8,16,512]{4,3,0,1,2:T(8,128)(2,1)S(1)} %get-tuple-element.24), channel_id=1, source_target_pairs={{0,16},{16,32},{32,48},{48,0},{1,17},{17,33},{33,49},{49,1},{2,18}... | collective-permute-start | bytes 1572872 | tf_op jit(solution)/shard_map/ppermute | solution.py:58
  83.9 1.4 collective-permute-done.9
  85.3 2.0 %collective-permute-start.8 = (bf16[512,512]{0,1:T(8,128)(2,1)S(1)}, bf16[512,512]{0,1:T(8,128)(2,1)S(1)}, u32[]{:S(2)}, u32[]{:S(2)}) collective-permute-start(bf16[512,512]{0,1:T(8,128)(2,1)S(1)} %bitcast.70), channel_id=1, source_target_pairs={{0,4},{4,8},{8,12},{12,0},{1,5},{5,9},{9,13},{13,1},{2,6},{6,10},{... | collective-permute-start | bytes 1572872 | tf_op jit(solution)/shard_map/ppermute | solution.py:51
  87.3 2.5 %collective-permute-done.5 = bf16[512,512]{0,1:T(8,128)(2,1)S(1)} collective-permute-done((bf16[512,512]{0,1:T(8,128)(2,1)S(1)}, bf16[512,512]{0,1:T(8,128)(2,1)S(1)}, u32[]{:S(2)}, u32[]{:S(2)}) %collective-permute-start.5) | collective-permute-done | bytes 524320 | tf_op jit(solution)/shard_map/ppermute | solution.py:49
  89.7 2.1 %collective-permute-start.6 = (bf16[512,512]{0,1:T(8,128)(2,1)S(1)}, bf16[512,512]{0,1:T(8,128)(2,1)S(1)}, u32[]{:S(2)}, u32[]{:S(2)}) collective-permute-start(bf16[512,512]{0,1:T(8,128)(2,1)S(1)} %bitcast.65), channel_id=1, source_target_pairs={{0,12},{4,0},{8,4},{12,8},{1,13},{5,1},{9,5},{13,9},{2,14},{6,2},{... | collective-permute-start | bytes 1572872 | tf_op jit(solution)/shard_map/ppermute | solution.py:52
  91.8 3.0 %collective-permute-start.10 = (bf16[512,512]{0,1:T(8,128)(2,1)S(1)}, bf16[512,512]{0,1:T(8,128)(2,1)S(1)}, u32[]{:S(2)}, u32[]{:S(2)}) collective-permute-start(bf16[512,512]{0,1:T(8,128)(2,1)S(1)} %collective-permute-done.9), channel_id=1, source_target_pairs={{0,12},{4,0},{8,4},{12,8},{1,13},{5,1},{9,5},{13,9},{2,14},{6,2},{... | collective-permute-start | bytes 1572872 | tf_op jit(solution)/shard_map/ppermute | solution.py:54
  94.8 0.6 collective-permute-done.3
  95.5 2.0 %collective-permute-start.7 = (bf16[512,512]{0,1:T(8,128)(2,1)S(1)}, bf16[512,512]{0,1:T(8,128)(2,1)S(1)}, u32[]{:S(2)}, u32[]{:S(2)}) collective-permute-start(bf16[512,512]{0,1:T(8,128)(2,1)S(1)} %collective-permute-done.5), channel_id=1, source_target_pairs={{0,4},{4,8},{8,12},{12,0},{1,5},{5,9},{9,13},{13,1},{2,6},{6,10},{... | collective-permute-start | bytes 1572872 | tf_op jit(solution)/shard_map/ppermute | solution.py:53
  97.5 10.5 %collective-permute-done.2 = bf16[2,2,8,16,512]{4,3,0,1,2:T(8,128)(2,1)} collective-permute-done((bf16[2,2,8,16,512]{4,3,0,1,2:T(8,128)(2,1)S(1)}, bf16[2,2,8,16,512]{4,3,0,1,2:T(8,128)(2,1)}, u32[]{:S(2)}, u32[]{:S(2)}) %collective-permute-start.2) | collective-permute-done | bytes 524320 | tf_op jit(solution)/shard_map/ppermute | solution.py:58
  107.9 1.6 pad_maximum_fusion
  111.5 0.4 convolution_add_fusion.2
  112.8 2.8 %collective-permute-done.10 = bf16[512,512]{0,1:T(8,128)(2,1)S(1)} collective-permute-done((bf16[512,512]{0,1:T(8,128)(2,1)S(1)}, bf16[512,512]{0,1:T(8,128)(2,1)S(1)}, u32[]{:S(2)}, u32[]{:S(2)}) %collective-permute-start.10) | collective-permute-done | bytes 524320 | tf_op jit(solution)/shard_map/ppermute | solution.py:54
  116.1 0.5 fusion.15
  116.8 22.7 %all_to_all.21 = bf16[16,32,512]{2,1,0:T(8,128)(2,1)S(1)} all-to-all(bf16[16,32,512]{2,1,0:T(8,128)(2,1)S(1)} %bitcast.72), channel_id=1, replica_groups=mesh['z2'=2,'z1'=4,'y'=4,'row'=4,'zh'=2,'core'=2] {'y','z1'}, dimensions={0} | all-to-all | bytes 1048576 | tf_op jit(solution)/shard_map/all_to_all | solution.py:77
  139.6 5.1 %collective-permute-start.11 = (f32[32,512]{1,0:T(8,128)S(1)}, f32[32,512]{1,0:T(8,128)S(1)}, u32[]{:S(2)}, u32[]{:S(2)}) collective-permute-start(f32[32,512]{1,0:T(8,128)S(1)} %convert_reduce_fusion), channel_id=1, source_target_pairs={{0,256},{256,0},{1,257},{257,1},{2,258},{258,2},{3,259},{259,3},{4... | collective-permute-start | bytes 196616 | tf_op jit(solution)/shard_map/ppermute | solution.py:19
  144.7 6.7 %collective-permute-done.11 = f32[32,512]{1,0:T(8,128)S(1)} collective-permute-done((f32[32,512]{1,0:T(8,128)S(1)}, f32[32,512]{1,0:T(8,128)S(1)}, u32[]{:S(2)}, u32[]{:S(2)}) %collective-permute-start.11) | collective-permute-done | bytes 65568 | tf_op jit(solution)/shard_map/ppermute | solution.py:19
  151.5 18.3 %all_to_all.22 = bf16[16,32,512]{2,1,0:T(8,128)(2,1)S(1)} all-to-all(bf16[16,32,512]{2,1,0:T(8,128)(2,1)S(1)} %broadcast_in_dim.8), channel_id=1, replica_groups=mesh['z2'=2,'z1'=4,'y'=4,'row'=4,'zh'=2,'core'=2] {'y','z1'}, dimensions={0} | all-to-all | bytes 1048576 | tf_op jit(solution)/shard_map/all_to_all | solution.py:11
  169.8 0.8 copy.50
  (26 shorter events, 4.0 us)
Async XLA Ops:
  27.5 30.8 %all-to-all-start.1 = ((bf16[16,8,16,512]{3,2,1,0:T(8,128)(2,1)}), bf16[16,8,16,512]{3,2,1,0:T(8,128)(2,1)S(1)}, u32[]{:S(2)}, u32[]{:S(2)}) async-start(bf16[16,8,16,512]{3,2,1,0:T(8,128)(2,1)} %broadcast_in_dim.7), calls=%async_computation.1 | async-start | bytes 4194304 | tf_op jit(solution)/shard_map/all_to_all | solution.py:11
  34.2 14.6 %collective-permute-start = (bf16[8,16,512]{2,1,0:T(8,128)(2,1)S(1)}, bf16[8,16,512]{2,1,0:T(8,128)(2,1)S(1)}, u32[]{:S(2)}, u32[]{:S(2)}) collective-permute-start(bf16[8,16,512]{2,1,0:T(8,128)(2,1)S(1)} %get-tuple-element.12), channel_id=1, source_target_pairs={{0,2},{2,0},{1,3},{3,1},{4,6},{6,4},{5,7},{7,5},{8,10},{10,8},{9,1... | collective-permute-start | bytes 393224 | tf_op jit(solution)/shard_map/ppermute | solution.py:19
  58.3 10.1 %copy-start = (bf16[2,512,2048]{2,1,0:T(8,128)(2,1)S(1)}, bf16[2,512,2048]{2,1,0:T(8,128)(2,1)}, u32[]{:S(2)}) copy-start(bf16[2,512,2048]{2,1,0:T(8,128)(2,1)} %param.5) | copy-start | bytes 12582916
  58.6 17.8 %collective-permute-start.1 = (bf16[2,8,16,512]{3,2,0,1:T(8,128)(2,1)S(1)}, bf16[2,8,16,512]{3,2,0,1:T(8,128)(2,1)S(1)}, u32[]{:S(2)}, u32[]{:S(2)}) collective-permute-start(bf16[2,8,16,512]{3,2,0,1:T(8,128)(2,1)S(1)} %pad_maximum_fusion.3), channel_id=1, source_target_pairs={{0,1},{1,0},{2,3},{3,2},{4,5},{5,4},{6,7},{7,6},{8,9},{9,8},{10,11... | collective-permute-start | bytes 786440 | tf_op jit(solution)/shard_map/ppermute | solution.py:19
  69.8 15.5 %collective-permute-start.9 = (bf16[512,512]{0,1:T(8,128)(2,1)S(1)}, bf16[512,512]{0,1:T(8,128)(2,1)S(1)}, u32[]{:S(2)}, u32[]{:S(2)}) collective-permute-start(bf16[512,512]{0,1:T(8,128)(2,1)S(1)} %bitcast.69), channel_id=1, source_target_pairs={{0,12},{4,0},{8,4},{12,8},{1,13},{5,1},{9,5},{13,9},{2,14},{6,2},{... | collective-permute-start | bytes 1572872 | tf_op jit(solution)/shard_map/ppermute | solution.py:50
  73.0 16.8 %collective-permute-start.5 = (bf16[512,512]{0,1:T(8,128)(2,1)S(1)}, bf16[512,512]{0,1:T(8,128)(2,1)S(1)}, u32[]{:S(2)}, u32[]{:S(2)}) collective-permute-start(bf16[512,512]{0,1:T(8,128)(2,1)S(1)} %bitcast.64), channel_id=1, source_target_pairs={{0,4},{4,8},{8,12},{12,0},{1,5},{5,9},{9,13},{13,1},{2,6},{6,10},{... | collective-permute-start | bytes 1572872 | tf_op jit(solution)/shard_map/ppermute | solution.py:49
  76.5 15.3 %collective-permute-start.4 = (bf16[2,2,8,16,512]{4,3,0,1,2:T(8,128)(2,1)S(1)}, bf16[2,2,8,16,512]{4,3,0,1,2:T(8,128)(2,1)}, u32[]{:S(2)}, u32[]{:S(2)}) collective-permute-start(bf16[2,2,8,16,512]{4,3,0,1,2:T(8,128)(2,1)S(1)} %get-tuple-element.24), channel_id=1, source_target_pairs={{0,48},{16,0},{32,16},{48,32},{1,49},{17,1},{33,17},{49,33},{2,50}... | collective-permute-start | bytes 1572872 | tf_op jit(solution)/shard_map/ppermute | solution.py:58
  79.3 16.1 %collective-permute-start.3 = (bf16[2,2,8,16,512]{4,3,0,1,2:T(8,128)(2,1)S(1)}, bf16[2,2,8,16,512]{4,3,0,1,2:T(8,128)(2,1)}, u32[]{:S(2)}, u32[]{:S(2)}) collective-permute-start(bf16[2,2,8,16,512]{4,3,0,1,2:T(8,128)(2,1)S(1)} %get-tuple-element.24), channel_id=1, source_target_pairs={{0,32},{16,48},{32,0},{48,16},{1,33},{17,49},{33,1},{49,17},{2,34}... | collective-permute-start | bytes 1572872 | tf_op jit(solution)/shard_map/ppermute | solution.py:58
  81.9 26.1 %collective-permute-start.2 = (bf16[2,2,8,16,512]{4,3,0,1,2:T(8,128)(2,1)S(1)}, bf16[2,2,8,16,512]{4,3,0,1,2:T(8,128)(2,1)}, u32[]{:S(2)}, u32[]{:S(2)}) collective-permute-start(bf16[2,2,8,16,512]{4,3,0,1,2:T(8,128)(2,1)S(1)} %get-tuple-element.24), channel_id=1, source_target_pairs={{0,16},{16,32},{32,48},{48,0},{1,17},{17,33},{33,49},{49,1},{2,18}... | collective-permute-start | bytes 1572872 | tf_op jit(solution)/shard_map/ppermute | solution.py:58
  85.3 26.2 %collective-permute-start.8 = (bf16[512,512]{0,1:T(8,128)(2,1)S(1)}, bf16[512,512]{0,1:T(8,128)(2,1)S(1)}, u32[]{:S(2)}, u32[]{:S(2)}) collective-permute-start(bf16[512,512]{0,1:T(8,128)(2,1)S(1)} %bitcast.70), channel_id=1, source_target_pairs={{0,4},{4,8},{8,12},{12,0},{1,5},{5,9},{9,13},{13,1},{2,6},{6,10},{... | collective-permute-start | bytes 1572872 | tf_op jit(solution)/shard_map/ppermute | solution.py:51
  89.7 22.7 %collective-permute-start.6 = (bf16[512,512]{0,1:T(8,128)(2,1)S(1)}, bf16[512,512]{0,1:T(8,128)(2,1)S(1)}, u32[]{:S(2)}, u32[]{:S(2)}) collective-permute-start(bf16[512,512]{0,1:T(8,128)(2,1)S(1)} %bitcast.65), channel_id=1, source_target_pairs={{0,12},{4,0},{8,4},{12,8},{1,13},{5,1},{9,5},{13,9},{2,14},{6,2},{... | collective-permute-start | bytes 1572872 | tf_op jit(solution)/shard_map/ppermute | solution.py:52
  91.8 23.8 %collective-permute-start.10 = (bf16[512,512]{0,1:T(8,128)(2,1)S(1)}, bf16[512,512]{0,1:T(8,128)(2,1)S(1)}, u32[]{:S(2)}, u32[]{:S(2)}) collective-permute-start(bf16[512,512]{0,1:T(8,128)(2,1)S(1)} %collective-permute-done.9), channel_id=1, source_target_pairs={{0,12},{4,0},{8,4},{12,8},{1,13},{5,1},{9,5},{13,9},{2,14},{6,2},{... | collective-permute-start | bytes 1572872 | tf_op jit(solution)/shard_map/ppermute | solution.py:54
  95.5 20.6 %collective-permute-start.7 = (bf16[512,512]{0,1:T(8,128)(2,1)S(1)}, bf16[512,512]{0,1:T(8,128)(2,1)S(1)}, u32[]{:S(2)}, u32[]{:S(2)}) collective-permute-start(bf16[512,512]{0,1:T(8,128)(2,1)S(1)} %collective-permute-done.5), channel_id=1, source_target_pairs={{0,4},{4,8},{8,12},{12,0},{1,5},{5,9},{9,13},{13,1},{2,6},{6,10},{... | collective-permute-start | bytes 1572872 | tf_op jit(solution)/shard_map/ppermute | solution.py:53
  139.6 11.8 %collective-permute-start.11 = (f32[32,512]{1,0:T(8,128)S(1)}, f32[32,512]{1,0:T(8,128)S(1)}, u32[]{:S(2)}, u32[]{:S(2)}) collective-permute-start(f32[32,512]{1,0:T(8,128)S(1)} %convert_reduce_fusion), channel_id=1, source_target_pairs={{0,256},{256,0},{1,257},{257,1},{2,258},{258,2},{3,259},{259,3},{4... | collective-permute-start | bytes 196616 | tf_op jit(solution)/shard_map/ppermute | solution.py:19

commit v9 on v3

--- a/solution.py
+++ b/solution.py
@@ -1,6 +1,7 @@
 import jax
 import jax.numpy as jnp
 from jax import lax
+from jax.experimental.layout import Layout, with_layout_constraint
 from jax.sharding import Mesh, PartitionSpec as P
 
 BF = jnp.bfloat16
@@ -26,21 +27,25 @@
 
 def solution(mesh):
     aux, row, col = (mesh.shape[name] for name in ("aux", "row", "col"))
-    zl, y, zh, core = aux // 4, 4, col // 2, 2
-    fine = Mesh(mesh.devices.reshape(zl, y, row, zh, core), ("zl", "y", "row", "zh", "core"))
+    z2, z1, y, zh, core = 2, aux // 8, 4, col // 2, 2
+    zl = z2 * z1
+    names = ("z2", "z1", "y", "row", "zh", "core")
+    fine = Mesh(mesh.devices.reshape(z2, z1, y, row, zh, core), names)
+    line = ("z2", "z1")
 
     def local(g_plus, g_minus, coulomb):
         count, rows, n = coulomb.shape
         depth, cols = g_minus.shape
         thin = g_plus.shape[1]
-        slabs = spread(jnp.concatenate([g_minus, g_plus.T]), "zl", zl)
+        slabs = spread(jnp.concatenate([g_minus, g_plus.T]), line, zl)
         minus, plus = slabs[:, :depth], slabs[:, depth:]
         theirs = partner(plus, "zh")
         minus = spread(minus, ("y", "row"), y * row)
+        minus, plus, theirs = lax.optimization_barrier((minus, plus, theirs))
         minus = minus.reshape(y, row, zl, depth, cols).transpose(2, 0, 1, 3, 4).reshape(n, cols)
         half = jnp.einsum("qik,kj->qij", coulomb, minus, preferred_element_type=F32).astype(BF)
+        half = with_layout_constraint(half, Layout((0, 1, 2)))
 
-        plus, theirs, later = lax.optimization_barrier((plus, theirs, half))
         plus = spread(order(plus, theirs, "zh"), "y", y)
         plus = order(plus, partner(plus, "core"), "core")
         plus = plus.reshape(core, y, zh, zl, thin, rows).transpose(3, 1, 2, 0, 4, 5).reshape(n, rows)
@@ -62,20 +67,18 @@
         pair += part(right, (me + 1) % row, 0)
         pair += part(top, (me + 2) % row, 0)
         pair += part(bottom, (me + 2) % row, cut)
-        total = jnp.sum(pair * later.astype(F32), axis=0)
+        total = jnp.sum(pair * half.astype(F32), axis=0)
 
-        total = lax.all_to_all(total.astype(BF).reshape(y, rows // y, cols), "y", 0, 0)
+        parts = y * z1
+        total = lax.all_to_all(total.astype(BF).reshape(parts, rows // parts, cols), ("y", "z1"), 0, 0)
         total = jnp.sum(total.astype(F32), axis=0)
-        total = lax.all_to_all(total.astype(BF).reshape(zl, rows // y // zl, cols), "zl", 0, 0)
-        total = -jnp.sum(total.astype(F32), axis=0)
-        whole = spread(total.astype(BF), "zl", zl)
-        whole = spread(whole, "y", y)
-        return whole.reshape(rows, cols)
+        total = -(total + partner(total, "z2"))
+        return spread(total.astype(BF), ("y", "z1"), parts).reshape(rows, cols)
 
     in_specs = (
-        P("row", ("zl", "y", "zh", "core")),
-        P(("zl", "y", "row"), ("zh", "core")),
-        P(("zl", "y"), "row", None),
+        P("row", ("z2", "z1", "y", "zh", "core")),
+        P(("z2", "z1", "y", "row"), ("zh", "core")),
+        P(("z2", "z1", "y"), "row", None),
     )
     out_specs = P("row", ("zh", "core"))
     return jax.shard_map(local, mesh=fine, in_specs=in_specs, out_specs=out_specs, check_vma=False)

time: 179 us -> 170 us (0.950)
  the two profiles are of different devices: /device:TPU:8 before, /device:TPU:4 now
where the time goes in v9:
time: 170 us; the launch traced here: 169 us
  blocking collectives  73 us (43%)
  starting transfers between devices  43.2 us (25%)
  waiting for transfers between devices  36.1 us (21%)
  matrix products  7.28 us (4%)
  local copies, waits for them, and re-layouts  7.13 us (4%)
  other arithmetic  2.44 us (1%)
    all_to_all x2, blocking collectives, spread(): lax.all_to_all(jnp.broadcast_to(block[None], (count,) + block.shape), axe...  48 us
    all_to_all x1, blocking collectives, local(): lax.all_to_all(total.astype(BF).reshape(parts, rows // parts, cols), ('y'...  25 us
    ppermute x3, starting transfers between devices, partner(): return lax.ppermute(block, axis, shift(2, 1))  19.8 us
    ppermute x3, waiting for transfers between devices, partner(): return lax.ppermute(block, axis, shift(2, 1))  17.3 us
    ppermute x1, waiting for transfers between devices, local(): right = lax.ppermute(half, 'row', shift(row, -1))  13.9 us
    all_to_all x2, starting transfers between devices, spread(): lax.all_to_all(jnp.broadcast_to(block[None], (count,) + block.shape), axe...  11.7 us
    dot_general x5, matrix products, part(): return jnp.einsum('ki,qkj->qij', block, strip, preferred_element_type=F32)  4.96 us
    ppermute x1, waiting for transfers between devices, local(): top = lax.ppermute(left[:, :cut], 'row', shift(row, 1))  4.3 us
  transfers between devices with their start and end apart: 9, of which 5 were waited for; matrix products, arithmetic and copies ran while one was open for 6% of the time, Pallas kernels for 0%

profile of v9, /device:TPU:4, one launch (start us, length us, event | category | flops | bytes accessed | tf_op | source)
XLA Modules:
  0.0 169.4 jit_solution(16145413565742346673)
XLA Ops:
  0.0 0.7 pad_maximum_fusion.1
  0.8 29.0 %all_to_all.25 = bf16[8,32,512]{2,1,0:T(8,128)(2,1)S(1)} all-to-all(bf16[8,32,512]{2,1,0:T(8,128)(2,1)S(1)} %broadcast_in_dim.8), channel_id=1, replica_groups=mesh['z2'=2,'z1'=4,'y'=4,'row'=4,'zh'=2,'core'=2] {'z2','z1'}, dimensions={0} | all-to-all | bytes 524288 | tf_op jit(solution)/shard_map/all_to_all | solution.py:12
  29.8 1.6 broadcast_in_dim.9
  31.4 7.4 %all-to-all-start.1 = ((bf16[16,8,16,512]{3,2,1,0:T(8,128)(2,1)}), bf16[16,8,16,512]{3,2,1,0:T(8,128)(2,1)S(1)}, u32[]{:S(2)}, u32[]{:S(2)}) async-start(bf16[16,8,16,512]{3,2,1,0:T(8,128)(2,1)} %broadcast_in_dim.9), calls=%async_computation.1 | async-start | bytes 4194304 | tf_op jit(solution)/shard_map/all_to_all | solution.py:12
  38.8 8.2 %collective-permute-start = (bf16[8,16,512]{2,1,0:T(8,128)(2,1)S(1)}, bf16[8,16,512]{2,1,0:T(8,128)(2,1)S(1)}, u32[]{:S(2)}, u32[]{:S(2)}) collective-permute-start(bf16[8,16,512]{2,1,0:T(8,128)(2,1)S(1)} %get-tuple-element.9), channel_id=1, source_target_pairs={{0,2},{2,0},{1,3},{3,1},{4,6},{6,4},{5,7},{7,5},{8,10},{10,8},{9,1... | collective-permute-start | bytes 393224 | tf_op jit(solution)/shard_map/ppermute | solution.py:20
  47.1 14.4 %collective-permute-done = bf16[8,16,512]{2,1,0:T(8,128)(2,1)S(1)} collective-permute-done((bf16[8,16,512]{2,1,0:T(8,128)(2,1)S(1)}, bf16[8,16,512]{2,1,0:T(8,128)(2,1)S(1)}, u32[]{:S(2)}, u32[]{:S(2)}) %collective-permute-start) | collective-permute-done | bytes 131104 | tf_op jit(solution)/shard_map/ppermute | solution.py:20
  61.5 1.2 broadcast_in_dim.10
  62.7 4.2 %all-to-all-start.2 = ((bf16[4,2,8,16,512]{4,3,1,2,0:T(8,128)(2,1)}), bf16[4,2,8,16,512]{4,3,1,2,0:T(8,128)(2,1)S(1)}, u32[]{:S(2)}, u32[]{:S(2)}) async-start(bf16[4,2,8,16,512]{4,3,1,2,0:T(8,128)(2,1)} %broadcast_in_dim.10), calls=%async_computation.2 | async-start | bytes 2097152 | tf_op jit(solution)/shard_map/all_to_all | solution.py:12
  66.9 0.2 copy.27
  67.2 1.9 %copy-done = bf16[2,512,2048]{2,1,0:T(8,128)(2,1)S(1)} copy-done((bf16[2,512,2048]{2,1,0:T(8,128)(2,1)S(1)}, bf16[2,512,2048]{2,1,0:T(8,128)(2,1)}, u32[]{:S(2)}) %copy-start) | copy-done | bytes 4194328
  69.1 2.3 %fusion.1 = bf16[2,512,512]{2,1,0:T(8,128)(2,1)S(1)} fusion(bf16[2048,512,1]{1,0,2:T(8,128)(2,1)S(1)} %bitcast.56, bf16[2,512,2048]{2,1,0:T(8,128)(2,1)S(1)} %copy-done), kind=kOutput, calls=%fused_computation.4 | convolution fusion | flops 2148007936 | bytes 7340032 | tf_op jit(solution)/shard_map/qik,kj->qij/dot_general | solution.py:46
  71.4 3.6 %collective-permute-start.3 = (bf16[2,512,512]{2,1,0:T(8,128)(2,1)S(1)}, bf16[2,512,512]{2,1,0:T(8,128)(2,1)}, u32[]{:S(2)}, u32[]{:S(2)}) collective-permute-start(bf16[2,512,512]{2,1,0:T(8,128)(2,1)S(1)} %fusion.1), channel_id=1, source_target_pairs={{0,12},{4,0},{8,4},{12,8},{1,13},{5,1},{9,5},{13,9},{2,14},{6,2},{... | collective-permute-start | bytes 3145736 | tf_op jit(solution)/shard_map/ppermute | solution.py:55
  75.1 2.2 %collective-permute-start.2 = (bf16[2,512,512]{2,1,0:T(8,128)(2,1)S(1)}, bf16[2,512,512]{2,1,0:T(8,128)(2,1)S(1)}, u32[]{:S(2)}, u32[]{:S(2)}) collective-permute-start(bf16[2,512,512]{2,1,0:T(8,128)(2,1)S(1)} %fusion.1), channel_id=1, source_target_pairs={{0,4},{4,8},{8,12},{12,0},{1,5},{5,9},{9,13},{13,1},{2,6},{6,10},{... | collective-permute-start | bytes 3145736 | tf_op jit(solution)/shard_map/ppermute | solution.py:54
  77.3 0.5 all-to-all-done.2
  77.8 1.9 %collective-permute-start.1 = (bf16[4,2,8,16,512]{4,3,1,2,0:T(8,128)(2,1)S(1)}, bf16[4,2,8,16,512]{4,3,1,2,0:T(8,128)(2,1)}, u32[]{:S(2)}, u32[]{:S(2)}) collective-permute-start(bf16[4,2,8,16,512]{4,3,1,2,0:T(8,128)(2,1)S(1)} %all-to-all-done.2), channel_id=1, source_target_pairs={{0,1},{1,0},{2,3},{3,2},{4,5},{5,4},{6,7},{7,6},{8,9},{9,8},{10,11... | collective-permute-start | bytes 3145736 | tf_op jit(solution)/shard_map/ppermute | solution.py:20
  79.8 13.9 %collective-permute-done.3 = bf16[2,512,512]{2,1,0:T(8,128)(2,1)} collective-permute-done((bf16[2,512,512]{2,1,0:T(8,128)(2,1)S(1)}, bf16[2,512,512]{2,1,0:T(8,128)(2,1)}, u32[]{:S(2)}, u32[]{:S(2)}) %collective-permute-start.3) | collective-permute-done | bytes 1048608 | tf_op jit(solution)/shard_map/ppermute | solution.py:55
  93.7 1.1 slice.19
  94.7 3.6 %collective-permute-start.5 = (bf16[2,256,512]{2,1,0:T(8,128)(2,1)S(1)}, bf16[2,256,512]{2,1,0:T(8,128)(2,1)S(1)}, u32[]{:S(2)}, u32[]{:S(2)}) collective-permute-start(bf16[2,256,512]{2,1,0:T(8,128)(2,1)S(1)} %slice.19), channel_id=1, source_target_pairs={{0,12},{4,0},{8,4},{12,8},{1,13},{5,1},{9,5},{13,9},{2,14},{6,2},{... | collective-permute-start | bytes 1572872 | tf_op jit(solution)/shard_map/ppermute | solution.py:58
  98.4 2.2 %collective-permute-start.4 = (bf16[2,256,512]{2,1,0:T(8,128)(2,1)S(1)}, bf16[2,256,512]{2,1,0:T(8,128)(2,1)S(1)}, u32[]{:S(2)}, u32[]{:S(2)}) collective-permute-start(bf16[2,256,512]{2,1,0:T(8,128)(2,1)S(1)} %slice.18), channel_id=1, source_target_pairs={{0,4},{4,8},{8,12},{12,0},{1,5},{5,9},{9,13},{13,1},{2,6},{6,10},{... | collective-permute-start | bytes 1572872 | tf_op jit(solution)/shard_map/ppermute | solution.py:57
  100.7 1.4 select_bitcast_fusion.1
  102.0 0.2 maximum_bitcast_fusion
  102.4 0.8 fusion.6
  103.2 2.0 %fusion.2 = f32[2,512,512]{1,2,0:T(8,128)S(1)} fusion(bf16[2,512,512]{2,1,0:T(8,128)(2,1)} %collective-permute-done.3, bf16[2048,512]{1,0:T(8,128)(2,1)S(1)} %bitcast.52, s32[]{:T(128)S(6)} %select_n.66), kind=kOutput, calls=%fused_computation.8 | convolution fusion | flops 536870912 | bytes 3670020 | tf_op jit(solution)/shard_map/ki,qkj->qij/dot_general | solution.py:63
  105.2 4.3 %collective-permute-done.4 = bf16[2,256,512]{2,1,0:T(8,128)(2,1)S(1)} collective-permute-done((bf16[2,256,512]{2,1,0:T(8,128)(2,1)S(1)}, bf16[2,256,512]{2,1,0:T(8,128)(2,1)S(1)}, u32[]{:S(2)}, u32[]{:S(2)}) %collective-permute-start.4) | collective-permute-done | bytes 524320 | tf_op jit(solution)/shard_map/ppermute | solution.py:57
  109.5 0.5 fusion.15
  110.0 0.8 fusion.4
  110.8 1.0 fusion
  111.8 25.0 %all_to_all.26 = bf16[16,32,512]{2,1,0:T(8,128)(2,1)S(1)} all-to-all(bf16[16,32,512]{2,1,0:T(8,128)(2,1)S(1)} %bitcast.58), channel_id=1, replica_groups=mesh['z2'=2,'z1'=4,'y'=4,'row'=4,'zh'=2,'core'=2] {'y','z1'}, dimensions={0} | all-to-all | bytes 1048576 | tf_op jit(solution)/shard_map/all_to_all | solution.py:73
  136.9 9.7 %collective-permute-start.6 = (f32[32,512]{1,0:T(8,128)S(1)}, f32[32,512]{1,0:T(8,128)S(1)}, u32[]{:S(2)}, u32[]{:S(2)}) collective-permute-start(f32[32,512]{1,0:T(8,128)S(1)} %convert_reduce_fusion), channel_id=1, source_target_pairs={{0,256},{256,0},{1,257},{257,1},{2,258},{258,2},{3,259},{259,3},{4... | collective-permute-start | bytes 196616 | tf_op jit(solution)/shard_map/ppermute | solution.py:20
  146.6 3.0 %collective-permute-done.6 = f32[32,512]{1,0:T(8,128)S(1)} collective-permute-done((f32[32,512]{1,0:T(8,128)S(1)}, f32[32,512]{1,0:T(8,128)S(1)}, u32[]{:S(2)}, u32[]{:S(2)}) %collective-permute-start.6) | collective-permute-done | bytes 65568 | tf_op jit(solution)/shard_map/ppermute | solution.py:20
  149.6 19.0 %all_to_all.27 = bf16[16,32,512]{2,1,0:T(8,128)(2,1)S(1)} all-to-all(bf16[16,32,512]{2,1,0:T(8,128)(2,1)S(1)} %broadcast_in_dim.11), channel_id=1, replica_groups=mesh['z2'=2,'z1'=4,'y'=4,'row'=4,'zh'=2,'core'=2] {'y','z1'}, dimensions={0} | all-to-all | bytes 1048576 | tf_op jit(solution)/shard_map/all_to_all | solution.py:12
  168.6 0.8 copy.49
  (15 shorter events, 0.5 us)
Async XLA Ops:
  31.4 30.0 %all-to-all-start.1 = ((bf16[16,8,16,512]{3,2,1,0:T(8,128)(2,1)}), bf16[16,8,16,512]{3,2,1,0:T(8,128)(2,1)S(1)}, u32[]{:S(2)}, u32[]{:S(2)}) async-start(bf16[16,8,16,512]{3,2,1,0:T(8,128)(2,1)} %broadcast_in_dim.9), calls=%async_computation.1 | async-start | bytes 4194304 | tf_op jit(solution)/shard_map/all_to_all | solution.py:12
  38.8 22.6 %collective-permute-start = (bf16[8,16,512]{2,1,0:T(8,128)(2,1)S(1)}, bf16[8,16,512]{2,1,0:T(8,128)(2,1)S(1)}, u32[]{:S(2)}, u32[]{:S(2)}) collective-permute-start(bf16[8,16,512]{2,1,0:T(8,128)(2,1)S(1)} %get-tuple-element.9), channel_id=1, source_target_pairs={{0,2},{2,0},{1,3},{3,1},{4,6},{6,4},{5,7},{7,5},{8,10},{10,8},{9,1... | collective-permute-start | bytes 393224 | tf_op jit(solution)/shard_map/ppermute | solution.py:20
  62.7 15.1 %all-to-all-start.2 = ((bf16[4,2,8,16,512]{4,3,1,2,0:T(8,128)(2,1)}), bf16[4,2,8,16,512]{4,3,1,2,0:T(8,128)(2,1)S(1)}, u32[]{:S(2)}, u32[]{:S(2)}) async-start(bf16[4,2,8,16,512]{4,3,1,2,0:T(8,128)(2,1)} %broadcast_in_dim.10), calls=%async_computation.2 | async-start | bytes 2097152 | tf_op jit(solution)/shard_map/all_to_all | solution.py:12
  66.9 2.2 %copy-start = (bf16[2,512,2048]{2,1,0:T(8,128)(2,1)S(1)}, bf16[2,512,2048]{2,1,0:T(8,128)(2,1)}, u32[]{:S(2)}) copy-start(bf16[2,512,2048]{2,1,0:T(8,128)(2,1)} %param.5) | copy-start | bytes 12582916
  71.4 22.2 %collective-permute-start.3 = (bf16[2,512,512]{2,1,0:T(8,128)(2,1)S(1)}, bf16[2,512,512]{2,1,0:T(8,128)(2,1)}, u32[]{:S(2)}, u32[]{:S(2)}) collective-permute-start(bf16[2,512,512]{2,1,0:T(8,128)(2,1)S(1)} %fusion.1), channel_id=1, source_target_pairs={{0,12},{4,0},{8,4},{12,8},{1,13},{5,1},{9,5},{13,9},{2,14},{6,2},{... | collective-permute-start | bytes 3145736 | tf_op jit(solution)/shard_map/ppermute | solution.py:55
  75.1 23.3 %collective-permute-start.2 = (bf16[2,512,512]{2,1,0:T(8,128)(2,1)S(1)}, bf16[2,512,512]{2,1,0:T(8,128)(2,1)S(1)}, u32[]{:S(2)}, u32[]{:S(2)}) collective-permute-start(bf16[2,512,512]{2,1,0:T(8,128)(2,1)S(1)} %fusion.1), channel_id=1, source_target_pairs={{0,4},{4,8},{8,12},{12,0},{1,5},{5,9},{9,13},{13,1},{2,6},{6,10},{... | collective-permute-start | bytes 3145736 | tf_op jit(solution)/shard_map/ppermute | solution.py:54
  77.8 22.9 %collective-permute-start.1 = (bf16[4,2,8,16,512]{4,3,1,2,0:T(8,128)(2,1)S(1)}, bf16[4,2,8,16,512]{4,3,1,2,0:T(8,128)(2,1)}, u32[]{:S(2)}, u32[]{:S(2)}) collective-permute-start(bf16[4,2,8,16,512]{4,3,1,2,0:T(8,128)(2,1)S(1)} %all-to-all-done.2), channel_id=1, source_target_pairs={{0,1},{1,0},{2,3},{3,2},{4,5},{5,4},{6,7},{7,6},{8,9},{9,8},{10,11... | collective-permute-start | bytes 3145736 | tf_op jit(solution)/shard_map/ppermute | solution.py:20
  94.7 16.0 %collective-permute-start.5 = (bf16[2,256,512]{2,1,0:T(8,128)(2,1)S(1)}, bf16[2,256,512]{2,1,0:T(8,128)(2,1)S(1)}, u32[]{:S(2)}, u32[]{:S(2)}) collective-permute-start(bf16[2,256,512]{2,1,0:T(8,128)(2,1)S(1)} %slice.19), channel_id=1, source_target_pairs={{0,12},{4,0},{8,4},{12,8},{1,13},{5,1},{9,5},{13,9},{2,14},{6,2},{... | collective-permute-start | bytes 1572872 | tf_op jit(solution)/shard_map/ppermute | solution.py:58
  98.4 11.1 %collective-permute-start.4 = (bf16[2,256,512]{2,1,0:T(8,128)(2,1)S(1)}, bf16[2,256,512]{2,1,0:T(8,128)(2,1)S(1)}, u32[]{:S(2)}, u32[]{:S(2)}) collective-permute-start(bf16[2,256,512]{2,1,0:T(8,128)(2,1)S(1)} %slice.18), channel_id=1, source_target_pairs={{0,4},{4,8},{8,12},{12,0},{1,5},{5,9},{9,13},{13,1},{2,6},{6,10},{... | collective-permute-start | bytes 1572872 | tf_op jit(solution)/shard_map/ppermute | solution.py:57
  136.9 12.7 %collective-permute-start.6 = (f32[32,512]{1,0:T(8,128)S(1)}, f32[32,512]{1,0:T(8,128)S(1)}, u32[]{:S(2)}, u32[]{:S(2)}) collective-permute-start(f32[32,512]{1,0:T(8,128)S(1)} %convert_reduce_fusion), channel_id=1, source_target_pairs={{0,256},{256,0},{1,257},{257,1},{2,258},{258,2},{3,259},{259,3},{4... | collective-permute-start | bytes 196616 | tf_op jit(solution)/shard_map/ppermute | solution.py:20

commit v10 on v9

--- a/solution.py
+++ b/solution.py
@@ -27,7 +27,7 @@
 
 def solution(mesh):
     aux, row, col = (mesh.shape[name] for name in ("aux", "row", "col"))
-    z2, z1, y, zh, core = 2, aux // 8, 4, col // 2, 2
+    z2, z1, y, zh, core = aux // 8, 2, 4, col // 2, 2
     zl = z2 * z1
     names = ("z2", "z1", "y", "row", "zh", "core")
     fine = Mesh(mesh.devices.reshape(z2, z1, y, row, zh, core), names)
@@ -71,8 +71,8 @@
 
         parts = y * z1
         total = lax.all_to_all(total.astype(BF).reshape(parts, rows // parts, cols), ("y", "z1"), 0, 0)
-        total = jnp.sum(total.astype(F32), axis=0)
-        total = -(total + partner(total, "z2"))
+        total = jnp.sum(total.astype(F32), axis=0).astype(BF)
+        total = -jnp.sum(spread(total, "z2", z2).astype(F32), axis=0)
         return spread(total.astype(BF), ("y", "z1"), parts).reshape(rows, cols)
 
     in_specs = (

time: 170 us -> 167 us (0.982)
  starting transfers between devices: 43.2 us -> 33.5 us
  blocking collectives: 73 us -> 82.2 us
  waiting for transfers between devices: 36.1 us -> 33.1 us
    all_to_all x2 -> x3, blocking collectives: 48 us -> 68.4 us  [spread(): lax.all_to_all(jnp.broadcast_to(block[None], (count,) + block.shape), axe...]
    all_to_all x1, blocking collectives: 25 us -> 13.8 us  [local(): lax.all_to_all(total.astype(BF).reshape(parts, rows // parts, cols), ('y'...]
    ppermute x3 -> x2, starting transfers between devices: 19.8 us -> 10.1 us  [partner(): return lax.ppermute(block, axis, shift(2, 1))]
    ppermute x3 -> x2, waiting for transfers between devices: 17.3 us -> 14.4 us  [partner(): return lax.ppermute(block, axis, shift(2, 1))]
  transfers between devices with their start and end apart: 9 -> 8, of which waited for: 5 -> 4; matrix products, arithmetic and copies ran while one was open for 6% -> 6% of each run, Pallas kernels for 0% -> 0%
where the time goes in v10:
time: 167 us; the launch traced here: 166 us
  blocking collectives  82.2 us (49%)
  starting transfers between devices  33.5 us (20%)
  waiting for transfers between devices  33.1 us (20%)
  matrix products  7.28 us (4%)
  local copies, waits for them, and re-layouts  7.14 us (4%)
  other arithmetic  2.47 us (1%)
    all_to_all x3, blocking collectives, spread(): lax.all_to_all(jnp.broadcast_to(block[None], (count,) + block.shape), axe...  68.4 us
    ppermute x2, waiting for transfers between devices, partner(): return lax.ppermute(block, axis, shift(2, 1))  14.4 us
    ppermute x1, waiting for transfers between devices, local(): right = lax.ppermute(half, 'row', shift(row, -1))  13.9 us
    all_to_all x1, blocking collectives, local(): lax.all_to_all(total.astype(BF).reshape(parts, rows // parts, cols), ('y'...  13.8 us
    all_to_all x2, starting transfers between devices, spread(): lax.all_to_all(jnp.broadcast_to(block[None], (count,) + block.shape), axe...  11.7 us
    ppermute x2, starting transfers between devices, partner(): return lax.ppermute(block, axis, shift(2, 1))  10.1 us
    dot_general x5, matrix products, part(): return jnp.einsum('ki,qkj->qij', block, strip, preferred_element_type=F32)  4.96 us
    ppermute x1, waiting for transfers between devices, local(): top = lax.ppermute(left[:, :cut], 'row', shift(row, 1))  4.3 us
  transfers between devices with their start and end apart: 8, of which 4 were waited for; matrix products, arithmetic and copies ran while one was open for 6% of the time, Pallas kernels for 0%

profile of v10, /device:TPU:4, one launch (start us, length us, event | category | flops | bytes accessed | tf_op | source)
XLA Modules:
  0.0 166.0 jit_solution(15188243900968895488)
XLA Ops:
  0.0 0.7 pad_maximum_fusion.1
  0.8 29.0 %all_to_all.30 = bf16[8,32,512]{2,1,0:T(8,128)(2,1)S(1)} all-to-all(bf16[8,32,512]{2,1,0:T(8,128)(2,1)S(1)} %broadcast_in_dim.10), channel_id=1, replica_groups=mesh['z2'=4,'z1'=2,'y'=4,'row'=4,'zh'=2,'core'=2] {'z2','z1'}, dimensions={0} | all-to-all | bytes 524288 | tf_op jit(solution)/shard_map/all_to_all | solution.py:12
  29.8 1.6 broadcast_in_dim.11
  31.4 7.4 %all-to-all-start.1 = ((bf16[16,8,16,512]{3,2,1,0:T(8,128)(2,1)}), bf16[16,8,16,512]{3,2,1,0:T(8,128)(2,1)S(1)}, u32[]{:S(2)}, u32[]{:S(2)}) async-start(bf16[16,8,16,512]{3,2,1,0:T(8,128)(2,1)} %broadcast_in_dim.11), calls=%async_computation.1 | async-start | bytes 4194304 | tf_op jit(solution)/shard_map/all_to_all | solution.py:12
  38.8 8.2 %collective-permute-start = (bf16[8,16,512]{2,1,0:T(8,128)(2,1)S(1)}, bf16[8,16,512]{2,1,0:T(8,128)(2,1)S(1)}, u32[]{:S(2)}, u32[]{:S(2)}) collective-permute-start(bf16[8,16,512]{2,1,0:T(8,128)(2,1)S(1)} %get-tuple-element.9), channel_id=1, source_target_pairs={{0,2},{2,0},{1,3},{3,1},{4,6},{6,4},{5,7},{7,5},{8,10},{10,8},{9,1... | collective-permute-start | bytes 393224 | tf_op jit(solution)/shard_map/ppermute | solution.py:20
  47.1 14.4 %collective-permute-done = bf16[8,16,512]{2,1,0:T(8,128)(2,1)S(1)} collective-permute-done((bf16[8,16,512]{2,1,0:T(8,128)(2,1)S(1)}, bf16[8,16,512]{2,1,0:T(8,128)(2,1)S(1)}, u32[]{:S(2)}, u32[]{:S(2)}) %collective-permute-start) | collective-permute-done | bytes 131104 | tf_op jit(solution)/shard_map/ppermute | solution.py:20
  61.5 1.2 broadcast_in_dim.12
  62.7 4.2 %all-to-all-start.2 = ((bf16[4,2,8,16,512]{4,3,1,2,0:T(8,128)(2,1)}), bf16[4,2,8,16,512]{4,3,1,2,0:T(8,128)(2,1)S(1)}, u32[]{:S(2)}, u32[]{:S(2)}) async-start(bf16[4,2,8,16,512]{4,3,1,2,0:T(8,128)(2,1)} %broadcast_in_dim.12), calls=%async_computation.2 | async-start | bytes 2097152 | tf_op jit(solution)/shard_map/all_to_all | solution.py:12
  66.9 0.2 copy.27
  67.2 1.9 %copy-done = bf16[2,512,2048]{2,1,0:T(8,128)(2,1)S(1)} copy-done((bf16[2,512,2048]{2,1,0:T(8,128)(2,1)S(1)}, bf16[2,512,2048]{2,1,0:T(8,128)(2,1)}, u32[]{:S(2)}) %copy-start) | copy-done | bytes 4194328
  69.1 2.3 %fusion.1 = bf16[2,512,512]{2,1,0:T(8,128)(2,1)S(1)} fusion(bf16[2048,512,1]{1,0,2:T(8,128)(2,1)S(1)} %bitcast.56, bf16[2,512,2048]{2,1,0:T(8,128)(2,1)S(1)} %copy-done), kind=kOutput, calls=%fused_computation.4 | convolution fusion | flops 2148007936 | bytes 7340032 | tf_op jit(solution)/shard_map/qik,kj->qij/dot_general | solution.py:46
  71.4 3.6 %collective-permute-start.3 = (bf16[2,512,512]{2,1,0:T(8,128)(2,1)S(1)}, bf16[2,512,512]{2,1,0:T(8,128)(2,1)}, u32[]{:S(2)}, u32[]{:S(2)}) collective-permute-start(bf16[2,512,512]{2,1,0:T(8,128)(2,1)S(1)} %fusion.1), channel_id=1, source_target_pairs={{0,12},{4,0},{8,4},{12,8},{1,13},{5,1},{9,5},{13,9},{2,14},{6,2},{... | collective-permute-start | bytes 3145736 | tf_op jit(solution)/shard_map/ppermute | solution.py:55
  75.1 2.2 %collective-permute-start.2 = (bf16[2,512,512]{2,1,0:T(8,128)(2,1)S(1)}, bf16[2,512,512]{2,1,0:T(8,128)(2,1)S(1)}, u32[]{:S(2)}, u32[]{:S(2)}) collective-permute-start(bf16[2,512,512]{2,1,0:T(8,128)(2,1)S(1)} %fusion.1), channel_id=1, source_target_pairs={{0,4},{4,8},{8,12},{12,0},{1,5},{5,9},{9,13},{13,1},{2,6},{6,10},{... | collective-permute-start | bytes 3145736 | tf_op jit(solution)/shard_map/ppermute | solution.py:54
  77.3 0.5 all-to-all-done.2
  77.8 1.9 %collective-permute-start.1 = (bf16[4,2,8,16,512]{4,3,1,2,0:T(8,128)(2,1)S(1)}, bf16[4,2,8,16,512]{4,3,1,2,0:T(8,128)(2,1)}, u32[]{:S(2)}, u32[]{:S(2)}) collective-permute-start(bf16[4,2,8,16,512]{4,3,1,2,0:T(8,128)(2,1)S(1)} %all-to-all-done.2), channel_id=1, source_target_pairs={{0,1},{1,0},{2,3},{3,2},{4,5},{5,4},{6,7},{7,6},{8,9},{9,8},{10,11... | collective-permute-start | bytes 3145736 | tf_op jit(solution)/shard_map/ppermute | solution.py:20
  79.8 13.9 %collective-permute-done.3 = bf16[2,512,512]{2,1,0:T(8,128)(2,1)} collective-permute-done((bf16[2,512,512]{2,1,0:T(8,128)(2,1)S(1)}, bf16[2,512,512]{2,1,0:T(8,128)(2,1)}, u32[]{:S(2)}, u32[]{:S(2)}) %collective-permute-start.3) | collective-permute-done | bytes 1048608 | tf_op jit(solution)/shard_map/ppermute | solution.py:55
  93.7 1.1 slice.19
  94.8 3.6 %collective-permute-start.5 = (bf16[2,256,512]{2,1,0:T(8,128)(2,1)S(1)}, bf16[2,256,512]{2,1,0:T(8,128)(2,1)S(1)}, u32[]{:S(2)}, u32[]{:S(2)}) collective-permute-start(bf16[2,256,512]{2,1,0:T(8,128)(2,1)S(1)} %slice.19), channel_id=1, source_target_pairs={{0,12},{4,0},{8,4},{12,8},{1,13},{5,1},{9,5},{13,9},{2,14},{6,2},{... | collective-permute-start | bytes 1572872 | tf_op jit(solution)/shard_map/ppermute | solution.py:58
  98.4 2.2 %collective-permute-start.4 = (bf16[2,256,512]{2,1,0:T(8,128)(2,1)S(1)}, bf16[2,256,512]{2,1,0:T(8,128)(2,1)S(1)}, u32[]{:S(2)}, u32[]{:S(2)}) collective-permute-start(bf16[2,256,512]{2,1,0:T(8,128)(2,1)S(1)} %slice.18), channel_id=1, source_target_pairs={{0,4},{4,8},{8,12},{12,0},{1,5},{5,9},{9,13},{13,1},{2,6},{6,10},{... | collective-permute-start | bytes 1572872 | tf_op jit(solution)/shard_map/ppermute | solution.py:57
  100.7 1.4 select_bitcast_fusion.1
  102.1 0.2 maximum_bitcast_fusion
  102.3 0.2 copy.29
  102.5 0.8 fusion.6
  103.2 2.0 %fusion.2 = f32[2,512,512]{1,2,0:T(8,128)S(1)} fusion(bf16[2,512,512]{2,1,0:T(8,128)(2,1)} %collective-permute-done.3, bf16[2048,512]{1,0:T(8,128)(2,1)S(1)} %bitcast.52, s32[]{:T(128)S(6)} %select_n.66), kind=kOutput, calls=%fused_computation.7 | convolution fusion | flops 536870912 | bytes 3670020 | tf_op jit(solution)/shard_map/ki,qkj->qij/dot_general | solution.py:63
  105.2 4.3 %collective-permute-done.4 = bf16[2,256,512]{2,1,0:T(8,128)(2,1)S(1)} collective-permute-done((bf16[2,256,512]{2,1,0:T(8,128)(2,1)S(1)}, bf16[2,256,512]{2,1,0:T(8,128)(2,1)S(1)}, u32[]{:S(2)}, u32[]{:S(2)}) %collective-permute-start.4) | collective-permute-done | bytes 524320 | tf_op jit(solution)/shard_map/ppermute | solution.py:57
  109.5 0.5 fusion.15
  110.0 0.8 fusion.4
  110.8 1.0 fusion
  111.8 13.8 %all_to_all.31 = bf16[8,64,512]{2,1,0:T(8,128)(2,1)S(1)} all-to-all(bf16[8,64,512]{2,1,0:T(8,128)(2,1)S(1)} %bitcast.58), channel_id=1, replica_groups=mesh['z2'=4,'z1'=2,'y'=4,'row'=4,'zh'=2,'core'=2] {'y','z1'}, dimensions={0} | all-to-all | bytes 1048576 | tf_op jit(solution)/shard_map/all_to_all | solution.py:73
  125.7 28.3 %all_to_all.32 = bf16[4,64,512]{2,1,0:T(8,128)(2,1)S(1)} all-to-all(bf16[4,64,512]{2,1,0:T(8,128)(2,1)S(1)} %broadcast_in_dim.13), channel_id=1, replica_groups=mesh['z2'=4,'z1'=2,'y'=4,'row'=4,'zh'=2,'core'=2] {'z2'}, dimensions={0} | all-to-all | bytes 524288 | tf_op jit(solution)/shard_map/all_to_all | solution.py:12
  154.1 11.1 %all_to_all.33 = bf16[8,64,512]{2,1,0:T(8,128)(2,1)S(1)} all-to-all(bf16[8,64,512]{2,1,0:T(8,128)(2,1)S(1)} %broadcast_in_dim.14), channel_id=1, replica_groups=mesh['z2'=4,'z1'=2,'y'=4,'row'=4,'zh'=2,'core'=2] {'y','z1'}, dimensions={0} | all-to-all | bytes 1048576 | tf_op jit(solution)/shard_map/all_to_all | solution.py:12
  165.2 0.8 copy.49
  (16 shorter events, 0.3 us)
Async XLA Ops:
  31.4 30.0 %all-to-all-start.1 = ((bf16[16,8,16,512]{3,2,1,0:T(8,128)(2,1)}), bf16[16,8,16,512]{3,2,1,0:T(8,128)(2,1)S(1)}, u32[]{:S(2)}, u32[]{:S(2)}) async-start(bf16[16,8,16,512]{3,2,1,0:T(8,128)(2,1)} %broadcast_in_dim.11), calls=%async_computation.1 | async-start | bytes 4194304 | tf_op jit(solution)/shard_map/all_to_all | solution.py:12
  38.8 22.6 %collective-permute-start = (bf16[8,16,512]{2,1,0:T(8,128)(2,1)S(1)}, bf16[8,16,512]{2,1,0:T(8,128)(2,1)S(1)}, u32[]{:S(2)}, u32[]{:S(2)}) collective-permute-start(bf16[8,16,512]{2,1,0:T(8,128)(2,1)S(1)} %get-tuple-element.9), channel_id=1, source_target_pairs={{0,2},{2,0},{1,3},{3,1},{4,6},{6,4},{5,7},{7,5},{8,10},{10,8},{9,1... | collective-permute-start | bytes 393224 | tf_op jit(solution)/shard_map/ppermute | solution.py:20
  62.7 15.1 %all-to-all-start.2 = ((bf16[4,2,8,16,512]{4,3,1,2,0:T(8,128)(2,1)}), bf16[4,2,8,16,512]{4,3,1,2,0:T(8,128)(2,1)S(1)}, u32[]{:S(2)}, u32[]{:S(2)}) async-start(bf16[4,2,8,16,512]{4,3,1,2,0:T(8,128)(2,1)} %broadcast_in_dim.12), calls=%async_computation.2 | async-start | bytes 2097152 | tf_op jit(solution)/shard_map/all_to_all | solution.py:12
  66.9 2.2 %copy-start = (bf16[2,512,2048]{2,1,0:T(8,128)(2,1)S(1)}, bf16[2,512,2048]{2,1,0:T(8,128)(2,1)}, u32[]{:S(2)}) copy-start(bf16[2,512,2048]{2,1,0:T(8,128)(2,1)} %param.5) | copy-start | bytes 12582916
  71.4 22.3 %collective-permute-start.3 = (bf16[2,512,512]{2,1,0:T(8,128)(2,1)S(1)}, bf16[2,512,512]{2,1,0:T(8,128)(2,1)}, u32[]{:S(2)}, u32[]{:S(2)}) collective-permute-start(bf16[2,512,512]{2,1,0:T(8,128)(2,1)S(1)} %fusion.1), channel_id=1, source_target_pairs={{0,12},{4,0},{8,4},{12,8},{1,13},{5,1},{9,5},{13,9},{2,14},{6,2},{... | collective-permute-start | bytes 3145736 | tf_op jit(solution)/shard_map/ppermute | solution.py:55
  75.1 23.3 %collective-permute-start.2 = (bf16[2,512,512]{2,1,0:T(8,128)(2,1)S(1)}, bf16[2,512,512]{2,1,0:T(8,128)(2,1)S(1)}, u32[]{:S(2)}, u32[]{:S(2)}) collective-permute-start(bf16[2,512,512]{2,1,0:T(8,128)(2,1)S(1)} %fusion.1), channel_id=1, source_target_pairs={{0,4},{4,8},{8,12},{12,0},{1,5},{5,9},{9,13},{13,1},{2,6},{6,10},{... | collective-permute-start | bytes 3145736 | tf_op jit(solution)/shard_map/ppermute | solution.py:54
  77.8 22.9 %collective-permute-start.1 = (bf16[4,2,8,16,512]{4,3,1,2,0:T(8,128)(2,1)S(1)}, bf16[4,2,8,16,512]{4,3,1,2,0:T(8,128)(2,1)}, u32[]{:S(2)}, u32[]{:S(2)}) collective-permute-start(bf16[4,2,8,16,512]{4,3,1,2,0:T(8,128)(2,1)S(1)} %all-to-all-done.2), channel_id=1, source_target_pairs={{0,1},{1,0},{2,3},{3,2},{4,5},{5,4},{6,7},{7,6},{8,9},{9,8},{10,11... | collective-permute-start | bytes 3145736 | tf_op jit(solution)/shard_map/ppermute | solution.py:20
  94.8 16.0 %collective-permute-start.5 = (bf16[2,256,512]{2,1,0:T(8,128)(2,1)S(1)}, bf16[2,256,512]{2,1,0:T(8,128)(2,1)S(1)}, u32[]{:S(2)}, u32[]{:S(2)}) collective-permute-start(bf16[2,256,512]{2,1,0:T(8,128)(2,1)S(1)} %slice.19), channel_id=1, source_target_pairs={{0,12},{4,0},{8,4},{12,8},{1,13},{5,1},{9,5},{13,9},{2,14},{6,2},{... | collective-permute-start | bytes 1572872 | tf_op jit(solution)/shard_map/ppermute | solution.py:58
  98.4 11.1 %collective-permute-start.4 = (bf16[2,256,512]{2,1,0:T(8,128)(2,1)S(1)}, bf16[2,256,512]{2,1,0:T(8,128)(2,1)S(1)}, u32[]{:S(2)}, u32[]{:S(2)}) collective-permute-start(bf16[2,256,512]{2,1,0:T(8,128)(2,1)S(1)} %slice.18), channel_id=1, source_target_pairs={{0,4},{4,8},{8,12},{12,0},{1,5},{5,9},{9,13},{13,1},{2,6},{6,10},{... | collective-permute-start | bytes 1572872 | tf_op jit(solution)/shard_map/ppermute | solution.py:57

commit v11 on v10

--- a/solution.py
+++ b/solution.py
@@ -28,27 +28,28 @@
 def solution(mesh):
     aux, row, col = (mesh.shape[name] for name in ("aux", "row", "col"))
     z2, z1, y, zh, core = aux // 8, 2, 4, col // 2, 2
-    zl = z2 * z1
     names = ("z2", "z1", "y", "row", "zh", "core")
     fine = Mesh(mesh.devices.reshape(z2, z1, y, row, zh, core), names)
-    line = ("z2", "z1")
 
     def local(g_plus, g_minus, coulomb):
         count, rows, n = coulomb.shape
         depth, cols = g_minus.shape
         thin = g_plus.shape[1]
-        slabs = spread(jnp.concatenate([g_minus, g_plus.T]), line, zl)
+        slabs = spread(jnp.concatenate([g_minus, g_plus.T]), "z2", z2)
         minus, plus = slabs[:, :depth], slabs[:, depth:]
         theirs = partner(plus, "zh")
-        minus = spread(minus, ("y", "row"), y * row)
+        minus = spread(minus, ("y", "z1"), y * z1)
         minus, plus, theirs = lax.optimization_barrier((minus, plus, theirs))
-        minus = minus.reshape(y, row, zl, depth, cols).transpose(2, 0, 1, 3, 4).reshape(n, cols)
+        minus, plus = lax.optimization_barrier((minus, order(plus, theirs, "zh")))
+        minus = spread(minus, "row", row)
+        minus, plus = lax.optimization_barrier((minus, plus))
+        minus = minus.reshape(row, y, z1, z2, depth, cols).transpose(3, 2, 1, 0, 4, 5).reshape(n, cols)
         half = jnp.einsum("qik,kj->qij", coulomb, minus, preferred_element_type=F32).astype(BF)
         half = with_layout_constraint(half, Layout((0, 1, 2)))
 
-        plus = spread(order(plus, theirs, "zh"), "y", y)
+        plus = spread(plus, ("y", "z1"), y * z1)
         plus = order(plus, partner(plus, "core"), "core")
-        plus = plus.reshape(core, y, zh, zl, thin, rows).transpose(3, 1, 2, 0, 4, 5).reshape(n, rows)
+        plus = plus.reshape(core, y, z1, zh, z2, thin, rows).transpose(4, 2, 1, 3, 0, 5, 6).reshape(n, rows)
 
         me = lax.axis_index("row")
         left = lax.ppermute(half, "row", shift(row, 1))

time: 167 us -> 175 us (1.048)
  the two profiles are of different devices: /device:TPU:4 before, /device:TPU:32 now
where the time goes in v11:
time: 175 us; the launch traced here: 174 us
  blocking collectives  95.1 us (54%)
  starting transfers between devices  34.3 us (20%)
  waiting for transfers between devices  28 us (16%)
  matrix products  7.27 us (4%)
  local copies, waits for them, and re-layouts  6.61 us (4%)
  other arithmetic  2.45 us (1%)
    all_to_all x4, blocking collectives, spread(): lax.all_to_all(jnp.broadcast_to(block[None], (count,) + block.shape), axe...  82.1 us
    ppermute x1, waiting for transfers between devices, local(): right = lax.ppermute(half, 'row', shift(row, -1))  14.4 us
    all_to_all x1, blocking collectives, local(): lax.all_to_all(total.astype(BF).reshape(parts, rows // parts, cols), ('y'...  13 us
    all_to_all x2, starting transfers between devices, spread(): lax.all_to_all(jnp.broadcast_to(block[None], (count,) + block.shape), axe...  12.3 us
    ppermute x2, starting transfers between devices, partner(): return lax.ppermute(block, axis, shift(2, 1))  10.3 us
    ppermute x2, waiting for transfers between devices, partner(): return lax.ppermute(block, axis, shift(2, 1))  8.22 us
    ppermute x1, waiting for transfers between devices, local(): top = lax.ppermute(left[:, :cut], 'row', shift(row, 1))  5.41 us
    dot_general x5, matrix products, part(): return jnp.einsum('ki,qkj->qij', block, strip, preferred_element_type=F32)  4.96 us
  transfers between devices with their start and end apart: 8, of which 3 were waited for; matrix products, arithmetic and copies ran while one was open for 5% of the time, Pallas kernels for 0%

profile of v11, /device:TPU:32, one launch (start us, length us, event | category | flops | bytes accessed | tf_op | source)
XLA Modules:
  0.0 174.1 jit_solution(17957483334746032418)
XLA Ops:
  0.0 0.7 pad_maximum_fusion.1
  0.8 21.1 %all_to_all.35 = bf16[4,32,512]{2,1,0:T(8,128)(2,1)S(1)} all-to-all(bf16[4,32,512]{2,1,0:T(8,128)(2,1)S(1)} %broadcast_in_dim.12), channel_id=1, replica_groups=mesh['z2'=4,'z1'=2,'y'=4,'row'=4,'zh'=2,'core'=2] {'z2'}, dimensions={0} | all-to-all | bytes 262144 | tf_op jit(solution)/shard_map/all_to_all | solution.py:12
  21.9 0.9 broadcast_in_dim.13
  22.7 6.6 %all-to-all-start.1 = ((bf16[8,4,16,512]{3,2,1,0:T(8,128)(2,1)}), bf16[8,4,16,512]{3,2,1,0:T(8,128)(2,1)S(1)}, u32[]{:S(2)}, u32[]{:S(2)}) async-start(bf16[8,4,16,512]{3,2,1,0:T(8,128)(2,1)} %broadcast_in_dim.13), calls=%async_computation.1 | async-start | bytes 1048576 | tf_op jit(solution)/shard_map/all_to_all | solution.py:12
  29.3 8.4 %collective-permute-start = (bf16[4,16,512]{2,1,0:T(8,128)(2,1)S(1)}, bf16[4,16,512]{2,1,0:T(8,128)(2,1)S(1)}, u32[]{:S(2)}, u32[]{:S(2)}) collective-permute-start(bf16[4,16,512]{2,1,0:T(8,128)(2,1)S(1)} %get-tuple-element.13), channel_id=1, source_target_pairs={{0,2},{2,0},{1,3},{3,1},{4,6},{6,4},{5,7},{7,5},{8,10},{10,8},{9,1... | collective-permute-start | bytes 196616 | tf_op jit(solution)/shard_map/ppermute | solution.py:20
  37.8 8.2 %collective-permute-done = bf16[4,16,512]{2,1,0:T(8,128)(2,1)S(1)} collective-permute-done((bf16[4,16,512]{2,1,0:T(8,128)(2,1)S(1)}, bf16[4,16,512]{2,1,0:T(8,128)(2,1)S(1)}, u32[]{:S(2)}, u32[]{:S(2)}) %collective-permute-start) | collective-permute-done | bytes 65568 | tf_op jit(solution)/shard_map/ppermute | solution.py:20
  46.0 0.3 broadcast_in_dim.14
  46.3 26.8 %all_to_all.36 = bf16[4,8,4,16,512]{4,3,2,1,0:T(8,128)(2,1)S(1)} all-to-all(bf16[4,8,4,16,512]{4,3,2,1,0:T(8,128)(2,1)S(1)} %broadcast_in_dim.14), channel_id=1, replica_groups=mesh['z2'=4,'z1'=2,'y'=4,'row'=4,'zh'=2,'core'=2] {'row'}, dimensions={0} | all-to-all | bytes 4194304 | tf_op jit(solution)/shard_map/all_to_all | solution.py:12
  73.1 1.1 broadcast_in_dim.15
  74.2 5.7 %all-to-all-start.3 = ((bf16[8,2,4,16,512]{4,3,2,1,0:T(8,128)(2,1)}), bf16[8,2,4,16,512]{4,3,2,1,0:T(8,128)(2,1)S(1)}, u32[]{:S(2)}, u32[]{:S(2)}) async-start(bf16[8,2,4,16,512]{4,3,2,1,0:T(8,128)(2,1)} %broadcast_in_dim.15), calls=%async_computation.3 | async-start | bytes 2097152 | tf_op jit(solution)/shard_map/all_to_all | solution.py:12
  79.9 0.2 copy.34
  80.1 1.9 %copy-done = bf16[2,512,2048]{2,1,0:T(8,128)(2,1)S(1)} copy-done((bf16[2,512,2048]{2,1,0:T(8,128)(2,1)S(1)}, bf16[2,512,2048]{2,1,0:T(8,128)(2,1)}, u32[]{:S(2)}) %copy-start) | copy-done | bytes 4194328
  82.1 2.3 %fusion.1 = bf16[2,512,512]{2,1,0:T(8,128)(2,1)S(1)} fusion(bf16[2048,512,1]{1,0,2:T(8,128)(2,1)S(1)} %bitcast.56, bf16[2,512,2048]{2,1,0:T(8,128)(2,1)S(1)} %copy-done), kind=kOutput, calls=%fused_computation.4 | convolution fusion | flops 2148007936 | bytes 7340032 | tf_op jit(solution)/shard_map/qik,kj->qij/dot_general | solution.py:47
  84.4 3.1 %collective-permute-start.3 = (bf16[2,512,512]{2,1,0:T(8,128)(2,1)S(1)}, bf16[2,512,512]{2,1,0:T(8,128)(2,1)}, u32[]{:S(2)}, u32[]{:S(2)}) collective-permute-start(bf16[2,512,512]{2,1,0:T(8,128)(2,1)S(1)} %fusion.1), channel_id=1, source_target_pairs={{0,12},{4,0},{8,4},{12,8},{1,13},{5,1},{9,5},{13,9},{2,14},{6,2},{... | collective-permute-start | bytes 3145736 | tf_op jit(solution)/shard_map/ppermute | solution.py:56
  87.5 2.8 %collective-permute-start.2 = (bf16[2,512,512]{2,1,0:T(8,128)(2,1)S(1)}, bf16[2,512,512]{2,1,0:T(8,128)(2,1)S(1)}, u32[]{:S(2)}, u32[]{:S(2)}) collective-permute-start(bf16[2,512,512]{2,1,0:T(8,128)(2,1)S(1)} %fusion.1), channel_id=1, source_target_pairs={{0,4},{4,8},{8,12},{12,0},{1,5},{5,9},{9,13},{13,1},{2,6},{6,10},{... | collective-permute-start | bytes 3145736 | tf_op jit(solution)/shard_map/ppermute | solution.py:55
  90.3 1.9 %collective-permute-start.1 = (bf16[8,2,4,16,512]{4,3,2,1,0:T(8,128)(2,1)S(1)}, bf16[8,2,4,16,512]{4,3,2,1,0:T(8,128)(2,1)}, u32[]{:S(2)}, u32[]{:S(2)}) collective-permute-start(bf16[8,2,4,16,512]{4,3,2,1,0:T(8,128)(2,1)S(1)} %all-to-all-done.3), channel_id=1, source_target_pairs={{0,1},{1,0},{2,3},{3,2},{4,5},{5,4},{6,7},{7,6},{8,9},{9,8},{10,11... | collective-permute-start | bytes 3145736 | tf_op jit(solution)/shard_map/ppermute | solution.py:20
  92.3 14.4 %collective-permute-done.3 = bf16[2,512,512]{2,1,0:T(8,128)(2,1)} collective-permute-done((bf16[2,512,512]{2,1,0:T(8,128)(2,1)S(1)}, bf16[2,512,512]{2,1,0:T(8,128)(2,1)}, u32[]{:S(2)}, u32[]{:S(2)}) %collective-permute-start.3) | collective-permute-done | bytes 1048608 | tf_op jit(solution)/shard_map/ppermute | solution.py:56
  106.7 1.1 slice.19
  107.7 3.5 %collective-permute-start.5 = (bf16[2,256,512]{2,1,0:T(8,128)(2,1)S(1)}, bf16[2,256,512]{2,1,0:T(8,128)(2,1)S(1)}, u32[]{:S(2)}, u32[]{:S(2)}) collective-permute-start(bf16[2,256,512]{2,1,0:T(8,128)(2,1)S(1)} %slice.19), channel_id=1, source_target_pairs={{0,12},{4,0},{8,4},{12,8},{1,13},{5,1},{9,5},{13,9},{2,14},{6,2},{... | collective-permute-start | bytes 1572872 | tf_op jit(solution)/shard_map/ppermute | solution.py:59
  111.3 2.3 %collective-permute-start.4 = (bf16[2,256,512]{2,1,0:T(8,128)(2,1)S(1)}, bf16[2,256,512]{2,1,0:T(8,128)(2,1)S(1)}, u32[]{:S(2)}, u32[]{:S(2)}) collective-permute-start(bf16[2,256,512]{2,1,0:T(8,128)(2,1)S(1)} %slice.18), channel_id=1, source_target_pairs={{0,4},{4,8},{8,12},{12,0},{1,5},{5,9},{9,13},{13,1},{2,6},{6,10},{... | collective-permute-start | bytes 1572872 | tf_op jit(solution)/shard_map/ppermute | solution.py:58
  113.7 1.4 broadcast_select_fusion.1
  115.0 0.2 maximum_bitcast_fusion
  115.4 0.8 fusion.6
  116.2 2.0 %fusion.2 = f32[2,512,512]{1,2,0:T(8,128)S(1)} fusion(bf16[2,512,512]{2,1,0:T(8,128)(2,1)} %collective-permute-done.3, bf16[2048,512]{1,0:T(8,128)(2,1)S(1)} %bitcast.49, s32[]{:T(128)S(6)} %select_n.66), kind=kOutput, calls=%fused_computation.7 | convolution fusion | flops 536870912 | bytes 3670020 | tf_op jit(solution)/shard_map/ki,qkj->qij/dot_general | solution.py:64
  118.2 5.4 %collective-permute-done.4 = bf16[2,256,512]{2,1,0:T(8,128)(2,1)S(1)} collective-permute-done((bf16[2,256,512]{2,1,0:T(8,128)(2,1)S(1)}, bf16[2,256,512]{2,1,0:T(8,128)(2,1)S(1)}, u32[]{:S(2)}, u32[]{:S(2)}) %collective-permute-start.4) | collective-permute-done | bytes 524320 | tf_op jit(solution)/shard_map/ppermute | solution.py:58
  123.6 0.5 fusion.15
  124.1 0.8 fusion.4
  124.9 1.0 fusion
  125.9 13.0 %all_to_all.37 = bf16[8,64,512]{2,1,0:T(8,128)(2,1)S(1)} all-to-all(bf16[8,64,512]{2,1,0:T(8,128)(2,1)S(1)} %bitcast.58), channel_id=1, replica_groups=mesh['z2'=4,'z1'=2,'y'=4,'row'=4,'zh'=2,'core'=2] {'y','z1'}, dimensions={0} | all-to-all | bytes 1048576 | tf_op jit(solution)/shard_map/all_to_all | solution.py:74
  139.0 21.1 %all_to_all.38 = bf16[4,64,512]{2,1,0:T(8,128)(2,1)S(1)} all-to-all(bf16[4,64,512]{2,1,0:T(8,128)(2,1)S(1)} %broadcast_in_dim.16), channel_id=1, replica_groups=mesh['z2'=4,'z1'=2,'y'=4,'row'=4,'zh'=2,'core'=2] {'z2'}, dimensions={0} | all-to-all | bytes 524288 | tf_op jit(solution)/shard_map/all_to_all | solution.py:12
  160.2 13.1 %all_to_all.39 = bf16[8,64,512]{2,1,0:T(8,128)(2,1)S(1)} all-to-all(bf16[8,64,512]{2,1,0:T(8,128)(2,1)S(1)} %broadcast_in_dim.17), channel_id=1, replica_groups=mesh['z2'=4,'z1'=2,'y'=4,'row'=4,'zh'=2,'core'=2] {'y','z1'}, dimensions={0} | all-to-all | bytes 1048576 | tf_op jit(solution)/shard_map/all_to_all | solution.py:12
  173.3 0.8 copy.55
  (17 shorter events, 0.5 us)
Async XLA Ops:
  22.7 23.3 %all-to-all-start.1 = ((bf16[8,4,16,512]{3,2,1,0:T(8,128)(2,1)}), bf16[8,4,16,512]{3,2,1,0:T(8,128)(2,1)S(1)}, u32[]{:S(2)}, u32[]{:S(2)}) async-start(bf16[8,4,16,512]{3,2,1,0:T(8,128)(2,1)} %broadcast_in_dim.13), calls=%async_computation.1 | async-start | bytes 1048576 | tf_op jit(solution)/shard_map/all_to_all | solution.py:12
  29.3 16.6 %collective-permute-start = (bf16[4,16,512]{2,1,0:T(8,128)(2,1)S(1)}, bf16[4,16,512]{2,1,0:T(8,128)(2,1)S(1)}, u32[]{:S(2)}, u32[]{:S(2)}) collective-permute-start(bf16[4,16,512]{2,1,0:T(8,128)(2,1)S(1)} %get-tuple-element.13), channel_id=1, source_target_pairs={{0,2},{2,0},{1,3},{3,1},{4,6},{6,4},{5,7},{7,5},{8,10},{10,8},{9,1... | collective-permute-start | bytes 196616 | tf_op jit(solution)/shard_map/ppermute | solution.py:20
  74.2 16.1 %all-to-all-start.3 = ((bf16[8,2,4,16,512]{4,3,2,1,0:T(8,128)(2,1)}), bf16[8,2,4,16,512]{4,3,2,1,0:T(8,128)(2,1)S(1)}, u32[]{:S(2)}, u32[]{:S(2)}) async-start(bf16[8,2,4,16,512]{4,3,2,1,0:T(8,128)(2,1)} %broadcast_in_dim.15), calls=%async_computation.3 | async-start | bytes 2097152 | tf_op jit(solution)/shard_map/all_to_all | solution.py:12
  79.9 2.2 %copy-start = (bf16[2,512,2048]{2,1,0:T(8,128)(2,1)S(1)}, bf16[2,512,2048]{2,1,0:T(8,128)(2,1)}, u32[]{:S(2)}) copy-start(bf16[2,512,2048]{2,1,0:T(8,128)(2,1)} %param.5) | copy-start | bytes 12582916
  84.4 22.2 %collective-permute-start.3 = (bf16[2,512,512]{2,1,0:T(8,128)(2,1)S(1)}, bf16[2,512,512]{2,1,0:T(8,128)(2,1)}, u32[]{:S(2)}, u32[]{:S(2)}) collective-permute-start(bf16[2,512,512]{2,1,0:T(8,128)(2,1)S(1)} %fusion.1), channel_id=1, source_target_pairs={{0,12},{4,0},{8,4},{12,8},{1,13},{5,1},{9,5},{13,9},{2,14},{6,2},{... | collective-permute-start | bytes 3145736 | tf_op jit(solution)/shard_map/ppermute | solution.py:56
  87.5 23.8 %collective-permute-start.2 = (bf16[2,512,512]{2,1,0:T(8,128)(2,1)S(1)}, bf16[2,512,512]{2,1,0:T(8,128)(2,1)S(1)}, u32[]{:S(2)}, u32[]{:S(2)}) collective-permute-start(bf16[2,512,512]{2,1,0:T(8,128)(2,1)S(1)} %fusion.1), channel_id=1, source_target_pairs={{0,4},{4,8},{8,12},{12,0},{1,5},{5,9},{9,13},{13,1},{2,6},{6,10},{... | collective-permute-start | bytes 3145736 | tf_op jit(solution)/shard_map/ppermute | solution.py:55
  90.3 23.4 %collective-permute-start.1 = (bf16[8,2,4,16,512]{4,3,2,1,0:T(8,128)(2,1)S(1)}, bf16[8,2,4,16,512]{4,3,2,1,0:T(8,128)(2,1)}, u32[]{:S(2)}, u32[]{:S(2)}) collective-permute-start(bf16[8,2,4,16,512]{4,3,2,1,0:T(8,128)(2,1)S(1)} %all-to-all-done.3), channel_id=1, source_target_pairs={{0,1},{1,0},{2,3},{3,2},{4,5},{5,4},{6,7},{7,6},{8,9},{9,8},{10,11... | collective-permute-start | bytes 3145736 | tf_op jit(solution)/shard_map/ppermute | solution.py:20
  107.7 17.1 %collective-permute-start.5 = (bf16[2,256,512]{2,1,0:T(8,128)(2,1)S(1)}, bf16[2,256,512]{2,1,0:T(8,128)(2,1)S(1)}, u32[]{:S(2)}, u32[]{:S(2)}) collective-permute-start(bf16[2,256,512]{2,1,0:T(8,128)(2,1)S(1)} %slice.19), channel_id=1, source_target_pairs={{0,12},{4,0},{8,4},{12,8},{1,13},{5,1},{9,5},{13,9},{2,14},{6,2},{... | collective-permute-start | bytes 1572872 | tf_op jit(solution)/shard_map/ppermute | solution.py:59
  111.3 12.3 %collective-permute-start.4 = (bf16[2,256,512]{2,1,0:T(8,128)(2,1)S(1)}, bf16[2,256,512]{2,1,0:T(8,128)(2,1)S(1)}, u32[]{:S(2)}, u32[]{:S(2)}) collective-permute-start(bf16[2,256,512]{2,1,0:T(8,128)(2,1)S(1)} %slice.18), channel_id=1, source_target_pairs={{0,4},{4,8},{8,12},{12,0},{1,5},{5,9},{9,13},{13,1},{2,6},{6,10},{... | collective-permute-start | bytes 1572872 | tf_op jit(solution)/shard_map/ppermute | solution.py:58

commit v12 on v10

--- a/solution.py
+++ b/solution.py
@@ -40,9 +40,9 @@
         slabs = spread(jnp.concatenate([g_minus, g_plus.T]), line, zl)
         minus, plus = slabs[:, :depth], slabs[:, depth:]
         theirs = partner(plus, "zh")
-        minus = spread(minus, ("y", "row"), y * row)
+        minus = spread(minus, ("row", "y"), y * row)
         minus, plus, theirs = lax.optimization_barrier((minus, plus, theirs))
-        minus = minus.reshape(y, row, zl, depth, cols).transpose(2, 0, 1, 3, 4).reshape(n, cols)
+        minus = minus.reshape(row, y, zl, depth, cols).transpose(2, 1, 0, 3, 4).reshape(n, cols)
         half = jnp.einsum("qik,kj->qij", coulomb, minus, preferred_element_type=F32).astype(BF)
         half = with_layout_constraint(half, Layout((0, 1, 2)))
 
@@ -70,10 +70,10 @@
         total = jnp.sum(pair * half.astype(F32), axis=0)
 
         parts = y * z1
-        total = lax.all_to_all(total.astype(BF).reshape(parts, rows // parts, cols), ("y", "z1"), 0, 0)
+        total = lax.all_to_all(total.astype(BF).reshape(parts, rows // parts, cols), ("z1", "y"), 0, 0)
         total = jnp.sum(total.astype(F32), axis=0).astype(BF)
         total = -jnp.sum(spread(total, "z2", z2).astype(F32), axis=0)
-        return spread(total.astype(BF), ("y", "z1"), parts).reshape(rows, cols)
+        return spread(total.astype(BF), ("z1", "y"), parts).reshape(rows, cols)
 
     in_specs = (
         P("row", ("z2", "z1", "y", "zh", "core")),

time: 167 us -> 163 us (0.976)
  the two profiles are of different devices: /device:TPU:4 before, /device:TPU:8 now
where the time goes in v12:
time: 163 us; the launch traced here: 162 us
  blocking collectives  73.4 us (45%)
  starting transfers between devices  36.5 us (22%)
  waiting for transfers between devices  35.2 us (22%)
  matrix products  7.27 us (4%)
  local copies, waits for them, and re-layouts  7.14 us (4%)
  other arithmetic  2.47 us (2%)
    all_to_all x3, blocking collectives, spread(): lax.all_to_all(jnp.broadcast_to(block[None], (count,) + block.shape), axe...  61.2 us
    ppermute x1, waiting for transfers between devices, local(): right = lax.ppermute(half, 'row', shift(row, -1))  15 us
    ppermute x2, waiting for transfers between devices, partner(): return lax.ppermute(block, axis, shift(2, 1))  14.4 us
    all_to_all x2, starting transfers between devices, spread(): lax.all_to_all(jnp.broadcast_to(block[None], (count,) + block.shape), axe...  12.3 us
    all_to_all x1, blocking collectives, local(): lax.all_to_all(total.astype(BF).reshape(parts, rows // parts, cols), ('z1...  12.3 us
    ppermute x2, starting transfers between devices, partner(): return lax.ppermute(block, axis, shift(2, 1))  10.1 us
    ppermute x1, waiting for transfers between devices, local(): top = lax.ppermute(left[:, :cut], 'row', shift(row, 1))  5.81 us
    ppermute x1, starting transfers between devices, local(): bottom = lax.ppermute(right[:, cut:], 'row', shift(row, -1))  5.71 us
  transfers between devices with their start and end apart: 8, of which 3 were waited for; matrix products, arithmetic and copies ran while one was open for 6% of the time, Pallas kernels for 0%

profile of v12, /device:TPU:8, one launch (start us, length us, event | category | flops | bytes accessed | tf_op | source)
XLA Modules:
  0.0 162.3 jit_solution(2695354631712578028)
XLA Ops:
  0.0 0.7 pad_maximum_fusion.1
  0.8 29.0 %all_to_all.30 = bf16[8,32,512]{2,1,0:T(8,128)(2,1)S(1)} all-to-all(bf16[8,32,512]{2,1,0:T(8,128)(2,1)S(1)} %broadcast_in_dim.10), channel_id=1, replica_groups=mesh['z2'=4,'z1'=2,'y'=4,'row'=4,'zh'=2,'core'=2] {'z2','z1'}, dimensions={0} | all-to-all | bytes 524288 | tf_op jit(solution)/shard_map/all_to_all | solution.py:12
  29.8 1.6 broadcast_in_dim.11
  31.4 7.4 %all-to-all-start.1 = ((bf16[16,8,16,512]{3,2,1,0:T(8,128)(2,1)}), bf16[16,8,16,512]{3,2,1,0:T(8,128)(2,1)S(1)}, u32[]{:S(2)}, u32[]{:S(2)}) async-start(bf16[16,8,16,512]{3,2,1,0:T(8,128)(2,1)} %broadcast_in_dim.11), calls=%async_computation.1 | async-start | bytes 4194304 | tf_op jit(solution)/shard_map/all_to_all | solution.py:12
  38.8 8.2 %collective-permute-start = (bf16[8,16,512]{2,1,0:T(8,128)(2,1)S(1)}, bf16[8,16,512]{2,1,0:T(8,128)(2,1)S(1)}, u32[]{:S(2)}, u32[]{:S(2)}) collective-permute-start(bf16[8,16,512]{2,1,0:T(8,128)(2,1)S(1)} %get-tuple-element.9), channel_id=1, source_target_pairs={{0,2},{2,0},{1,3},{3,1},{4,6},{6,4},{5,7},{7,5},{8,10},{10,8},{9,1... | collective-permute-start | bytes 393224 | tf_op jit(solution)/shard_map/ppermute | solution.py:20
  47.0 14.4 %collective-permute-done = bf16[8,16,512]{2,1,0:T(8,128)(2,1)S(1)} collective-permute-done((bf16[8,16,512]{2,1,0:T(8,128)(2,1)S(1)}, bf16[8,16,512]{2,1,0:T(8,128)(2,1)S(1)}, u32[]{:S(2)}, u32[]{:S(2)}) %collective-permute-start) | collective-permute-done | bytes 131104 | tf_op jit(solution)/shard_map/ppermute | solution.py:20
  61.5 1.2 broadcast_in_dim.12
  62.6 4.9 %all-to-all-start.2 = ((bf16[4,2,8,16,512]{4,3,1,2,0:T(8,128)(2,1)}), bf16[4,2,8,16,512]{4,3,1,2,0:T(8,128)(2,1)S(1)}, u32[]{:S(2)}, u32[]{:S(2)}) async-start(bf16[4,2,8,16,512]{4,3,1,2,0:T(8,128)(2,1)} %broadcast_in_dim.12), calls=%async_computation.2 | async-start | bytes 2097152 | tf_op jit(solution)/shard_map/all_to_all | solution.py:12
  67.5 0.2 copy.50
  67.8 1.9 %copy-done = bf16[2,512,2048]{2,1,0:T(8,128)(2,1)S(1)} copy-done((bf16[2,512,2048]{2,1,0:T(8,128)(2,1)S(1)}, bf16[2,512,2048]{2,1,0:T(8,128)(2,1)}, u32[]{:S(2)}) %copy-start) | copy-done | bytes 4194328
  69.7 2.3 %fusion.1 = bf16[2,512,512]{2,1,0:T(8,128)(2,1)S(1)} fusion(bf16[2048,512,1]{1,0,2:T(8,128)(2,1)S(1)} %bitcast.56, bf16[2,512,2048]{2,1,0:T(8,128)(2,1)S(1)} %copy-done), kind=kOutput, calls=%fused_computation.4 | convolution fusion | flops 2148007936 | bytes 7340032 | tf_op jit(solution)/shard_map/qik,kj->qij/dot_general | solution.py:46
  72.1 4.5 %collective-permute-start.3 = (bf16[2,512,512]{2,1,0:T(8,128)(2,1)S(1)}, bf16[2,512,512]{2,1,0:T(8,128)(2,1)}, u32[]{:S(2)}, u32[]{:S(2)}) collective-permute-start(bf16[2,512,512]{2,1,0:T(8,128)(2,1)S(1)} %fusion.1), channel_id=1, source_target_pairs={{0,12},{4,0},{8,4},{12,8},{1,13},{5,1},{9,5},{13,9},{2,14},{6,2},{... | collective-permute-start | bytes 3145736 | tf_op jit(solution)/shard_map/ppermute | solution.py:55
  76.5 1.9 %collective-permute-start.2 = (bf16[2,512,512]{2,1,0:T(8,128)(2,1)S(1)}, bf16[2,512,512]{2,1,0:T(8,128)(2,1)S(1)}, u32[]{:S(2)}, u32[]{:S(2)}) collective-permute-start(bf16[2,512,512]{2,1,0:T(8,128)(2,1)S(1)} %fusion.1), channel_id=1, source_target_pairs={{0,4},{4,8},{8,12},{12,0},{1,5},{5,9},{9,13},{13,1},{2,6},{6,10},{... | collective-permute-start | bytes 3145736 | tf_op jit(solution)/shard_map/ppermute | solution.py:54
  78.5 1.9 %collective-permute-start.1 = (bf16[4,2,8,16,512]{4,3,1,2,0:T(8,128)(2,1)S(1)}, bf16[4,2,8,16,512]{4,3,1,2,0:T(8,128)(2,1)}, u32[]{:S(2)}, u32[]{:S(2)}) collective-permute-start(bf16[4,2,8,16,512]{4,3,1,2,0:T(8,128)(2,1)S(1)} %all-to-all-done.2), channel_id=1, source_target_pairs={{0,1},{1,0},{2,3},{3,2},{4,5},{5,4},{6,7},{7,6},{8,9},{9,8},{10,11... | collective-permute-start | bytes 3145736 | tf_op jit(solution)/shard_map/ppermute | solution.py:20
  80.4 15.0 %collective-permute-done.3 = bf16[2,512,512]{2,1,0:T(8,128)(2,1)} collective-permute-done((bf16[2,512,512]{2,1,0:T(8,128)(2,1)S(1)}, bf16[2,512,512]{2,1,0:T(8,128)(2,1)}, u32[]{:S(2)}, u32[]{:S(2)}) %collective-permute-start.3) | collective-permute-done | bytes 1048608 | tf_op jit(solution)/shard_map/ppermute | solution.py:55
  95.5 1.1 slice.19
  96.5 5.7 %collective-permute-start.5 = (bf16[2,256,512]{2,1,0:T(8,128)(2,1)S(1)}, bf16[2,256,512]{2,1,0:T(8,128)(2,1)S(1)}, u32[]{:S(2)}, u32[]{:S(2)}) collective-permute-start(bf16[2,256,512]{2,1,0:T(8,128)(2,1)S(1)} %slice.19), channel_id=1, source_target_pairs={{0,12},{4,0},{8,4},{12,8},{1,13},{5,1},{9,5},{13,9},{2,14},{6,2},{... | collective-permute-start | bytes 1572872 | tf_op jit(solution)/shard_map/ppermute | solution.py:58
  102.3 1.9 %collective-permute-start.4 = (bf16[2,256,512]{2,1,0:T(8,128)(2,1)S(1)}, bf16[2,256,512]{2,1,0:T(8,128)(2,1)S(1)}, u32[]{:S(2)}, u32[]{:S(2)}) collective-permute-start(bf16[2,256,512]{2,1,0:T(8,128)(2,1)S(1)} %slice.18), channel_id=1, source_target_pairs={{0,4},{4,8},{8,12},{12,0},{1,5},{5,9},{9,13},{13,1},{2,6},{6,10},{... | collective-permute-start | bytes 1572872 | tf_op jit(solution)/shard_map/ppermute | solution.py:57
  104.2 1.4 select_bitcast_fusion.1
  105.6 0.2 maximum_bitcast_fusion
  105.8 0.2 copy.52
  106.0 0.8 fusion.6
  106.8 2.0 %fusion.2 = f32[2,512,512]{1,2,0:T(8,128)S(1)} fusion(bf16[2,512,512]{2,1,0:T(8,128)(2,1)} %collective-permute-done.3, bf16[2048,512]{1,0:T(8,128)(2,1)S(1)} %bitcast.52, s32[]{:T(128)S(6)} %select_n.66), kind=kOutput, calls=%fused_computation.7 | convolution fusion | flops 536870912 | bytes 3670020 | tf_op jit(solution)/shard_map/ki,qkj->qij/dot_general | solution.py:63
  108.8 5.8 %collective-permute-done.4 = bf16[2,256,512]{2,1,0:T(8,128)(2,1)S(1)} collective-permute-done((bf16[2,256,512]{2,1,0:T(8,128)(2,1)S(1)}, bf16[2,256,512]{2,1,0:T(8,128)(2,1)S(1)}, u32[]{:S(2)}, u32[]{:S(2)}) %collective-permute-start.4) | collective-permute-done | bytes 524320 | tf_op jit(solution)/shard_map/ppermute | solution.py:57
  114.6 0.5 fusion.15
  115.1 0.8 fusion.4
  115.9 1.0 fusion
  116.8 12.3 %all_to_all.31 = bf16[8,64,512]{2,1,0:T(8,128)(2,1)S(1)} all-to-all(bf16[8,64,512]{2,1,0:T(8,128)(2,1)S(1)} %bitcast.58), channel_id=1, replica_groups=mesh['z2'=4,'z1'=2,'y'=4,'row'=4,'zh'=2,'core'=2] {'z1','y'}, dimensions={0} | all-to-all | bytes 1048576 | tf_op jit(solution)/shard_map/all_to_all | solution.py:73
  129.1 0.1 reduce_sum.31
  129.2 21.3 %all_to_all.32 = bf16[4,64,512]{2,1,0:T(8,128)(2,1)S(1)} all-to-all(bf16[4,64,512]{2,1,0:T(8,128)(2,1)S(1)} %broadcast_in_dim.13), channel_id=1, replica_groups=mesh['z2'=4,'z1'=2,'y'=4,'row'=4,'zh'=2,'core'=2] {'z2'}, dimensions={0} | all-to-all | bytes 524288 | tf_op jit(solution)/shard_map/all_to_all | solution.py:12
  150.6 10.9 %all_to_all.33 = bf16[8,64,512]{2,1,0:T(8,128)(2,1)S(1)} all-to-all(bf16[8,64,512]{2,1,0:T(8,128)(2,1)S(1)} %broadcast_in_dim.14), channel_id=1, replica_groups=mesh['z2'=4,'z1'=2,'y'=4,'row'=4,'zh'=2,'core'=2] {'z1','y'}, dimensions={0} | all-to-all | bytes 1048576 | tf_op jit(solution)/shard_map/all_to_all | solution.py:12
  161.5 0.8 copy.72
  (16 shorter events, 0.3 us)
Async XLA Ops:
  31.4 30.0 %all-to-all-start.1 = ((bf16[16,8,16,512]{3,2,1,0:T(8,128)(2,1)}), bf16[16,8,16,512]{3,2,1,0:T(8,128)(2,1)S(1)}, u32[]{:S(2)}, u32[]{:S(2)}) async-start(bf16[16,8,16,512]{3,2,1,0:T(8,128)(2,1)} %broadcast_in_dim.11), calls=%async_computation.1 | async-start | bytes 4194304 | tf_op jit(solution)/shard_map/all_to_all | solution.py:12
  38.8 22.6 %collective-permute-start = (bf16[8,16,512]{2,1,0:T(8,128)(2,1)S(1)}, bf16[8,16,512]{2,1,0:T(8,128)(2,1)S(1)}, u32[]{:S(2)}, u32[]{:S(2)}) collective-permute-start(bf16[8,16,512]{2,1,0:T(8,128)(2,1)S(1)} %get-tuple-element.9), channel_id=1, source_target_pairs={{0,2},{2,0},{1,3},{3,1},{4,6},{6,4},{5,7},{7,5},{8,10},{10,8},{9,1... | collective-permute-start | bytes 393224 | tf_op jit(solution)/shard_map/ppermute | solution.py:20
  62.6 15.8 %all-to-all-start.2 = ((bf16[4,2,8,16,512]{4,3,1,2,0:T(8,128)(2,1)}), bf16[4,2,8,16,512]{4,3,1,2,0:T(8,128)(2,1)S(1)}, u32[]{:S(2)}, u32[]{:S(2)}) async-start(bf16[4,2,8,16,512]{4,3,1,2,0:T(8,128)(2,1)} %broadcast_in_dim.12), calls=%async_computation.2 | async-start | bytes 2097152 | tf_op jit(solution)/shard_map/all_to_all | solution.py:12
  67.5 2.2 %copy-start = (bf16[2,512,2048]{2,1,0:T(8,128)(2,1)S(1)}, bf16[2,512,2048]{2,1,0:T(8,128)(2,1)}, u32[]{:S(2)}) copy-start(bf16[2,512,2048]{2,1,0:T(8,128)(2,1)} %param.5) | copy-start | bytes 12582916
  72.1 23.4 %collective-permute-start.3 = (bf16[2,512,512]{2,1,0:T(8,128)(2,1)S(1)}, bf16[2,512,512]{2,1,0:T(8,128)(2,1)}, u32[]{:S(2)}, u32[]{:S(2)}) collective-permute-start(bf16[2,512,512]{2,1,0:T(8,128)(2,1)S(1)} %fusion.1), channel_id=1, source_target_pairs={{0,12},{4,0},{8,4},{12,8},{1,13},{5,1},{9,5},{13,9},{2,14},{6,2},{... | collective-permute-start | bytes 3145736 | tf_op jit(solution)/shard_map/ppermute | solution.py:55
  76.5 25.7 %collective-permute-start.2 = (bf16[2,512,512]{2,1,0:T(8,128)(2,1)S(1)}, bf16[2,512,512]{2,1,0:T(8,128)(2,1)S(1)}, u32[]{:S(2)}, u32[]{:S(2)}) collective-permute-start(bf16[2,512,512]{2,1,0:T(8,128)(2,1)S(1)} %fusion.1), channel_id=1, source_target_pairs={{0,4},{4,8},{8,12},{12,0},{1,5},{5,9},{9,13},{13,1},{2,6},{6,10},{... | collective-permute-start | bytes 3145736 | tf_op jit(solution)/shard_map/ppermute | solution.py:54
  78.5 25.8 %collective-permute-start.1 = (bf16[4,2,8,16,512]{4,3,1,2,0:T(8,128)(2,1)S(1)}, bf16[4,2,8,16,512]{4,3,1,2,0:T(8,128)(2,1)}, u32[]{:S(2)}, u32[]{:S(2)}) collective-permute-start(bf16[4,2,8,16,512]{4,3,1,2,0:T(8,128)(2,1)S(1)} %all-to-all-done.2), channel_id=1, source_target_pairs={{0,1},{1,0},{2,3},{3,2},{4,5},{5,4},{6,7},{7,6},{8,9},{9,8},{10,11... | collective-permute-start | bytes 3145736 | tf_op jit(solution)/shard_map/ppermute | solution.py:20
  96.5 19.3 %collective-permute-start.5 = (bf16[2,256,512]{2,1,0:T(8,128)(2,1)S(1)}, bf16[2,256,512]{2,1,0:T(8,128)(2,1)S(1)}, u32[]{:S(2)}, u32[]{:S(2)}) collective-permute-start(bf16[2,256,512]{2,1,0:T(8,128)(2,1)S(1)} %slice.19), channel_id=1, source_target_pairs={{0,12},{4,0},{8,4},{12,8},{1,13},{5,1},{9,5},{13,9},{2,14},{6,2},{... | collective-permute-start | bytes 1572872 | tf_op jit(solution)/shard_map/ppermute | solution.py:58
  102.3 12.3 %collective-permute-start.4 = (bf16[2,256,512]{2,1,0:T(8,128)(2,1)S(1)}, bf16[2,256,512]{2,1,0:T(8,128)(2,1)S(1)}, u32[]{:S(2)}, u32[]{:S(2)}) collective-permute-start(bf16[2,256,512]{2,1,0:T(8,128)(2,1)S(1)} %slice.18), channel_id=1, source_target_pairs={{0,4},{4,8},{8,12},{12,0},{1,5},{5,9},{9,13},{13,1},{2,6},{6,10},{... | collective-permute-start | bytes 1572872 | tf_op jit(solution)/shard_map/ppermute | solution.py:57

commit v13 on v12

--- a/solution.py
+++ b/solution.py
@@ -53,20 +53,17 @@
         me = lax.axis_index("row")
         left = lax.ppermute(half, "row", shift(row, 1))
         right = lax.ppermute(half, "row", shift(row, -1))
-        cut = rows // 2
-        top = lax.ppermute(left[:, :cut], "row", shift(row, 1))
-        bottom = lax.ppermute(right[:, cut:], "row", shift(row, -1))
+        far0 = lax.ppermute(left[:1], "row", shift(row, 1))
+        far1 = lax.ppermute(right[1:], "row", shift(row, -1))
 
-        def part(strip, owner, start):
-            size = strip.shape[1]
-            block = lax.dynamic_slice_in_dim(plus, owner * rows + start, size, axis=0)
+        def part(strip, owner):
+            block = lax.dynamic_slice_in_dim(plus, owner * rows, rows, axis=0)
             return jnp.einsum("ki,qkj->qij", block, strip, preferred_element_type=F32)
 
-        pair = part(half, me, 0)
-        pair += part(left, (me + row - 1) % row, 0)
-        pair += part(right, (me + 1) % row, 0)
-        pair += part(top, (me + 2) % row, 0)
-        pair += part(bottom, (me + 2) % row, cut)
+        pair = part(half, me)
+        pair += part(left, (me + row - 1) % row)
+        pair += part(right, (me + 1) % row)
+        pair += jnp.concatenate([part(far0, (me + 2) % row), part(far1, (me + 2) % row)])
         total = jnp.sum(pair * half.astype(F32), axis=0)
 
         parts = y * z1

time: 163 us -> 165 us (1.012)
  transfers between devices with their start and end apart: 8 -> 8, of which waited for: 3 -> 4; matrix products, arithmetic and copies ran while one was open for 6% -> 5% of each run, Pallas kernels for 0% -> 0%
where the time goes in v13:
time: 165 us; the launch traced here: 164 us
  blocking collectives  73.4 us (44%)
  starting transfers between devices  36.3 us (22%)
  waiting for transfers between devices  35.7 us (22%)
  matrix products  8.23 us (5%)
  local copies, waits for them, and re-layouts  7.94 us (5%)
  other arithmetic  2.47 us (1%)
    all_to_all x3, blocking collectives, spread(): lax.all_to_all(jnp.broadcast_to(block[None], (count,) + block.shape), axe...  61.2 us
    ppermute x1, waiting for transfers between devices, local(): right = lax.ppermute(half, 'row', shift(row, -1))  15.1 us
    ppermute x2, waiting for transfers between devices, partner(): return lax.ppermute(block, axis, shift(2, 1))  14.4 us
    all_to_all x2, starting transfers between devices, spread(): lax.all_to_all(jnp.broadcast_to(block[None], (count,) + block.shape), axe...  12.3 us
    all_to_all x1, blocking collectives, local(): lax.all_to_all(total.astype(BF).reshape(parts, rows // parts, cols), ('z1...  12.3 us
    ppermute x2, starting transfers between devices, partner(): return lax.ppermute(block, axis, shift(2, 1))  10.1 us
    dot_general x5, matrix products, part(): return jnp.einsum('ki,qkj->qij', block, strip, preferred_element_type=F32)  5.91 us
    ppermute x1, starting transfers between devices, local(): far1 = lax.ppermute(right[1:], 'row', shift(row, -1))  5.59 us
  transfers between devices with their start and end apart: 8, of which 4 were waited for; matrix products, arithmetic and copies ran while one was open for 5% of the time, Pallas kernels for 0%

profile of v13, /device:TPU:8, one launch (start us, length us, event | category | flops | bytes accessed | tf_op | source)
XLA Modules:
  0.0 164.4 jit_solution(14930502021621225946)
XLA Ops:
  0.0 0.7 pad_maximum_fusion.1
  0.8 29.0 %all_to_all.30 = bf16[8,32,512]{2,1,0:T(8,128)(2,1)S(1)} all-to-all(bf16[8,32,512]{2,1,0:T(8,128)(2,1)S(1)} %broadcast_in_dim.10), channel_id=1, replica_groups=mesh['z2'=4,'z1'=2,'y'=4,'row'=4,'zh'=2,'core'=2] {'z2','z1'}, dimensions={0} | all-to-all | bytes 524288 | tf_op jit(solution)/shard_map/all_to_all | solution.py:12
  29.8 1.6 broadcast_in_dim.11
  31.4 7.4 %all-to-all-start.1 = ((bf16[16,8,16,512]{3,2,1,0:T(8,128)(2,1)}), bf16[16,8,16,512]{3,2,1,0:T(8,128)(2,1)S(1)}, u32[]{:S(2)}, u32[]{:S(2)}) async-start(bf16[16,8,16,512]{3,2,1,0:T(8,128)(2,1)} %broadcast_in_dim.11), calls=%async_computation.1 | async-start | bytes 4194304 | tf_op jit(solution)/shard_map/all_to_all | solution.py:12
  38.8 8.2 %collective-permute-start = (bf16[8,16,512]{2,1,0:T(8,128)(2,1)S(1)}, bf16[8,16,512]{2,1,0:T(8,128)(2,1)S(1)}, u32[]{:S(2)}, u32[]{:S(2)}) collective-permute-start(bf16[8,16,512]{2,1,0:T(8,128)(2,1)S(1)} %get-tuple-element.9), channel_id=1, source_target_pairs={{0,2},{2,0},{1,3},{3,1},{4,6},{6,4},{5,7},{7,5},{8,10},{10,8},{9,1... | collective-permute-start | bytes 393224 | tf_op jit(solution)/shard_map/ppermute | solution.py:20
  47.0 14.4 %collective-permute-done = bf16[8,16,512]{2,1,0:T(8,128)(2,1)S(1)} collective-permute-done((bf16[8,16,512]{2,1,0:T(8,128)(2,1)S(1)}, bf16[8,16,512]{2,1,0:T(8,128)(2,1)S(1)}, u32[]{:S(2)}, u32[]{:S(2)}) %collective-permute-start) | collective-permute-done | bytes 131104 | tf_op jit(solution)/shard_map/ppermute | solution.py:20
  61.5 1.2 broadcast_in_dim.12
  62.6 4.9 %all-to-all-start.2 = ((bf16[4,2,8,16,512]{4,3,1,2,0:T(8,128)(2,1)}), bf16[4,2,8,16,512]{4,3,1,2,0:T(8,128)(2,1)S(1)}, u32[]{:S(2)}, u32[]{:S(2)}) async-start(bf16[4,2,8,16,512]{4,3,1,2,0:T(8,128)(2,1)} %broadcast_in_dim.12), calls=%async_computation.2 | async-start | bytes 2097152 | tf_op jit(solution)/shard_map/all_to_all | solution.py:12
  67.5 0.2 copy.42
  67.8 1.9 %copy-done = bf16[2,512,2048]{2,1,0:T(8,128)(2,1)S(1)} copy-done((bf16[2,512,2048]{2,1,0:T(8,128)(2,1)S(1)}, bf16[2,512,2048]{2,1,0:T(8,128)(2,1)}, u32[]{:S(2)}) %copy-start) | copy-done | bytes 4194328
  69.7 2.3 %fusion.2 = bf16[2,512,512]{2,1,0:T(8,128)(2,1)S(1)} fusion(bf16[2048,512,1]{1,0,2:T(8,128)(2,1)S(1)} %bitcast.59, bf16[2,512,2048]{2,1,0:T(8,128)(2,1)S(1)} %copy-done), kind=kOutput, calls=%fused_computation.5 | convolution fusion | flops 2148007936 | bytes 7340032 | tf_op jit(solution)/shard_map/qik,kj->qij/dot_general | solution.py:46
  72.1 4.5 %collective-permute-start.3 = (bf16[2,512,512]{2,1,0:T(8,128)(2,1)S(1)}, bf16[2,512,512]{2,1,0:T(8,128)(2,1)S(1)}, u32[]{:S(2)}, u32[]{:S(2)}) collective-permute-start(bf16[2,512,512]{2,1,0:T(8,128)(2,1)S(1)} %fusion.2), channel_id=1, source_target_pairs={{0,12},{4,0},{8,4},{12,8},{1,13},{5,1},{9,5},{13,9},{2,14},{6,2},{... | collective-permute-start | bytes 3145736 | tf_op jit(solution)/shard_map/ppermute | solution.py:55
  76.5 1.9 %collective-permute-start.2 = (bf16[2,512,512]{2,1,0:T(8,128)(2,1)S(1)}, bf16[2,512,512]{2,1,0:T(8,128)(2,1)}, u32[]{:S(2)}, u32[]{:S(2)}) collective-permute-start(bf16[2,512,512]{2,1,0:T(8,128)(2,1)S(1)} %fusion.2), channel_id=1, source_target_pairs={{0,4},{4,8},{8,12},{12,0},{1,5},{5,9},{9,13},{13,1},{2,6},{6,10},{... | collective-permute-start | bytes 3145736 | tf_op jit(solution)/shard_map/ppermute | solution.py:54
  78.5 1.9 %collective-permute-start.1 = (bf16[4,2,8,16,512]{4,3,1,2,0:T(8,128)(2,1)S(1)}, bf16[4,2,8,16,512]{4,3,1,2,0:T(8,128)(2,1)}, u32[]{:S(2)}, u32[]{:S(2)}) collective-permute-start(bf16[4,2,8,16,512]{4,3,1,2,0:T(8,128)(2,1)S(1)} %all-to-all-done.2), channel_id=1, source_target_pairs={{0,1},{1,0},{2,3},{3,2},{4,5},{5,4},{6,7},{7,6},{8,9},{9,8},{10,11... | collective-permute-start | bytes 3145736 | tf_op jit(solution)/shard_map/ppermute | solution.py:20
  80.4 15.1 %collective-permute-done.3 = bf16[2,512,512]{2,1,0:T(8,128)(2,1)S(1)} collective-permute-done((bf16[2,512,512]{2,1,0:T(8,128)(2,1)S(1)}, bf16[2,512,512]{2,1,0:T(8,128)(2,1)S(1)}, u32[]{:S(2)}, u32[]{:S(2)}) %collective-permute-start.3) | collective-permute-done | bytes 1048608 | tf_op jit(solution)/shard_map/ppermute | solution.py:55
  95.5 0.8 slice.19
  96.3 5.6 %collective-permute-start.5 = (bf16[1,512,512]{2,1,0:T(8,128)(2,1)}, bf16[1,512,512]{2,1,0:T(8,128)(2,1)}, u32[]{:S(2)}, u32[]{:S(2)}) collective-permute-start(bf16[1,512,512]{2,1,0:T(8,128)(2,1)} %slice.19), channel_id=1, source_target_pairs={{0,12},{4,0},{8,4},{12,8},{1,13},{5,1},{9,5},{13,9},{2,14},{6,2},{... | collective-permute-start | bytes 1572872 | tf_op jit(solution)/shard_map/ppermute | solution.py:57
  101.9 1.1 slice.18
  103.0 1.9 %collective-permute-start.4 = (bf16[1,512,512]{2,1,0:T(8,128)(2,1)S(1)}, bf16[1,512,512]{2,1,0:T(8,128)(2,1)S(1)}, u32[]{:S(2)}, u32[]{:S(2)}) collective-permute-start(bf16[1,512,512]{2,1,0:T(8,128)(2,1)S(1)} %slice.18), channel_id=1, source_target_pairs={{0,4},{4,8},{8,12},{12,0},{1,5},{5,9},{9,13},{13,1},{2,6},{6,10},{... | collective-permute-start | bytes 1572872 | tf_op jit(solution)/shard_map/ppermute | solution.py:56
  105.0 1.4 select_bitcast_fusion.1
  106.3 0.2 maximum_bitcast_fusion
  106.7 2.2 %collective-permute-done.5 = bf16[1,512,512]{2,1,0:T(8,128)(2,1)} collective-permute-done((bf16[1,512,512]{2,1,0:T(8,128)(2,1)}, bf16[1,512,512]{2,1,0:T(8,128)(2,1)}, u32[]{:S(2)}, u32[]{:S(2)}) %collective-permute-start.5) | collective-permute-done | bytes 524320 | tf_op jit(solution)/shard_map/ppermute | solution.py:57
  109.0 1.5 convolution_bitcast_fusion
  110.5 0.8 fusion.8
  111.3 4.0 %collective-permute-done.4 = bf16[1,512,512]{2,1,0:T(8,128)(2,1)S(1)} collective-permute-done((bf16[1,512,512]{2,1,0:T(8,128)(2,1)S(1)}, bf16[1,512,512]{2,1,0:T(8,128)(2,1)S(1)}, u32[]{:S(2)}, u32[]{:S(2)}) %collective-permute-start.4) | collective-permute-done | bytes 524320 | tf_op jit(solution)/shard_map/ppermute | solution.py:56
  115.3 0.5 convolution_bitcast_fusion.1
  115.8 2.0 %fusion.6 = f32[2,512,512]{1,2,0:T(8,128)S(1)} fusion(bf16[2,512,512]{2,1,0:T(8,128)(2,1)} %collective-permute-done.2, bf16[2048,512]{1,0:T(8,128)(2,1)S(1)} %bitcast.55, s32[]{:T(128)S(6)} %select_n.62), kind=kOutput, calls=%fused_computation.13 | convolution fusion | flops 536870912 | bytes 3670020 | tf_op jit(solution)/shard_map/ki,qkj->qij/dot_general | solution.py:61
  117.8 1.2 fusion.1
  119.0 12.3 %all_to_all.31 = bf16[8,64,512]{2,1,0:T(8,128)(2,1)S(1)} all-to-all(bf16[8,64,512]{2,1,0:T(8,128)(2,1)S(1)} %bitcast.58), channel_id=1, replica_groups=mesh['z2'=4,'z1'=2,'y'=4,'row'=4,'zh'=2,'core'=2] {'z1','y'}, dimensions={0} | all-to-all | bytes 1048576 | tf_op jit(solution)/shard_map/all_to_all | solution.py:70
  131.3 21.3 %all_to_all.32 = bf16[4,64,512]{2,1,0:T(8,128)(2,1)S(1)} all-to-all(bf16[4,64,512]{2,1,0:T(8,128)(2,1)S(1)} %broadcast_in_dim.13), channel_id=1, replica_groups=mesh['z2'=4,'z1'=2,'y'=4,'row'=4,'zh'=2,'core'=2] {'z2'}, dimensions={0} | all-to-all | bytes 524288 | tf_op jit(solution)/shard_map/all_to_all | solution.py:12
  152.7 10.9 %all_to_all.33 = bf16[8,64,512]{2,1,0:T(8,128)(2,1)S(1)} all-to-all(bf16[8,64,512]{2,1,0:T(8,128)(2,1)S(1)} %broadcast_in_dim.14), channel_id=1, replica_groups=mesh['z2'=4,'z1'=2,'y'=4,'row'=4,'zh'=2,'core'=2] {'z1','y'}, dimensions={0} | all-to-all | bytes 1048576 | tf_op jit(solution)/shard_map/all_to_all | solution.py:12
  163.6 0.8 copy.60
  (16 shorter events, 0.5 us)
Async XLA Ops:
  31.4 30.0 %all-to-all-start.1 = ((bf16[16,8,16,512]{3,2,1,0:T(8,128)(2,1)}), bf16[16,8,16,512]{3,2,1,0:T(8,128)(2,1)S(1)}, u32[]{:S(2)}, u32[]{:S(2)}) async-start(bf16[16,8,16,512]{3,2,1,0:T(8,128)(2,1)} %broadcast_in_dim.11), calls=%async_computation.1 | async-start | bytes 4194304 | tf_op jit(solution)/shard_map/all_to_all | solution.py:12
  38.8 22.6 %collective-permute-start = (bf16[8,16,512]{2,1,0:T(8,128)(2,1)S(1)}, bf16[8,16,512]{2,1,0:T(8,128)(2,1)S(1)}, u32[]{:S(2)}, u32[]{:S(2)}) collective-permute-start(bf16[8,16,512]{2,1,0:T(8,128)(2,1)S(1)} %get-tuple-element.9), channel_id=1, source_target_pairs={{0,2},{2,0},{1,3},{3,1},{4,6},{6,4},{5,7},{7,5},{8,10},{10,8},{9,1... | collective-permute-start | bytes 393224 | tf_op jit(solution)/shard_map/ppermute | solution.py:20
  62.6 15.8 %all-to-all-start.2 = ((bf16[4,2,8,16,512]{4,3,1,2,0:T(8,128)(2,1)}), bf16[4,2,8,16,512]{4,3,1,2,0:T(8,128)(2,1)S(1)}, u32[]{:S(2)}, u32[]{:S(2)}) async-start(bf16[4,2,8,16,512]{4,3,1,2,0:T(8,128)(2,1)} %broadcast_in_dim.12), calls=%async_computation.2 | async-start | bytes 2097152 | tf_op jit(solution)/shard_map/all_to_all | solution.py:12
  67.5 2.2 %copy-start = (bf16[2,512,2048]{2,1,0:T(8,128)(2,1)S(1)}, bf16[2,512,2048]{2,1,0:T(8,128)(2,1)}, u32[]{:S(2)}) copy-start(bf16[2,512,2048]{2,1,0:T(8,128)(2,1)} %param.5) | copy-start | bytes 12582916
  72.1 23.4 %collective-permute-start.3 = (bf16[2,512,512]{2,1,0:T(8,128)(2,1)S(1)}, bf16[2,512,512]{2,1,0:T(8,128)(2,1)S(1)}, u32[]{:S(2)}, u32[]{:S(2)}) collective-permute-start(bf16[2,512,512]{2,1,0:T(8,128)(2,1)S(1)} %fusion.2), channel_id=1, source_target_pairs={{0,12},{4,0},{8,4},{12,8},{1,13},{5,1},{9,5},{13,9},{2,14},{6,2},{... | collective-permute-start | bytes 3145736 | tf_op jit(solution)/shard_map/ppermute | solution.py:55
  76.5 25.4 %collective-permute-start.2 = (bf16[2,512,512]{2,1,0:T(8,128)(2,1)S(1)}, bf16[2,512,512]{2,1,0:T(8,128)(2,1)}, u32[]{:S(2)}, u32[]{:S(2)}) collective-permute-start(bf16[2,512,512]{2,1,0:T(8,128)(2,1)S(1)} %fusion.2), channel_id=1, source_target_pairs={{0,4},{4,8},{8,12},{12,0},{1,5},{5,9},{9,13},{13,1},{2,6},{6,10},{... | collective-permute-start | bytes 3145736 | tf_op jit(solution)/shard_map/ppermute | solution.py:54
  78.5 26.5 %collective-permute-start.1 = (bf16[4,2,8,16,512]{4,3,1,2,0:T(8,128)(2,1)S(1)}, bf16[4,2,8,16,512]{4,3,1,2,0:T(8,128)(2,1)}, u32[]{:S(2)}, u32[]{:S(2)}) collective-permute-start(bf16[4,2,8,16,512]{4,3,1,2,0:T(8,128)(2,1)S(1)} %all-to-all-done.2), channel_id=1, source_target_pairs={{0,1},{1,0},{2,3},{3,2},{4,5},{5,4},{6,7},{7,6},{8,9},{9,8},{10,11... | collective-permute-start | bytes 3145736 | tf_op jit(solution)/shard_map/ppermute | solution.py:20
  96.3 12.7 %collective-permute-start.5 = (bf16[1,512,512]{2,1,0:T(8,128)(2,1)}, bf16[1,512,512]{2,1,0:T(8,128)(2,1)}, u32[]{:S(2)}, u32[]{:S(2)}) collective-permute-start(bf16[1,512,512]{2,1,0:T(8,128)(2,1)} %slice.19), channel_id=1, source_target_pairs={{0,12},{4,0},{8,4},{12,8},{1,13},{5,1},{9,5},{13,9},{2,14},{6,2},{... | collective-permute-start | bytes 1572872 | tf_op jit(solution)/shard_map/ppermute | solution.py:57
  103.0 12.3 %collective-permute-start.4 = (bf16[1,512,512]{2,1,0:T(8,128)(2,1)S(1)}, bf16[1,512,512]{2,1,0:T(8,128)(2,1)S(1)}, u32[]{:S(2)}, u32[]{:S(2)}) collective-permute-start(bf16[1,512,512]{2,1,0:T(8,128)(2,1)S(1)} %slice.18), channel_id=1, source_target_pairs={{0,4},{4,8},{8,12},{12,0},{1,5},{5,9},{9,13},{13,1},{2,6},{6,10},{... | collective-permute-start | bytes 1572872 | tf_op jit(solution)/shard_map/ppermute | solution.py:56

commit v14 on v12

--- a/solution.py
+++ b/solution.py
@@ -39,7 +39,8 @@
         thin = g_plus.shape[1]
         slabs = spread(jnp.concatenate([g_minus, g_plus.T]), line, zl)
         minus, plus = slabs[:, :depth], slabs[:, depth:]
-        theirs = partner(plus, "zh")
+        last = zl * zh - 1
+        theirs = lax.ppermute(plus, ("z2", "z1", "zh"), [(at, last - at) for at in range(zl * zh)])
         minus = spread(minus, ("row", "y"), y * row)
         minus, plus, theirs = lax.optimization_barrier((minus, plus, theirs))
         minus = minus.reshape(row, y, zl, depth, cols).transpose(2, 1, 0, 3, 4).reshape(n, cols)

time: 163 us -> 163 us (level)
  the two profiles are of different devices: /device:TPU:8 before, /device:TPU:32 now
where the time goes in v14:
time: 163 us; the launch traced here: 162 us
  blocking collectives  73.6 us (45%)
  waiting for transfers between devices  42.4 us (26%)
  starting transfers between devices  29.1 us (18%)
  matrix products  7.28 us (4%)
  local copies, waits for them, and re-layouts  7.14 us (4%)
  other arithmetic  2.47 us (2%)
    all_to_all x3, blocking collectives, spread(): lax.all_to_all(jnp.broadcast_to(block[None], (count,) + block.shape), axe...  60.9 us
    ppermute x1, waiting for transfers between devices, local(): right = lax.ppermute(half, 'row', shift(row, -1))  14.9 us
    all_to_all x1, blocking collectives, local(): lax.all_to_all(total.astype(BF).reshape(parts, rows // parts, cols), ('z1...  12.8 us
    all_to_all x2, waiting for transfers between devices, spread(): lax.all_to_all(jnp.broadcast_to(block[None], (count,) + block.shape), axe...  11.4 us
    all_to_all x2, starting transfers between devices, spread(): lax.all_to_all(jnp.broadcast_to(block[None], (count,) + block.shape), axe...  10.6 us
    ppermute x1, waiting for transfers between devices, local(): lax.ppermute(plus, ('z2', 'z1', 'zh'), [(at, last - at) for at in range(z...  9.63 us
    ppermute x1, waiting for transfers between devices, local(): top = lax.ppermute(left[:, :cut], 'row', shift(row, 1))  6.42 us
    ppermute x1, starting transfers between devices, local(): bottom = lax.ppermute(right[:, cut:], 'row', shift(row, -1))  5.71 us
  transfers between devices with their start and end apart: 8, of which 5 were waited for; matrix products, arithmetic and copies ran while one was open for 6% of the time, Pallas kernels for 0%

profile of v14, /device:TPU:32, one launch (start us, length us, event | category | flops | bytes accessed | tf_op | source)
XLA Modules:
  0.0 162.3 jit_solution(16307745512661373489)
XLA Ops:
  0.0 0.7 pad_maximum_fusion.1
  0.8 28.7 %all_to_all.30 = bf16[8,32,512]{2,1,0:T(8,128)(2,1)S(1)} all-to-all(bf16[8,32,512]{2,1,0:T(8,128)(2,1)S(1)} %broadcast_in_dim.10), channel_id=1, replica_groups=mesh['z2'=4,'z1'=2,'y'=4,'row'=4,'zh'=2,'core'=2] {'z2','z1'}, dimensions={0} | all-to-all | bytes 524288 | tf_op jit(solution)/shard_map/all_to_all | solution.py:12
  29.5 1.6 broadcast_in_dim.11
  31.1 7.0 %all-to-all-start.1 = ((bf16[16,8,16,512]{3,2,1,0:T(8,128)(2,1)}), bf16[16,8,16,512]{3,2,1,0:T(8,128)(2,1)S(1)}, u32[]{:S(2)}, u32[]{:S(2)}) async-start(bf16[16,8,16,512]{3,2,1,0:T(8,128)(2,1)} %broadcast_in_dim.11), calls=%async_computation.1 | async-start | bytes 4194304 | tf_op jit(solution)/shard_map/all_to_all | solution.py:12
  38.1 3.1 %collective-permute-start = (bf16[8,16,512]{2,1,0:T(8,128)(2,1)S(1)}, bf16[8,16,512]{2,1,0:T(8,128)(2,1)S(1)}, u32[]{:S(2)}, u32[]{:S(2)}) collective-permute-start(bf16[8,16,512]{2,1,0:T(8,128)(2,1)S(1)} %get-tuple-element.9), channel_id=1, source_target_pairs={{0,450},{2,448},{64,386},{66,384},{128,322},{130,320},{192,258},{1... | collective-permute-start | bytes 393224 | tf_op jit(solution)/shard_map/ppermute | solution.py:43
  41.2 9.6 %collective-permute-done = bf16[8,16,512]{2,1,0:T(8,128)(2,1)S(1)} collective-permute-done((bf16[8,16,512]{2,1,0:T(8,128)(2,1)S(1)}, bf16[8,16,512]{2,1,0:T(8,128)(2,1)S(1)}, u32[]{:S(2)}, u32[]{:S(2)}) %collective-permute-start) | collective-permute-done | bytes 131104 | tf_op jit(solution)/shard_map/ppermute | solution.py:43
  50.9 10.9 %all-to-all-done.1 = bf16[16,8,16,512]{3,2,1,0:T(8,128)(2,1)S(1)} async-done(((bf16[16,8,16,512]{3,2,1,0:T(8,128)(2,1)}), bf16[16,8,16,512]{3,2,1,0:T(8,128)(2,1)S(1)}, u32[]{:S(2)}, u32[]{:S(2)}) %all-to-all-start.1) | async-done | bytes 2097184 | tf_op jit(solution)/shard_map/all_to_all | solution.py:12
  61.9 1.2 broadcast_in_dim.12
  63.0 3.6 %all-to-all-start.2 = ((bf16[4,2,8,16,512]{4,3,1,2,0:T(8,128)(2,1)}), bf16[4,2,8,16,512]{4,3,1,2,0:T(8,128)(2,1)S(1)}, u32[]{:S(2)}, u32[]{:S(2)}) async-start(bf16[4,2,8,16,512]{4,3,1,2,0:T(8,128)(2,1)} %broadcast_in_dim.12), calls=%async_computation.2 | async-start | bytes 2097152 | tf_op jit(solution)/shard_map/all_to_all | solution.py:12
  66.6 0.2 copy.50
  66.9 1.9 %copy-done = bf16[2,512,2048]{2,1,0:T(8,128)(2,1)S(1)} copy-done((bf16[2,512,2048]{2,1,0:T(8,128)(2,1)S(1)}, bf16[2,512,2048]{2,1,0:T(8,128)(2,1)}, u32[]{:S(2)}) %copy-start) | copy-done | bytes 4194328
  68.8 2.3 %fusion.1 = bf16[2,512,512]{2,1,0:T(8,128)(2,1)S(1)} fusion(bf16[2048,512,1]{1,0,2:T(8,128)(2,1)S(1)} %bitcast.56, bf16[2,512,2048]{2,1,0:T(8,128)(2,1)S(1)} %copy-done), kind=kOutput, calls=%fused_computation.4 | convolution fusion | flops 2148007936 | bytes 7340032 | tf_op jit(solution)/shard_map/qik,kj->qij/dot_general | solution.py:47
  71.1 3.6 %collective-permute-start.3 = (bf16[2,512,512]{2,1,0:T(8,128)(2,1)S(1)}, bf16[2,512,512]{2,1,0:T(8,128)(2,1)}, u32[]{:S(2)}, u32[]{:S(2)}) collective-permute-start(bf16[2,512,512]{2,1,0:T(8,128)(2,1)S(1)} %fusion.1), channel_id=1, source_target_pairs={{0,12},{4,0},{8,4},{12,8},{1,13},{5,1},{9,5},{13,9},{2,14},{6,2},{... | collective-permute-start | bytes 3145736 | tf_op jit(solution)/shard_map/ppermute | solution.py:56
  74.7 2.3 %collective-permute-start.2 = (bf16[2,512,512]{2,1,0:T(8,128)(2,1)S(1)}, bf16[2,512,512]{2,1,0:T(8,128)(2,1)S(1)}, u32[]{:S(2)}, u32[]{:S(2)}) collective-permute-start(bf16[2,512,512]{2,1,0:T(8,128)(2,1)S(1)} %fusion.1), channel_id=1, source_target_pairs={{0,4},{4,8},{8,12},{12,0},{1,5},{5,9},{9,13},{13,1},{2,6},{6,10},{... | collective-permute-start | bytes 3145736 | tf_op jit(solution)/shard_map/ppermute | solution.py:55
  77.0 0.5 all-to-all-done.2
  77.5 1.9 %collective-permute-start.1 = (bf16[4,2,8,16,512]{4,3,1,2,0:T(8,128)(2,1)S(1)}, bf16[4,2,8,16,512]{4,3,1,2,0:T(8,128)(2,1)}, u32[]{:S(2)}, u32[]{:S(2)}) collective-permute-start(bf16[4,2,8,16,512]{4,3,1,2,0:T(8,128)(2,1)S(1)} %all-to-all-done.2), channel_id=1, source_target_pairs={{0,1},{1,0},{2,3},{3,2},{4,5},{5,4},{6,7},{7,6},{8,9},{9,8},{10,11... | collective-permute-start | bytes 3145736 | tf_op jit(solution)/shard_map/ppermute | solution.py:20
  79.5 14.9 %collective-permute-done.3 = bf16[2,512,512]{2,1,0:T(8,128)(2,1)} collective-permute-done((bf16[2,512,512]{2,1,0:T(8,128)(2,1)S(1)}, bf16[2,512,512]{2,1,0:T(8,128)(2,1)}, u32[]{:S(2)}, u32[]{:S(2)}) %collective-permute-start.3) | collective-permute-done | bytes 1048608 | tf_op jit(solution)/shard_map/ppermute | solution.py:56
  94.4 1.1 slice.19
  95.5 5.7 %collective-permute-start.5 = (bf16[2,256,512]{2,1,0:T(8,128)(2,1)S(1)}, bf16[2,256,512]{2,1,0:T(8,128)(2,1)S(1)}, u32[]{:S(2)}, u32[]{:S(2)}) collective-permute-start(bf16[2,256,512]{2,1,0:T(8,128)(2,1)S(1)} %slice.19), channel_id=1, source_target_pairs={{0,12},{4,0},{8,4},{12,8},{1,13},{5,1},{9,5},{13,9},{2,14},{6,2},{... | collective-permute-start | bytes 1572872 | tf_op jit(solution)/shard_map/ppermute | solution.py:59
  101.3 1.9 %collective-permute-start.4 = (bf16[2,256,512]{2,1,0:T(8,128)(2,1)S(1)}, bf16[2,256,512]{2,1,0:T(8,128)(2,1)S(1)}, u32[]{:S(2)}, u32[]{:S(2)}) collective-permute-start(bf16[2,256,512]{2,1,0:T(8,128)(2,1)S(1)} %slice.18), channel_id=1, source_target_pairs={{0,4},{4,8},{8,12},{12,0},{1,5},{5,9},{9,13},{13,1},{2,6},{6,10},{... | collective-permute-start | bytes 1572872 | tf_op jit(solution)/shard_map/ppermute | solution.py:58
  103.2 1.4 select_bitcast_fusion.1
  104.6 0.2 maximum_bitcast_fusion
  105.0 0.8 fusion.6
  105.7 2.0 %fusion.2 = f32[2,512,512]{1,2,0:T(8,128)S(1)} fusion(bf16[2,512,512]{2,1,0:T(8,128)(2,1)} %collective-permute-done.3, bf16[2048,512]{1,0:T(8,128)(2,1)S(1)} %bitcast.52, s32[]{:T(128)S(6)} %select_n.66), kind=kOutput, calls=%fused_computation.7 | convolution fusion | flops 536870912 | bytes 3670020 | tf_op jit(solution)/shard_map/ki,qkj->qij/dot_general | solution.py:64
  107.7 6.4 %collective-permute-done.4 = bf16[2,256,512]{2,1,0:T(8,128)(2,1)S(1)} collective-permute-done((bf16[2,256,512]{2,1,0:T(8,128)(2,1)S(1)}, bf16[2,256,512]{2,1,0:T(8,128)(2,1)S(1)}, u32[]{:S(2)}, u32[]{:S(2)}) %collective-permute-start.4) | collective-permute-done | bytes 524320 | tf_op jit(solution)/shard_map/ppermute | solution.py:58
  114.2 0.5 fusion.15
  114.7 0.8 fusion.4
  115.4 1.0 fusion
  116.4 12.8 %all_to_all.31 = bf16[8,64,512]{2,1,0:T(8,128)(2,1)S(1)} all-to-all(bf16[8,64,512]{2,1,0:T(8,128)(2,1)S(1)} %bitcast.58), channel_id=1, replica_groups=mesh['z2'=4,'z1'=2,'y'=4,'row'=4,'zh'=2,'core'=2] {'z1','y'}, dimensions={0} | all-to-all | bytes 1048576 | tf_op jit(solution)/shard_map/all_to_all | solution.py:74
  129.3 19.3 %all_to_all.32 = bf16[4,64,512]{2,1,0:T(8,128)(2,1)S(1)} all-to-all(bf16[4,64,512]{2,1,0:T(8,128)(2,1)S(1)} %broadcast_in_dim.13), channel_id=1, replica_groups=mesh['z2'=4,'z1'=2,'y'=4,'row'=4,'zh'=2,'core'=2] {'z2'}, dimensions={0} | all-to-all | bytes 524288 | tf_op jit(solution)/shard_map/all_to_all | solution.py:12
  148.7 12.9 %all_to_all.33 = bf16[8,64,512]{2,1,0:T(8,128)(2,1)S(1)} all-to-all(bf16[8,64,512]{2,1,0:T(8,128)(2,1)S(1)} %broadcast_in_dim.14), channel_id=1, replica_groups=mesh['z2'=4,'z1'=2,'y'=4,'row'=4,'zh'=2,'core'=2] {'z1','y'}, dimensions={0} | all-to-all | bytes 1048576 | tf_op jit(solution)/shard_map/all_to_all | solution.py:12
  161.5 0.8 copy.72
  (16 shorter events, 0.5 us)
Async XLA Ops:
  31.1 30.7 %all-to-all-start.1 = ((bf16[16,8,16,512]{3,2,1,0:T(8,128)(2,1)}), bf16[16,8,16,512]{3,2,1,0:T(8,128)(2,1)S(1)}, u32[]{:S(2)}, u32[]{:S(2)}) async-start(bf16[16,8,16,512]{3,2,1,0:T(8,128)(2,1)} %broadcast_in_dim.11), calls=%async_computation.1 | async-start | bytes 4194304 | tf_op jit(solution)/shard_map/all_to_all | solution.py:12
  38.1 12.7 %collective-permute-start = (bf16[8,16,512]{2,1,0:T(8,128)(2,1)S(1)}, bf16[8,16,512]{2,1,0:T(8,128)(2,1)S(1)}, u32[]{:S(2)}, u32[]{:S(2)}) collective-permute-start(bf16[8,16,512]{2,1,0:T(8,128)(2,1)S(1)} %get-tuple-element.9), channel_id=1, source_target_pairs={{0,450},{2,448},{64,386},{66,384},{128,322},{130,320},{192,258},{1... | collective-permute-start | bytes 393224 | tf_op jit(solution)/shard_map/ppermute | solution.py:43
  63.0 14.5 %all-to-all-start.2 = ((bf16[4,2,8,16,512]{4,3,1,2,0:T(8,128)(2,1)}), bf16[4,2,8,16,512]{4,3,1,2,0:T(8,128)(2,1)S(1)}, u32[]{:S(2)}, u32[]{:S(2)}) async-start(bf16[4,2,8,16,512]{4,3,1,2,0:T(8,128)(2,1)} %broadcast_in_dim.12), calls=%async_computation.2 | async-start | bytes 2097152 | tf_op jit(solution)/shard_map/all_to_all | solution.py:12
  66.6 2.2 %copy-start = (bf16[2,512,2048]{2,1,0:T(8,128)(2,1)S(1)}, bf16[2,512,2048]{2,1,0:T(8,128)(2,1)}, u32[]{:S(2)}) copy-start(bf16[2,512,2048]{2,1,0:T(8,128)(2,1)} %param.5) | copy-start | bytes 12582916
  71.1 23.3 %collective-permute-start.3 = (bf16[2,512,512]{2,1,0:T(8,128)(2,1)S(1)}, bf16[2,512,512]{2,1,0:T(8,128)(2,1)}, u32[]{:S(2)}, u32[]{:S(2)}) collective-permute-start(bf16[2,512,512]{2,1,0:T(8,128)(2,1)S(1)} %fusion.1), channel_id=1, source_target_pairs={{0,12},{4,0},{8,4},{12,8},{1,13},{5,1},{9,5},{13,9},{2,14},{6,2},{... | collective-permute-start | bytes 3145736 | tf_op jit(solution)/shard_map/ppermute | solution.py:56
  74.7 26.5 %collective-permute-start.2 = (bf16[2,512,512]{2,1,0:T(8,128)(2,1)S(1)}, bf16[2,512,512]{2,1,0:T(8,128)(2,1)S(1)}, u32[]{:S(2)}, u32[]{:S(2)}) collective-permute-start(bf16[2,512,512]{2,1,0:T(8,128)(2,1)S(1)} %fusion.1), channel_id=1, source_target_pairs={{0,4},{4,8},{8,12},{12,0},{1,5},{5,9},{9,13},{13,1},{2,6},{6,10},{... | collective-permute-start | bytes 3145736 | tf_op jit(solution)/shard_map/ppermute | solution.py:55
  77.5 25.7 %collective-permute-start.1 = (bf16[4,2,8,16,512]{4,3,1,2,0:T(8,128)(2,1)S(1)}, bf16[4,2,8,16,512]{4,3,1,2,0:T(8,128)(2,1)}, u32[]{:S(2)}, u32[]{:S(2)}) collective-permute-start(bf16[4,2,8,16,512]{4,3,1,2,0:T(8,128)(2,1)S(1)} %all-to-all-done.2), channel_id=1, source_target_pairs={{0,1},{1,0},{2,3},{3,2},{4,5},{5,4},{6,7},{7,6},{8,9},{9,8},{10,11... | collective-permute-start | bytes 3145736 | tf_op jit(solution)/shard_map/ppermute | solution.py:20
  95.5 19.9 %collective-permute-start.5 = (bf16[2,256,512]{2,1,0:T(8,128)(2,1)S(1)}, bf16[2,256,512]{2,1,0:T(8,128)(2,1)S(1)}, u32[]{:S(2)}, u32[]{:S(2)}) collective-permute-start(bf16[2,256,512]{2,1,0:T(8,128)(2,1)S(1)} %slice.19), channel_id=1, source_target_pairs={{0,12},{4,0},{8,4},{12,8},{1,13},{5,1},{9,5},{13,9},{2,14},{6,2},{... | collective-permute-start | bytes 1572872 | tf_op jit(solution)/shard_map/ppermute | solution.py:59
  101.3 12.9 %collective-permute-start.4 = (bf16[2,256,512]{2,1,0:T(8,128)(2,1)S(1)}, bf16[2,256,512]{2,1,0:T(8,128)(2,1)S(1)}, u32[]{:S(2)}, u32[]{:S(2)}) collective-permute-start(bf16[2,256,512]{2,1,0:T(8,128)(2,1)S(1)} %slice.18), channel_id=1, source_target_pairs={{0,4},{4,8},{8,12},{12,0},{1,5},{5,9},{9,13},{13,1},{2,6},{6,10},{... | collective-permute-start | bytes 1572872 | tf_op jit(solution)/shard_map/ppermute | solution.py:58
